TPU v7x, 256 devices: a whole 4x4x8 slice. The times are simulated.
256 devices in a mesh: gy: 32 (over x, y, core), gz: 8 (over z).
Axes of the slice: x: 4, y: 4, z: 8, core: 2. Of those that a mesh axis runs over, the one named last changes fastest.
Arguments:
- template: float32 [32, 512, 512], P('gz', 'gy'), may hold values from -4 to 4
- target_image: float32 [32, 512, 512], P('gz', 'gy'), may hold values from -4 to 4
- departure_shifts: int32 [4, 3, 32, 512, 512], P(None, None, 'gz', 'gy'), may hold values from -2 to 1
- departure_fractions: float32 [4, 3], replicated, may hold values from 0.1 to 0.9
Outputs:
- update: float32 [3, 32, 512, 512], P(None, 'gz', 'gy')
- deformed: float32 [32, 512, 512], P('gz', 'gy')
All inputs are finite; a program needn't handle non-finite values.
Results may differ from a plain program's by a relative error of at most 0.00029.
Values sent between devices are 32-bit elements; how exact they have to be, the bound alone decides.
No kernel may reach another device: no remote copies, remote signals or barrier semaphores. Data moves between devices by JAX's collectives and lax.ppermute only.
A program may use at most 128 MiB of HBM per device.

v0:
```python
import functools

import jax
import jax.numpy as jnp
import ml_dtypes
import numpy as np
from jax import lax
from jax.experimental import pallas as pl
from jax.experimental.pallas import tpu as pltpu
from jax.sharding import PartitionSpec as P

NX = 512
CHEB = 8
DAMPING = 0.25
ACROSS_WEIGHT = 0.0625
ALONG_SCALE = 32.0
SHIFT = 0.25
HIGH = lax.Precision.HIGH


def hartley(length):
    index = np.arange(length)
    angle = 2.0 * np.pi / length * (np.outer(index, index) % length)
    return (np.cos(angle) + np.sin(angle)) / np.sqrt(length)


def smoother_tables(length_y, length_x, rows):
    weight = (length_y / ALONG_SCALE) ** 2
    sine = np.sin(np.pi * np.arange(length_x) / length_x) ** 2
    a = DAMPING + 4.0 * ACROSS_WEIGHT * sine
    root = np.sqrt(a * a + 4.0 * weight * a)
    r = 2.0 * weight / (a + 2.0 * weight + root)
    y = np.arange(rows)
    local = r ** np.abs(y[:, None, None] - y[None, :, None]) / root
    down = r ** (rows - 1 - y)[:, None]
    up = r ** y[:, None]
    ends = np.stack([down, up])
    spread = np.stack([r ** (y + 1)[:, None], r ** (rows - y)[:, None]]) / root
    return local, ends, spread, r**rows, 1.0 / (1.0 - r**length_y)


def chebyshev_stencil(length_x):
    center = SHIFT + 6.0 - 2.0 * np.cos(2.0 * np.pi * np.arange(length_x) / length_x)
    reach = CHEB - 1
    size = 2 * reach + 1
    rhs = np.zeros((size, size, length_x))
    rhs[reach, reach] = 1.0

    def operate(field):
        wide = np.pad(field, ((1, 1), (1, 1), (0, 0)))
        beside = wide[2:, 1:-1] + wide[:-2, 1:-1] + wide[1:-1, 2:] + wide[1:-1, :-2]
        return center * field - beside

    low = SHIFT
    high = SHIFT + 12.0
    theta = (high + low) / 2.0
    delta = (high - low) / 2.0
    sigma = theta / delta
    ratio_now = 1.0 / sigma
    residual = rhs
    direction = rhs / theta
    result = np.zeros_like(rhs)
    for turn in range(CHEB):
        result = result + direction
        if turn + 1 < CHEB:
            residual = residual - operate(direction)
            ratio_next = 1.0 / (2.0 * sigma - ratio_now)
            direction = ratio_next * ratio_now * direction + 2.0 * ratio_next / delta * residual
            ratio_now = ratio_next
    return result[reach:, reach:]


def ring(axis, offset):
    peers = lax.axis_size(axis)
    return [(i, (i + offset) % peers) for i in range(peers)]


def shift_to(x, axis, offset):
    return lax.ppermute(x, axis, ring(axis, offset))


def cubic_weights(f):
    return (
        -f * (f - 1.0) * (f - 2.0) * (1.0 / 6.0),
        (f + 1.0) * (f - 1.0) * (f - 2.0) * 0.5,
        -(f + 1.0) * f * (f - 2.0) * 0.5,
        (f + 1.0) * f * (f - 1.0) * (1.0 / 6.0),
    )


def blend(w, parts):
    total = w[0] * parts[0]
    for node in range(1, 4):
        total = total + w[node] * parts[node]
    return total


def choose(moves, parts):
    result = parts[3]
    for offset in (0, -1, -2):
        result = jnp.where(moves == offset, parts[offset + 2], result)
    return result


def x_pass(field, moves, w):
    turn = lambda value, by: value if by == 0 else pltpu.roll(value, by % NX, 1)
    filtered = blend(w, [turn(field, 1 - node) for node in range(4)])
    return choose(moves, [turn(filtered, -offset) for offset in (-2, -1, 0, 1)])


def y_pass(padded_ref, filtered_ref, layer, rows, moves, w):
    parts = [padded_ref[layer, node : node + rows + 3, :] for node in range(4)]
    filtered_ref[layer, 0 : rows + 3, :] = blend(w, parts)
    return choose(moves, [filtered_ref[layer, k : k + rows, :] for k in range(4)])


def z_filter(layers, filtered_ref, w):
    for m in range(len(layers) - 3):
        filtered_ref[m] = blend(w, [layers[m + node]() for node in range(4)])


def layers_of(before_ref, field_ref, after_ref, count):
    return [
        functools.partial(lambda ref, i: ref[i], ref, i)
        for ref, layers in ((before_ref, count), (field_ref, field_ref.shape[0]), (after_ref, count))
        for i in range(layers)
    ]


def weights_at(fractions_ref, step, way):
    return cubic_weights(fractions_ref[step, way])


def padded_rows(count):
    return -(-count // 8) * 8


def store_wide(wide_ref, layer, before, own, after):
    place = 0
    for part in (before, own, after):
        if part is not None:
            wide_ref[layer, place : place + part.shape[0], :] = part
            place = place + part.shape[0]
    rest = wide_ref.shape[1] - place
    if rest > 0:
        wide_ref[layer, place:, :] = jnp.zeros((rest, NX), wide_ref.dtype)


class Plan:
    def __init__(self, last):
        self.halos = {}
        halo = last
        for step in (3, 2):
            self.halos[step, 2] = self.halos[step, 1] = halo
            halo = halo + 3
            if step == 3:
                self.halos[step, 0] = halo
        self.second = halo
        halo = 0
        for step in (1, 0):
            self.halos[step, 2] = self.halos[step, 1] = halo
            halo = halo + 3
            if step == 1:
                self.halos[step, 0] = halo
        self.first = halo
        self.places = {}
        place = self.first
        for key in sorted(self.halos):
            if self.halos[key] > 0:
                self.places[key] = place
                place = place + self.halos[key]
        self.total = place

    def moves(self, refs, key, layer, wide_ref):
        before_ref, after_ref, shifts_ref = refs
        own = shifts_ref[key[0], key[1], layer]
        if key not in self.places:
            return own
        start, stop = self.places[key], self.places[key] + self.halos[key]
        store_wide(
            wide_ref,
            layer,
            before_ref[layer, start:stop, :],
            own.astype(jnp.float32),
            after_ref[layer, start:stop, :],
        )
        return wide_ref[layer]


PLAN = Plan(1)
HEIGHT = 16


def copies_of(pairs, sems):
    copies = [pltpu.make_async_copy(source, place, sems.at[i]) for i, (source, place) in enumerate(pairs)]
    for copy in copies:
        copy.start()
    return copies


def start_kernel(image_hbm, shifts_hbm, fractions_hbm, out_ref, low_ref, high_ref,
                 image_ref, shifts_ref, fractions_ref, sems):
    copies = copies_of(
        ((fractions_hbm, fractions_ref), (image_hbm, image_ref), (shifts_hbm, shifts_ref)), sems
    )
    for copy in copies:
        copy.wait()
    w = weights_at(fractions_ref, 0, 0)
    depth = image_ref.shape[0]
    for layer in range(depth):
        out_ref[layer] = x_pass(image_ref[layer], shifts_ref[0, 0, layer], w)
        low_ref[layer, 0 : PLAN.first, :] = out_ref[layer, 0 : PLAN.first, :]
        high_ref[layer, 0 : PLAN.first, :] = out_ref[layer, HEIGHT - PLAN.first :, :]
        for key, place in PLAN.places.items():
            count = PLAN.halos[key]
            source = shifts_ref.at[key[0], key[1], layer]
            low_ref[layer, place : place + count, :] = source[0:count, :].astype(jnp.float32)
            high_ref[layer, place : place + count, :] = source[HEIGHT - count :, :].astype(jnp.float32)


def y_kernel(step, image_ref, low_ref, high_ref, before_ref, after_ref, shifts_ref, fractions_ref,
             out_ref, padded_ref, filtered_ref, wide_ref):
    rows = out_ref.shape[1]
    w = weights_at(fractions_ref, step, 1)
    depth = image_ref.shape[0]
    halo = PLAN.halos[step, 1] + 3
    for layer in range(depth):
        store_wide(
            padded_ref, layer, low_ref[layer, 0:halo, :], image_ref[layer], high_ref[layer, 0:halo, :]
        )
        moves = PLAN.moves((before_ref, after_ref, shifts_ref), (step, 1), layer, wide_ref)
        out_ref[layer] = y_pass(padded_ref, filtered_ref, layer, rows, moves, w)


def z_x_y_kernel(step, rows_out, below_ref, image_ref, above_ref, before_ref, after_ref, shifts_ref,
                 fractions_ref, *rest):
    *outs, padded_ref, filtered_y_ref, filtered_ref, wide_ref = rest
    refs = (before_ref, after_ref, shifts_ref)
    depth = image_ref.shape[0]
    z_filter(layers_of(below_ref, image_ref, above_ref, 3), filtered_ref, weights_at(fractions_ref, step, 2))
    wx = weights_at(fractions_ref, step + 1, 0)
    wy = weights_at(fractions_ref, step + 1, 1)
    rows = image_ref.shape[1]
    for layer in range(depth):
        moves = PLAN.moves(refs, (step, 2), layer, wide_ref)
        value = choose(moves, [filtered_ref[layer + k] for k in range(4)])
        moves = PLAN.moves(refs, (step + 1, 0), layer, wide_ref)
        value = x_pass(value, moves, wx)
        if rows_out is None:
            outs[0][layer] = value
            outs[1][layer, 0 : PLAN.second, :] = outs[0][layer, 0 : PLAN.second, :]
            outs[2][layer, 0 : PLAN.second, :] = outs[0][layer, HEIGHT - PLAN.second :, :]
            continue
        padded_ref[layer, 0:rows, :] = value
        padded_ref[layer, rows:, :] = jnp.zeros((padded_ref.shape[1] - rows, NX), jnp.float32)
        moves = PLAN.moves(refs, (step + 1, 1), layer, wide_ref.at[:, 0:rows_out, :])
        value = y_pass(padded_ref, filtered_y_ref, layer, rows_out, moves, wy)
        outs[0][layer] = value
        if len(outs) > 1:
            if layer < 3:
                outs[1][layer] = value
            if layer >= depth - 3:
                outs[2][layer - depth + 3] = value
    if len(outs) > 1 and rows_out is not None:
        outs[1][3] = shifts_ref[3, 2, 0].astype(jnp.float32)
        outs[2][3] = shifts_ref[3, 2, depth - 1].astype(jnp.float32)


def split(x):
    high = x.astype(jnp.bfloat16)
    return high, (x - high.astype(jnp.float32)).astype(jnp.bfloat16)


def product(a, b):
    return jnp.dot(a, b, preferred_element_type=jnp.float32)


def force_kernel(below_ref, image_ref, above_ref, before_ref, after_ref, shifts_ref, fractions_ref,
                 first_ref, last_ref, target_hbm, table_high_hbm, table_low_hbm, pairs_hbm, ends_hbm,
                 out_ref, spectrum_ref, coarse_ref, parcels_ref, filtered_ref, wide_ref, frame_ref, force_ref,
                 target_ref, table_high_ref, table_low_ref, pairs_ref, ends_ref, sems):
    copies = copies_of(
        (
            (target_hbm, target_ref),
            (table_high_hbm, table_high_ref),
            (table_low_hbm, table_low_ref),
            (pairs_hbm, pairs_ref),
            (ends_hbm, ends_ref),
        ),
        sems,
    )
    refs = (before_ref, after_ref, shifts_ref)
    depth = image_ref.shape[0]
    z_filter(layers_of(below_ref, image_ref, above_ref, 4), filtered_ref, weights_at(fractions_ref, 3, 2))
    own = slice(1, 1 + HEIGHT)
    outer = []
    for moves_ref, base in ((first_ref, 0), (last_ref, depth + 1)):
        outer.append(choose(moves_ref[3], [filtered_ref[base + k, own, :] for k in range(4)]))
    for layer in range(depth):
        moves = PLAN.moves(refs, (3, 2), layer, wide_ref)
        frame_ref[layer] = choose(moves, [filtered_ref[layer + 1 + k] for k in range(4)])
    copies[0].wait()
    for layer in range(depth):
        image = frame_ref[layer, own, :]
        out_ref[layer] = image
        miss = (image - target_ref[layer]) * 0.5
        below = outer[0] if layer == 0 else frame_ref[layer - 1, own, :]
        above = outer[1] if layer == depth - 1 else frame_ref[layer + 1, own, :]
        slopes = (
            pltpu.roll(image, NX - 1, 1) - pltpu.roll(image, 1, 1),
            frame_ref[layer, 2 : 2 + HEIGHT, :] - frame_ref[layer, 0:HEIGHT, :],
            above - below,
        )
        for way in range(3):
            place = (way * depth + layer) * HEIGHT
            force_ref[place : place + HEIGHT, :] = miss * slopes[way]
    for copy in copies[1:]:
        copy.wait()
    high, low = split(force_ref[...])
    result = product(high, table_high_ref[...])
    result = result + product(high, table_low_ref[...])
    result = result + product(low, table_high_ref[...])
    spectrum_ref[...] = result[:, :NX]
    high, low = split(result[:, NX:])
    coarse = product(pairs_ref[...], high) + product(pairs_ref[...], low)
    coarse_ref[...] = coarse.reshape(coarse_ref.shape)
    share = parcels_ref.shape[1]
    across = NX // 128
    for side in range(2):
        for line in range(3 * depth):
            part = spectrum_ref[line * HEIGHT : (line + 1) * HEIGHT, :] * ends_ref[side]
            row = jnp.sum(part, axis=0, keepdims=True)
            place = side * 3 * depth + line
            for lane in range(across):
                parcel = place // share * across + lane
                parcels_ref[parcel, place % share, :] = row[0, lane * 128 : (lane + 1) * 128]


def carry_kernel(place_ref, carried_ref, tables_ref, out_ref):
    peers = carried_ref.shape[0]
    across = NX // 128
    place = place_ref[0]
    forward = place < peers // 2
    table = tables_ref[lax.rem(place, across)]
    power, scale = table[0:1], table[1:2]

    def sums_of(turn, power):
        sums = turn(carried_ref[...], 1) * scale[None]
        reach = 1
        while reach < peers:
            sums = sums + power[None] * turn(sums, reach)
            power = power * power
            reach = reach * 2
        return sums

    @pl.when(forward)
    def _():
        out_ref[...] = sums_of(lambda x, k: jnp.concatenate([x[peers - k :], x[: peers - k]]), power)

    @pl.when(jnp.logical_not(forward))
    def _():
        out_ref[...] = sums_of(lambda x, k: jnp.concatenate([x[k:], x[:k]]), power)


def stencil_kernel(low_ref, before_ref, own_ref, after_ref, high_ref, stencil_ref,
                   out_ref, up_ref, down_ref, wide_ref):
    reach = CHEB - 1
    ways = own_ref.shape[0]
    layers = own_ref.shape[1]
    half = own_ref.shape[2]
    for way in range(ways):
        column = [
            functools.partial(lambda ref, i: ref[way, i], ref, i)
            for ref in (low_ref, before_ref, own_ref, after_ref, high_ref)
            for i in range(ref.shape[1])
        ]
        for layer in range(layers):
            center = reach + layer
            sums = [column[center]()]
            for k in range(1, reach + 1):
                sums.append(column[center - k]() + column[center + k]())
            wide_ref[way, layer] = jnp.zeros((3 * half, NX // 2), jnp.float32)
            for dy in range(reach + 1):
                total = stencil_ref[0, dy : dy + 1, :] * sums[0]
                for dz in range(1, reach + 1 - dy):
                    total = total + stencil_ref[dz, dy : dy + 1, :] * sums[dz]
                for sign in (-1, 1) if dy > 0 else (1,):
                    rows = slice(half + sign * dy, 2 * half + sign * dy)
                    wide_ref[way, layer, rows, :] += total
            up_ref[way, layer] = wide_ref[way, layer, 0:half, :]
            out_ref[way, layer] = wide_ref[way, layer, half : 2 * half, :]
            down_ref[way, layer] = wide_ref[way, layer, 2 * half :, :]


def call(kernel, outs, scratch, *args, smem=(), hbm=(), copies=0):
    vmem = pl.BlockSpec(memory_space=pltpu.VMEM)
    spaces = {i: pltpu.SMEM for i in smem} | {i: pltpu.HBM for i in hbm}
    specs = [pl.BlockSpec(memory_space=spaces.get(i, pltpu.VMEM)) for i in range(len(args))]
    shape = lambda dims: jax.ShapeDtypeStruct(dims, jnp.float32)
    scratch = [pltpu.VMEM(dims, jnp.float32) if isinstance(dims, tuple) else dims for dims in scratch]
    if copies:
        scratch.append(pltpu.SemaphoreType.DMA((copies,)))
    return pl.pallas_call(
        kernel,
        out_shape=tuple(shape(dims) for dims in outs),
        in_specs=specs,
        out_specs=tuple(vmem for _ in outs),
        scratch_shapes=scratch,
        compiler_params=pltpu.CompilerParams(vmem_limit_bytes=12 * 2**20),
    )(*args)


def f32(table):
    return jnp.asarray(table, jnp.float32)


def bf16_pair(table):
    high = np.asarray(table, np.float32).astype(ml_dtypes.bfloat16)
    low = (np.asarray(table, np.float64) - high.astype(np.float64)).astype(ml_dtypes.bfloat16)
    return jnp.asarray(high), jnp.asarray(low)


def dot(a, b):
    return jnp.dot(a, b, precision=HIGH, preferred_element_type=jnp.float32)


def on_device(template, target_image, departure_shifts, departure_fractions):
    depth, height = template.shape[0], template.shape[1]
    peers_y = lax.axis_size("gy")
    length_y = height * peers_y
    shifts, fractions = departure_shifts, departure_fractions
    block = lambda layers, rows: (layers, padded_rows(rows), NX)
    full = (depth, height, NX)

    image, low, high = call(
        start_kernel,
        [full, (depth, PLAN.total, NX), (depth, PLAN.total, NX)],
        [full, pltpu.VMEM(shifts.shape, jnp.int32), pltpu.SMEM(fractions.shape, jnp.float32)],
        template, shifts, fractions, hbm=(0, 1, 2), copies=3,
    )
    before = shift_to(high, "gy", 1)
    after = shift_to(low, "gy", -1)
    halos = (before, after, shifts, fractions)

    def y_step(step, image, low, high):
        rows = padded_rows(height + 2 * PLAN.halos[step, 1])
        (image,) = call(
            functools.partial(y_kernel, step),
            [(depth, rows, NX)],
            [(depth, rows + 8, NX), (depth, rows + 8, NX), (depth, rows, NX)],
            image, low, high, *halos, smem=(6,),
        )
        return image, image[:3], image[depth - 3 :]

    def exchange_z(down, up):
        return shift_to(up, "gz", 1), shift_to(down, "gz", -1)

    def z_step(step, outs, rows_out, below, image, above):
        rows = image.shape[1]
        layers = 3
        return call(
            functools.partial(z_x_y_kernel, step, rows_out),
            outs,
            [(depth, rows + 8, NX), (depth, rows + 8, NX), (depth + 2 * layers - 3, rows, NX), (depth, rows, NX)],
            below, image, above, *halos, smem=(6,),
        )

    image, down, up = y_step(0, image, before, after)
    below, above = exchange_z(down, up)
    image, down, up = z_step(0, [full, full, full], height, below, image, above)
    below, above = exchange_z(down, up)
    outer_low, outer_high = below, above
    edge = (depth, PLAN.second, NX)
    image, low, high = z_step(1, [full, edge, edge], None, below, image, above)
    low, high = shift_to(high, "gy", 1), shift_to(low, "gy", -1)
    image, down, up = y_step(2, image, low, high)
    below, above = exchange_z(down, up)
    rows = padded_rows(height + 2)
    (image,) = z_step(2, [(depth, rows, NX)], rows, below, image, above)
    below, above = exchange_z(image, image)

    half, lanes = NX // 2, 128
    across = NX // lanes
    groups = peers_y // across
    share = 2 * 3 * depth // groups
    fine_x = hartley(NX)
    coarse_x = np.repeat(hartley(half), 2, axis=0)
    local, ends, spread, ratio, wrap = smoother_tables(length_y, NX, height)
    pair_z = np.kron(np.eye(depth // 2), np.ones((1, 2)))
    pair_y = np.kron(np.eye(height // 2), np.ones((1, 2)))
    pairs = np.kron(np.eye(3), np.kron(pair_z, pair_y))
    lines = 3 * depth
    coarse_shape = (3, depth // 2, height // 2, half)
    image, spectrum, coarse, parcels = call(
        force_kernel,
        [full, (lines * height, NX), coarse_shape, (peers_y, share, lanes)],
        [
            (3 * depth - 3, rows, NX), (depth, rows, NX), (depth, rows, NX), (lines * height, NX), full,
            pltpu.VMEM((NX, NX + half), jnp.bfloat16), pltpu.VMEM((NX, NX + half), jnp.bfloat16),
            pltpu.VMEM(pairs.shape, jnp.bfloat16), ends.shape,
        ],
        below, image, above, *halos, outer_low, outer_high, target_image,
        *bf16_pair(np.concatenate([fine_x, coarse_x], axis=1)),
        jnp.asarray(pairs / 8.0, jnp.bfloat16), f32(ends), smem=(6,), hbm=(9, 10, 11, 12, 13), copies=5,
    )

    carried = lax.all_to_all(parcels, "gy", 0, 0, tiled=True)
    coarse_low = shift_to(coarse, "gz", 1)
    coarse_high = shift_to(coarse, "gz", -1)
    far_low = shift_to(jnp.concatenate([coarse_low[:, 1:], coarse, coarse_high], axis=1), "gz", 3)
    far_high = shift_to(jnp.concatenate([coarse_low, coarse, coarse_high[:, :1]], axis=1), "gz", -3)

    carried, far_low, far_high = lax.optimization_barrier((carried, far_low, far_high))
    place = lax.axis_index("gy").reshape(1).astype(jnp.int32)
    tables = f32(np.stack([ratio, wrap]).reshape(2, across, lanes).transpose(1, 0, 2))
    (sums,) = call(carry_kernel, [(peers_y, share, lanes)], [], place, carried, tables, smem=(0,))
    returned = lax.all_to_all(sums, "gy", 0, 0, tiled=True)

    own, up, down = call(
        stencil_kernel,
        [coarse_shape] * 3,
        [(3, depth // 2, 3 * height // 2, half)],
        far_low, coarse_low, coarse, coarse_high, far_high, f32(chebyshev_stencil(half)),
    )
    solved = own + shift_to(up, "gy", -1) + shift_to(down, "gy", 1)

    spectrum = spectrum.reshape(lines, height, NX)
    smooth = f32(local[0]) * spectrum[:, 0:1]
    for y in range(1, height):
        smooth = smooth + f32(local[y]) * spectrum[:, y : y + 1]
    carries = returned.reshape(groups, across, share, lanes).transpose(0, 2, 1, 3)
    carries = carries.reshape(2, lines, NX)
    smooth = smooth + f32(spread[0]) * carries[0][:, None] + f32(spread[1]) * carries[1][:, None]
    smooth = smooth.reshape(lines * height, NX)
    solved = dot(f32(pairs.T), solved.reshape(lines * height // 4, half))
    update = dot(smooth, f32(-fine_x)) + dot(solved, f32(-coarse_x.T))
    return (update.reshape(3, depth, height, NX), image)


def solution(mesh):
    return jax.shard_map(
        on_device,
        mesh=mesh,
        in_specs=(P("gz", "gy", None), P("gz", "gy", None), P(None, None, "gz", "gy", None), P()),
        out_specs=(P(None, "gz", "gy", None), P("gz", "gy", None)),
        check_vma=False,
    )
```

profile of v0, /device:TPU:64, one launch (start us, length us, event | category | flops | bytes accessed | tf_op | source)
XLA Modules:
  0.0 114.8 jit_solution(7895838213858223641)
XLA Ops:
  4.8 5.1 %collective-permute-start.1 = (f32[4,29,512]{2,1,0:T(8,128)S(1)}, f32[4,29,512]{2,1,0:T(8,128)S(1)}, u32[]{:S(2)}, u32[]{:S(2)}) collective-permute-start(f32[4,29,512]{2,1,0:T(8,128)S(1)} %get-tuple-element.23), channel_id=1, source_target_pairs={{0,248},{8,0},{16,8},{24,16},{32,24},{40,32},{48,40},{56,48},{64,5... | collective-permute-start | bytes 712712 | tf_op jit(solution)/shard_map/ppermute | solution.py:79
  9.8 4.1 %collective-permute-done.low_ref.before_ref = f32[4,29,512]{2,1,0:T(8,128)S(1)} collective-permute-done((f32[4,29,512]{2,1,0:T(8,128)S(1)}, f32[4,29,512]{2,1,0:T(8,128)S(1)}, u32[]{:S(2)}, u32[]{:S(2)}) %collective-permute-start) | collective-permute-done | bytes 237600 | tf_op jit(solution)/shard_map/ppermute | solution.py:79
  14.9 1.9 %collective-permute-start.2 = (f32[3,24,512]{2,1,0:T(8,128)S(1)}, f32[3,24,512]{2,1,0:T(8,128)S(1)}, u32[]{:S(2)}, u32[]{:S(2)}) collective-permute-start(f32[3,24,512]{2,1,0:T(8,128)S(1)} %get-tuple-element.59), channel_id=1, source_target_pairs={{0,1},{1,2},{2,3},{3,4},{4,5},{5,6},{6,7},{7,0},{8,9},{9,10},{10,1... | collective-permute-start | bytes 442376 | tf_op jit(solution)/shard_map/ppermute | solution.py:79
  16.8 3.1 %collective-permute-done.3.above_ref = f32[3,24,512]{2,1,0:T(8,128)S(1)} collective-permute-done((f32[3,24,512]{2,1,0:T(8,128)S(1)}, f32[3,24,512]{2,1,0:T(8,128)S(1)}, u32[]{:S(2)}, u32[]{:S(2)}) %collective-permute-start.3) | collective-permute-done | bytes 147488 | tf_op jit(solution)/shard_map/ppermute | solution.py:79
  21.4 3.1 %collective-permute-start.4 = (f32[4,16,512]{2,1,0:T(8,128)S(1)}, f32[4,16,512]{2,1,0:T(8,128)S(1)}, u32[]{:S(2)}, u32[]{:S(2)}) collective-permute-start(f32[4,16,512]{2,1,0:T(8,128)S(1)} %get-tuple-element.24), channel_id=1, source_target_pairs={{0,1},{1,2},{2,3},{3,4},{4,5},{5,6},{6,7},{7,0},{8,9},{9,10},{10,1... | collective-permute-start | bytes 393224 | tf_op jit(solution)/shard_map/ppermute | solution.py:79
  25.5 2.9 %collective-permute-done.4.below_ref.first_ref = f32[4,16,512]{2,1,0:T(8,128)S(1)} collective-permute-done((f32[4,16,512]{2,1,0:T(8,128)S(1)}, f32[4,16,512]{2,1,0:T(8,128)S(1)}, u32[]{:S(2)}, u32[]{:S(2)}) %collective-permute-start.4) | collective-permute-done | bytes 131104 | tf_op jit(solution)/shard_map/ppermute | solution.py:79
  28.4 2.3 %collective-permute-done.5.above_ref.last_ref = f32[4,16,512]{2,1,0:T(8,128)S(1)} collective-permute-done((f32[4,16,512]{2,1,0:T(8,128)S(1)}, f32[4,16,512]{2,1,0:T(8,128)S(1)}, u32[]{:S(2)}, u32[]{:S(2)}) %collective-permute-start.5) | collective-permute-done | bytes 131104 | tf_op jit(solution)/shard_map/ppermute | solution.py:79
  31.8 5.1 %collective-permute-start.7 = (f32[4,7,512]{2,1,0:T(8,128)S(1)}, f32[4,7,512]{2,1,0:T(8,128)S(1)}, u32[]{:S(2)}, u32[]{:S(2)}) collective-permute-start(f32[4,7,512]{2,1,0:T(8,128)S(1)} %get-tuple-element.29), channel_id=1, source_target_pairs={{0,248},{8,0},{16,8},{24,16},{32,24},{40,32},{48,40},{56,48},{64,5... | collective-permute-start | bytes 172040 | tf_op jit(solution)/shard_map/ppermute | solution.py:79
  36.9 1.9 %collective-permute-done.6.low_ref = f32[4,7,512]{2,1,0:T(8,128)S(1)} collective-permute-done((f32[4,7,512]{2,1,0:T(8,128)S(1)}, f32[4,7,512]{2,1,0:T(8,128)S(1)}, u32[]{:S(2)}, u32[]{:S(2)}) %collective-permute-start.6) | collective-permute-done | bytes 57376 | tf_op jit(solution)/shard_map/ppermute | solution.py:79
  40.7 2.4 %collective-permute-start.8 = (f32[3,24,512]{2,1,0:T(8,128)S(1)}, f32[3,24,512]{2,1,0:T(8,128)S(1)}, u32[]{:S(2)}, u32[]{:S(2)}) collective-permute-start(f32[3,24,512]{2,1,0:T(8,128)S(1)} %get-tuple-element.57), channel_id=1, source_target_pairs={{0,1},{1,2},{2,3},{3,4},{4,5},{5,6},{6,7},{7,0},{8,9},{9,10},{10,1... | collective-permute-start | bytes 442376 | tf_op jit(solution)/shard_map/ppermute | solution.py:79
  43.1 3.0 %collective-permute-done.9.above_ref = f32[3,24,512]{2,1,0:T(8,128)S(1)} collective-permute-done((f32[3,24,512]{2,1,0:T(8,128)S(1)}, f32[3,24,512]{2,1,0:T(8,128)S(1)}, u32[]{:S(2)}, u32[]{:S(2)}) %collective-permute-start.9) | collective-permute-done | bytes 147488 | tf_op jit(solution)/shard_map/ppermute | solution.py:79
  47.0 1.4 %shard_map.307.image_ref = f32[4,24,512]{2,1,0:T(8,128)S(1)} custom-call(f32[3,24,512]{2,1,0:T(8,128)S(1)} %collective-permute-done.8.below_ref, f32[4,24,512]{2,1,0:T(8,128)S(1)} %shard_map.306.image_ref, f32[3,24,512]{2,1,0:T(8,128)S(1)} %collective-permute-done.9.above_ref, f32[4,29,512]{2,1,0:T(8,128)S(1)} %collective-permute-done.low_ref.before_ref, ...), custom_call_target="tpu_custom_call" | custom-call | tf_op jit(solution)/shard_map/pallas_call | solution.py:403
  48.4 3.3 %collective-permute-start.11 = (f32[4,24,512]{2,1,0:T(8,128)S(1)}, f32[4,24,512]{2,1,0:T(8,128)S(1)}, u32[]{:S(2)}, u32[]{:S(2)}) collective-permute-start(f32[4,24,512]{2,1,0:T(8,128)S(1)} %shard_map.307.image_ref), channel_id=1, source_target_pairs={{0,7},{1,0},{2,1},{3,2},{4,3},{5,4},{6,5},{7,6},{8,15},{9,8},{10,9... | collective-permute-start | bytes 589832 | tf_op jit(solution)/shard_map/ppermute | solution.py:79
  51.8 3.2 %collective-permute-done.11.above_ref = f32[4,24,512]{2,1,0:T(8,128)S(1)} collective-permute-done((f32[4,24,512]{2,1,0:T(8,128)S(1)}, f32[4,24,512]{2,1,0:T(8,128)S(1)}, u32[]{:S(2)}, u32[]{:S(2)}) %collective-permute-start.11) | collective-permute-done | bytes 196640 | tf_op jit(solution)/shard_map/ppermute | solution.py:79
  54.9 3.8 %collective-permute-done.10.below_ref = f32[4,24,512]{2,1,0:T(8,128)} collective-permute-done((f32[4,24,512]{2,1,0:T(8,128)S(1)}, f32[4,24,512]{2,1,0:T(8,128)}, u32[]{:S(2)}, u32[]{:S(2)}) %collective-permute-start.10) | collective-permute-done | bytes 196640 | tf_op jit(solution)/shard_map/ppermute | solution.py:79
  62.4 3.3 %shard_map.308 = (f32[4,16,512]{2,1,0:T(8,128)}, f32[192,512]{1,0:T(8,128)S(1)}, f32[3,2,8,256]{3,2,1,0:T(8,128)}, f32[32,3,128]{2,1,0:T(4,128)S(1)}) custom-call(f32[4,24,512]{2,1,0:T(8,128)} %collective-permute-done.10.below_ref, f32[4,24,512]{2,1,0:T(8,128)S(1)} %shard_map.307.image_ref, f32[4,24,512]{2,1,0:T(8,128)S(1)} %collective-permute-done.11.above_ref, ...), custom_call_target="tpu_custom_call" | custom-call | tf_op jit(solution)/shard_map/pallas_call | solution.py:403
  66.4 2.1 %collective-permute-start.13 = (f32[3,2,8,256]{3,2,1,0:T(8,128)}, f32[3,2,8,256]{3,2,1,0:T(8,128)S(1)}, u32[]{:S(2)}, u32[]{:S(2)}) collective-permute-start(f32[3,2,8,256]{3,2,1,0:T(8,128)} %get-tuple-element.32.own_ref), channel_id=1, source_target_pairs={{0,7},{1,0},{2,1},{3,2},{4,3},{5,4},{6,5},{7,6},{8,15},{9,8},{10,9... | collective-permute-start | bytes 147464 | tf_op jit(solution)/shard_map/ppermute | solution.py:79
  68.8 4.4 %all-to-all-start = ((f32[32,3,128]{2,1,0:T(4,128)}), f32[32,3,128]{2,1,0:T(4,128)S(1)}, u32[]{:S(2)}, u32[]{:S(2)}) async-start(f32[32,3,128]{2,1,0:T(4,128)} %copy-done.10), calls=%async_computation | async-start | bytes 131072 | tf_op jit(solution)/shard_map/all_to_all | solution.py:507
  74.3 3.8 %collective-permute-start.15 = (f32[3,5,8,256]{3,2,1,0:T(8,128)S(1)}, f32[3,5,8,256]{3,2,1,0:T(8,128)S(1)}, u32[]{:S(2)}, u32[]{:S(2)}) collective-permute-start(f32[3,5,8,256]{3,2,1,0:T(8,128)S(1)} %get-tuple-element.62), channel_id=1, source_target_pairs={{0,5},{1,6},{2,7},{3,0},{4,1},{5,2},{6,3},{7,4},{8,13},{9,14},{10,... | collective-permute-start | bytes 368648 | tf_op jit(solution)/shard_map/ppermute | solution.py:79
  80.7 6.5 %collective-permute-done.15.high_ref = f32[3,5,8,256]{3,2,1,0:T(8,128)S(1)} collective-permute-done((f32[3,5,8,256]{3,2,1,0:T(8,128)S(1)}, f32[3,5,8,256]{3,2,1,0:T(8,128)S(1)}, u32[]{:S(2)}, u32[]{:S(2)}) %collective-permute-start.15) | collective-permute-done | bytes 122912 | tf_op jit(solution)/shard_map/ppermute | solution.py:79
  87.2 3.8 %collective-permute-done.14.low_ref = f32[3,5,8,256]{3,2,1,0:T(8,128)S(1)} collective-permute-done((f32[3,5,8,256]{3,2,1,0:T(8,128)S(1)}, f32[3,5,8,256]{3,2,1,0:T(8,128)S(1)}, u32[]{:S(2)}, u32[]{:S(2)}) %collective-permute-start.14) | collective-permute-done | bytes 122912 | tf_op jit(solution)/shard_map/ppermute | solution.py:79
  91.7 7.3 %all-to-all-start.1 = ((f32[32,3,128]{2,1,0:T(4,128)}), f32[32,3,128]{2,1,0:T(4,128)S(1)}, u32[]{:S(2)}, u32[]{:S(2)}) async-start(f32[32,3,128]{2,1,0:T(4,128)} %shard_map.309), calls=%async_computation.1 | async-start | bytes 131072 | tf_op jit(solution)/shard_map/all_to_all | solution.py:517
  100.8 5.0 %collective-permute-start.16 = (f32[3,2,8,256]{3,2,1,0:T(8,128)S(1)}, f32[3,2,8,256]{3,2,1,0:T(8,128)S(1)}, u32[]{:S(2)}, u32[]{:S(2)}) collective-permute-start(f32[3,2,8,256]{3,2,1,0:T(8,128)S(1)} %get-tuple-element.37), channel_id=1, source_target_pairs={{0,248},{8,0},{16,8},{24,16},{32,24},{40,32},{48,40},{56,48},{64,5... | collective-permute-start | bytes 147464 | tf_op jit(solution)/shard_map/ppermute | solution.py:79
  107.6 5.1 %collective-permute-done.17 = f32[3,2,8,256]{3,2,1,0:T(8,128)S(1)} collective-permute-done((f32[3,2,8,256]{3,2,1,0:T(8,128)S(1)}, f32[3,2,8,256]{3,2,1,0:T(8,128)S(1)}, u32[]{:S(2)}, u32[]{:S(2)}) %collective-permute-start.17) | collective-permute-done | bytes 49184 | tf_op jit(solution)/shard_map/ppermute | solution.py:79
  (120 shorter events, 25.8 us)
Async XLA Ops:
  4.7 9.2 %collective-permute-start = (f32[4,29,512]{2,1,0:T(8,128)S(1)}, f32[4,29,512]{2,1,0:T(8,128)S(1)}, u32[]{:S(2)}, u32[]{:S(2)}) collective-permute-start(f32[4,29,512]{2,1,0:T(8,128)S(1)} %get-tuple-element.22), channel_id=1, source_target_pairs={{0,8},{8,16},{16,24},{24,32},{32,40},{40,48},{48,56},{56,64},{64,7... | collective-permute-start | bytes 712712 | tf_op jit(solution)/shard_map/ppermute | solution.py:79
  4.8 9.1 %collective-permute-start.1 = (f32[4,29,512]{2,1,0:T(8,128)S(1)}, f32[4,29,512]{2,1,0:T(8,128)S(1)}, u32[]{:S(2)}, u32[]{:S(2)}) collective-permute-start(f32[4,29,512]{2,1,0:T(8,128)S(1)} %get-tuple-element.23), channel_id=1, source_target_pairs={{0,248},{8,0},{16,8},{24,16},{32,24},{40,32},{48,40},{56,48},{64,5... | collective-permute-start | bytes 712712 | tf_op jit(solution)/shard_map/ppermute | solution.py:79
  14.7 5.2 %collective-permute-start.3 = (f32[3,24,512]{2,1,0:T(8,128)S(1)}, f32[3,24,512]{2,1,0:T(8,128)S(1)}, u32[]{:S(2)}, u32[]{:S(2)}) collective-permute-start(f32[3,24,512]{2,1,0:T(8,128)S(1)} %get-tuple-element.58), channel_id=1, source_target_pairs={{0,7},{1,0},{2,1},{3,2},{4,3},{5,4},{6,5},{7,6},{8,15},{9,8},{10,9... | collective-permute-start | bytes 442376 | tf_op jit(solution)/shard_map/ppermute | solution.py:79
  14.9 5.1 %collective-permute-start.2 = (f32[3,24,512]{2,1,0:T(8,128)S(1)}, f32[3,24,512]{2,1,0:T(8,128)S(1)}, u32[]{:S(2)}, u32[]{:S(2)}) collective-permute-start(f32[3,24,512]{2,1,0:T(8,128)S(1)} %get-tuple-element.59), channel_id=1, source_target_pairs={{0,1},{1,2},{2,3},{3,4},{4,5},{5,6},{6,7},{7,0},{8,9},{9,10},{10,1... | collective-permute-start | bytes 442376 | tf_op jit(solution)/shard_map/ppermute | solution.py:79
  21.4 7.0 %collective-permute-start.4 = (f32[4,16,512]{2,1,0:T(8,128)S(1)}, f32[4,16,512]{2,1,0:T(8,128)S(1)}, u32[]{:S(2)}, u32[]{:S(2)}) collective-permute-start(f32[4,16,512]{2,1,0:T(8,128)S(1)} %get-tuple-element.24), channel_id=1, source_target_pairs={{0,1},{1,2},{2,3},{3,4},{4,5},{5,6},{6,7},{7,0},{8,9},{9,10},{10,1... | collective-permute-start | bytes 393224 | tf_op jit(solution)/shard_map/ppermute | solution.py:79
  24.5 6.2 %collective-permute-start.5 = (f32[4,16,512]{2,1,0:T(8,128)S(1)}, f32[4,16,512]{2,1,0:T(8,128)S(1)}, u32[]{:S(2)}, u32[]{:S(2)}) collective-permute-start(f32[4,16,512]{2,1,0:T(8,128)S(1)} %get-tuple-element.26), channel_id=1, source_target_pairs={{0,7},{1,0},{2,1},{3,2},{4,3},{5,4},{6,5},{7,6},{8,15},{9,8},{10,9... | collective-permute-start | bytes 393224 | tf_op jit(solution)/shard_map/ppermute | solution.py:79
  31.7 7.1 %collective-permute-start.6 = (f32[4,7,512]{2,1,0:T(8,128)S(1)}, f32[4,7,512]{2,1,0:T(8,128)S(1)}, u32[]{:S(2)}, u32[]{:S(2)}) collective-permute-start(f32[4,7,512]{2,1,0:T(8,128)S(1)} %get-tuple-element.28), channel_id=1, source_target_pairs={{0,8},{8,16},{16,24},{24,32},{32,40},{40,48},{48,56},{56,64},{64,7... | collective-permute-start | bytes 172040 | tf_op jit(solution)/shard_map/ppermute | solution.py:79
  31.8 7.0 %collective-permute-start.7 = (f32[4,7,512]{2,1,0:T(8,128)S(1)}, f32[4,7,512]{2,1,0:T(8,128)S(1)}, u32[]{:S(2)}, u32[]{:S(2)}) collective-permute-start(f32[4,7,512]{2,1,0:T(8,128)S(1)} %get-tuple-element.29), channel_id=1, source_target_pairs={{0,248},{8,0},{16,8},{24,16},{32,24},{40,32},{48,40},{56,48},{64,5... | collective-permute-start | bytes 172040 | tf_op jit(solution)/shard_map/ppermute | solution.py:79
  39.7 6.4 %collective-permute-start.9 = (f32[3,24,512]{2,1,0:T(8,128)S(1)}, f32[3,24,512]{2,1,0:T(8,128)S(1)}, u32[]{:S(2)}, u32[]{:S(2)}) collective-permute-start(f32[3,24,512]{2,1,0:T(8,128)S(1)} %get-tuple-element.56), channel_id=1, source_target_pairs={{0,7},{1,0},{2,1},{3,2},{4,3},{5,4},{6,5},{7,6},{8,15},{9,8},{10,9... | collective-permute-start | bytes 442376 | tf_op jit(solution)/shard_map/ppermute | solution.py:79
  40.7 6.4 %collective-permute-start.8 = (f32[3,24,512]{2,1,0:T(8,128)S(1)}, f32[3,24,512]{2,1,0:T(8,128)S(1)}, u32[]{:S(2)}, u32[]{:S(2)}) collective-permute-start(f32[3,24,512]{2,1,0:T(8,128)S(1)} %get-tuple-element.57), channel_id=1, source_target_pairs={{0,1},{1,2},{2,3},{3,4},{4,5},{5,6},{6,7},{7,0},{8,9},{9,10},{10,1... | collective-permute-start | bytes 442376 | tf_op jit(solution)/shard_map/ppermute | solution.py:79
  48.4 6.5 %collective-permute-start.11 = (f32[4,24,512]{2,1,0:T(8,128)S(1)}, f32[4,24,512]{2,1,0:T(8,128)S(1)}, u32[]{:S(2)}, u32[]{:S(2)}) collective-permute-start(f32[4,24,512]{2,1,0:T(8,128)S(1)} %shard_map.307.image_ref), channel_id=1, source_target_pairs={{0,7},{1,0},{2,1},{3,2},{4,3},{5,4},{6,5},{7,6},{8,15},{9,8},{10,9... | collective-permute-start | bytes 589832 | tf_op jit(solution)/shard_map/ppermute | solution.py:79
  51.8 7.0 %collective-permute-start.10 = (f32[4,24,512]{2,1,0:T(8,128)S(1)}, f32[4,24,512]{2,1,0:T(8,128)}, u32[]{:S(2)}, u32[]{:S(2)}) collective-permute-start(f32[4,24,512]{2,1,0:T(8,128)S(1)} %shard_map.307.image_ref), channel_id=1, source_target_pairs={{0,1},{1,2},{2,3},{3,4},{4,5},{5,6},{6,7},{7,0},{8,9},{9,10},{10,1... | collective-permute-start | bytes 589832 | tf_op jit(solution)/shard_map/ppermute | solution.py:79
  66.3 32.7 %copy-start.21 = (f32[16,512]{1,0:T(8,128)S(1)}, f32[16,512]{1,0:T(8,128)}, u32[]{:S(2)}) copy-start(f32[16,512]{1,0:T(8,128)} %constant.78.clone) | copy-start | bytes 98308
  66.3 32.7 %copy-start.22 = (f32[16,512]{1,0:T(8,128)S(1)}, f32[16,512]{1,0:T(8,128)}, u32[]{:S(2)}) copy-start(f32[16,512]{1,0:T(8,128)} %constant.77.clone) | copy-start | bytes 98308
  66.4 6.9 %collective-permute-start.13 = (f32[3,2,8,256]{3,2,1,0:T(8,128)}, f32[3,2,8,256]{3,2,1,0:T(8,128)S(1)}, u32[]{:S(2)}, u32[]{:S(2)}) collective-permute-start(f32[3,2,8,256]{3,2,1,0:T(8,128)} %get-tuple-element.32.own_ref), channel_id=1, source_target_pairs={{0,7},{1,0},{2,1},{3,2},{4,3},{5,4},{6,5},{7,6},{8,15},{9,8},{10,9... | collective-permute-start | bytes 147464 | tf_op jit(solution)/shard_map/ppermute | solution.py:79
  68.5 4.8 %collective-permute-start.12 = (f32[3,2,8,256]{3,2,1,0:T(8,128)}, f32[3,2,8,256]{3,2,1,0:T(8,128)S(1)}, u32[]{:S(2)}, u32[]{:S(2)}) collective-permute-start(f32[3,2,8,256]{3,2,1,0:T(8,128)} %get-tuple-element.32.own_ref), channel_id=1, source_target_pairs={{0,1},{1,2},{2,3},{3,4},{4,5},{5,6},{6,7},{7,0},{8,9},{9,10},{10,1... | collective-permute-start | bytes 147464 | tf_op jit(solution)/shard_map/ppermute | solution.py:79
  68.8 11.9 %all-to-all-start = ((f32[32,3,128]{2,1,0:T(4,128)}), f32[32,3,128]{2,1,0:T(4,128)S(1)}, u32[]{:S(2)}, u32[]{:S(2)}) async-start(f32[32,3,128]{2,1,0:T(4,128)} %copy-done.10), calls=%async_computation | async-start | bytes 131072 | tf_op jit(solution)/shard_map/all_to_all | solution.py:507
  73.4 33.3 %copy-start.16 = (f32[16,512]{1,0:T(8,128)S(1)}, f32[16,512]{1,0:T(8,128)}, u32[]{:S(2)}) copy-start(f32[16,512]{1,0:T(8,128)} %constant.83.clone) | copy-start | bytes 98308
  73.4 33.3 %copy-start.17 = (f32[16,512]{1,0:T(8,128)S(1)}, f32[16,512]{1,0:T(8,128)}, u32[]{:S(2)}) copy-start(f32[16,512]{1,0:T(8,128)} %constant.82.clone) | copy-start | bytes 98308
  74.3 12.9 %collective-permute-start.15 = (f32[3,5,8,256]{3,2,1,0:T(8,128)S(1)}, f32[3,5,8,256]{3,2,1,0:T(8,128)S(1)}, u32[]{:S(2)}, u32[]{:S(2)}) collective-permute-start(f32[3,5,8,256]{3,2,1,0:T(8,128)S(1)} %get-tuple-element.62), channel_id=1, source_target_pairs={{0,5},{1,6},{2,7},{3,0},{4,1},{5,2},{6,3},{7,4},{8,13},{9,14},{10,... | collective-permute-start | bytes 368648 | tf_op jit(solution)/shard_map/ppermute | solution.py:79
  78.1 13.0 %collective-permute-start.14 = (f32[3,5,8,256]{3,2,1,0:T(8,128)S(1)}, f32[3,5,8,256]{3,2,1,0:T(8,128)S(1)}, u32[]{:S(2)}, u32[]{:S(2)}) collective-permute-start(f32[3,5,8,256]{3,2,1,0:T(8,128)S(1)} %get-tuple-element.63), channel_id=1, source_target_pairs={{0,3},{1,4},{2,5},{3,6},{4,7},{5,0},{6,1},{7,2},{8,11},{9,12},{10,... | collective-permute-start | bytes 368648 | tf_op jit(solution)/shard_map/ppermute | solution.py:79
  91.7 14.8 %all-to-all-start.1 = ((f32[32,3,128]{2,1,0:T(4,128)}), f32[32,3,128]{2,1,0:T(4,128)S(1)}, u32[]{:S(2)}, u32[]{:S(2)}) async-start(f32[32,3,128]{2,1,0:T(4,128)} %shard_map.309), calls=%async_computation.1 | async-start | bytes 131072 | tf_op jit(solution)/shard_map/all_to_all | solution.py:517
  100.8 6.8 %collective-permute-start.16 = (f32[3,2,8,256]{3,2,1,0:T(8,128)S(1)}, f32[3,2,8,256]{3,2,1,0:T(8,128)S(1)}, u32[]{:S(2)}, u32[]{:S(2)}) collective-permute-start(f32[3,2,8,256]{3,2,1,0:T(8,128)S(1)} %get-tuple-element.37), channel_id=1, source_target_pairs={{0,248},{8,0},{16,8},{24,16},{32,24},{40,32},{48,40},{56,48},{64,5... | collective-permute-start | bytes 147464 | tf_op jit(solution)/shard_map/ppermute | solution.py:79
  105.8 6.8 %collective-permute-start.17 = (f32[3,2,8,256]{3,2,1,0:T(8,128)S(1)}, f32[3,2,8,256]{3,2,1,0:T(8,128)S(1)}, u32[]{:S(2)}, u32[]{:S(2)}) collective-permute-start(f32[3,2,8,256]{3,2,1,0:T(8,128)S(1)} %get-tuple-element.38), channel_id=1, source_target_pairs={{0,8},{8,16},{16,24},{24,32},{32,40},{40,48},{48,56},{56,64},{64,7... | collective-permute-start | bytes 147464 | tf_op jit(solution)/shard_map/ppermute | solution.py:79
  (30 other events, 571.6 us)
where the time goes:
time: 115 us
  starting transfers between devices  47.1 us (41%)
  waiting for transfers between devices  43.5 us (38%)
  Pallas kernels  11.5 us (10%)
  local copies, waits for them, and re-layouts  7.8 us (7%)
  matrix products  2.04 us (2%)
  other arithmetic  1.6 us (1%)
  between operations  1.26 us (1%)
    ppermute x18, waiting for transfers between devices, shift_to(): return lax.ppermute(x, axis, ring(axis, offset))  41.5 us
    ppermute x18, starting transfers between devices, shift_to(): return lax.ppermute(x, axis, ring(axis, offset))  35.4 us
    pallas_call x9, Pallas kernels, call(): pl.pallas_call(kernel, out_shape=tuple((shape(dims) for dims in outs)), i...  11.5 us
    unnamed x80, local copies, waits for them, and re-layouts  7.47 us
    all_to_all x1, starting transfers between devices, on_device(): returned = lax.all_to_all(sums, 'gy', 0, 0, tiled=True)  7.26 us
    all_to_all x1, starting transfers between devices, on_device(): carried = lax.all_to_all(parcels, 'gy', 0, 0, tiled=True)  4.37 us
  transfers between devices with their start and end apart: 20, of which 16 were waited for; matrix products, arithmetic and copies ran while one was open for 2% of the time, Pallas kernels for 1%

commit v1 on v0

--- a/solution.py
+++ b/solution.py
@@ -276,19 +276,9 @@
 
 
 def force_kernel(below_ref, image_ref, above_ref, before_ref, after_ref, shifts_ref, fractions_ref,
-                 first_ref, last_ref, target_hbm, table_high_hbm, table_low_hbm, pairs_hbm, ends_hbm,
+                 first_ref, last_ref, target_ref, table_high_ref, table_low_ref, pairs_ref, ends_ref,
                  out_ref, spectrum_ref, coarse_ref, parcels_ref, filtered_ref, wide_ref, frame_ref, force_ref,
-                 target_ref, table_high_ref, table_low_ref, pairs_ref, ends_ref, sems):
-    copies = copies_of(
-        (
-            (target_hbm, target_ref),
-            (table_high_hbm, table_high_ref),
-            (table_low_hbm, table_low_ref),
-            (pairs_hbm, pairs_ref),
-            (ends_hbm, ends_ref),
-        ),
-        sems,
-    )
+                 tails_ref):
     refs = (before_ref, after_ref, shifts_ref)
     depth = image_ref.shape[0]
     z_filter(layers_of(below_ref, image_ref, above_ref, 4), filtered_ref, weights_at(fractions_ref, 3, 2))
@@ -299,7 +289,6 @@
     for layer in range(depth):
         moves = PLAN.moves(refs, (3, 2), layer, wide_ref)
         frame_ref[layer] = choose(moves, [filtered_ref[layer + 1 + k] for k in range(4)])
-    copies[0].wait()
     for layer in range(depth):
         image = frame_ref[layer, own, :]
         out_ref[layer] = image
@@ -314,8 +303,6 @@
         for way in range(3):
             place = (way * depth + layer) * HEIGHT
             force_ref[place : place + HEIGHT, :] = miss * slopes[way]
-    for copy in copies[1:]:
-        copy.wait()
     high, low = split(force_ref[...])
     result = product(high, table_high_ref[...])
     result = result + product(high, table_low_ref[...])
@@ -324,75 +311,76 @@
     high, low = split(result[:, NX:])
     coarse = product(pairs_ref[...], high) + product(pairs_ref[...], low)
     coarse_ref[...] = coarse.reshape(coarse_ref.shape)
-    share = parcels_ref.shape[1]
     across = NX // 128
     for side in range(2):
         for line in range(3 * depth):
             part = spectrum_ref[line * HEIGHT : (line + 1) * HEIGHT, :] * ends_ref[side]
             row = jnp.sum(part, axis=0, keepdims=True)
-            place = side * 3 * depth + line
+            place = (side * 3 * depth + line) * across
             for lane in range(across):
-                parcel = place // share * across + lane
-                parcels_ref[parcel, place % share, :] = row[0, lane * 128 : (lane + 1) * 128]
-
-
-def carry_kernel(place_ref, carried_ref, tables_ref, out_ref):
+                tails_ref[place + lane, :] = row[0, lane * 128 : (lane + 1) * 128]
+    for peer in range(parcels_ref.shape[0]):
+        parcels_ref[peer] = tails_ref[...]
+
+
+def load_kernel(*refs):
+    count = len(refs) // 2
+    for i in range(count):
+        refs[count + i][...] = refs[i][...]
+
+
+def carry_kernel(place_ref, carried_ref, tables_ref, out_ref, sums_ref):
     peers = carried_ref.shape[0]
     across = NX // 128
+    lines = out_ref.shape[1]
+    rows = lines * across
     place = place_ref[0]
-    forward = place < peers // 2
-    table = tables_ref[lax.rem(place, across)]
-    power, scale = table[0:1], table[1:2]
-
-    def sums_of(turn, power):
-        sums = turn(carried_ref[...], 1) * scale[None]
-        reach = 1
-        while reach < peers:
-            sums = sums + power[None] * turn(sums, reach)
-            power = power * power
-            reach = reach * 2
-        return sums
-
-    @pl.when(forward)
-    def _():
-        out_ref[...] = sums_of(lambda x, k: jnp.concatenate([x[peers - k :], x[: peers - k]]), power)
-
-    @pl.when(jnp.logical_not(forward))
-    def _():
-        out_ref[...] = sums_of(lambda x, k: jnp.concatenate([x[k:], x[:k]]), power)
-
-
-def stencil_kernel(low_ref, before_ref, own_ref, after_ref, high_ref, stencil_ref,
-                   out_ref, up_ref, down_ref, wide_ref):
+    for side, sign in ((0, -1), (1, 1)):
+        total = jnp.zeros((rows, 128), jnp.float32)
+        for away in range(peers, 0, -1):
+            peer = lax.rem(place + sign * away + peers, peers)
+            total = total * tables_ref[0] + carried_ref[peer, side * rows : (side + 1) * rows, :]
+        sums_ref[side] = total * tables_ref[1]
+        for line in range(lines):
+            for lane in range(across):
+                out_ref[side, line, lane * 128 : (lane + 1) * 128] = sums_ref[side, line * across + lane, :]
+
+
+def stencil_kernel(before_ref, own_ref, after_ref, stencil_ref, own_out, up_out, down_out, far_out,
+                   up_two_out, down_two_out, wide_ref, part_ref):
     reach = CHEB - 1
-    ways = own_ref.shape[0]
-    layers = own_ref.shape[1]
-    half = own_ref.shape[2]
+    ways, layers, half = own_ref.shape[0], own_ref.shape[1], own_ref.shape[2]
     for way in range(ways):
-        column = [
-            functools.partial(lambda ref, i: ref[way, i], ref, i)
-            for ref in (low_ref, before_ref, own_ref, after_ref, high_ref)
-            for i in range(ref.shape[1])
-        ]
         for layer in range(layers):
-            center = reach + layer
-            sums = [column[center]()]
+            wide_ref[layer, 0:half, :] = before_ref[way, layer]
+            wide_ref[layer, half : 2 * half, :] = own_ref[way, layer]
+            wide_ref[layer, 2 * half :, :] = after_ref[way, layer]
+            sums = [own_ref[way, layer]]
             for k in range(1, reach + 1):
-                sums.append(column[center - k]() + column[center + k]())
-            wide_ref[way, layer] = jnp.zeros((3 * half, NX // 2), jnp.float32)
-            for dy in range(reach + 1):
-                total = stencil_ref[0, dy : dy + 1, :] * sums[0]
-                for dz in range(1, reach + 1 - dy):
-                    total = total + stencil_ref[dz, dy : dy + 1, :] * sums[dz]
-                for sign in (-1, 1) if dy > 0 else (1,):
-                    rows = slice(half + sign * dy, 2 * half + sign * dy)
-                    wide_ref[way, layer, rows, :] += total
-            up_ref[way, layer] = wide_ref[way, layer, 0:half, :]
-            out_ref[way, layer] = wide_ref[way, layer, half : 2 * half, :]
-            down_ref[way, layer] = wide_ref[way, layer, 2 * half :, :]
-
-
-def call(kernel, outs, scratch, *args, smem=(), hbm=(), copies=0):
+                sums.append(
+                    wide_ref[layer, half - k : 2 * half - k, :] + wide_ref[layer, half + k : 2 * half + k, :]
+                )
+            for dz in range(reach + 1):
+                total = stencil_ref[dz, 0:1, :] * sums[0]
+                for dy in range(1, reach + 1 - dz):
+                    total = total + stencil_ref[dz, dy : dy + 1, :] * sums[dy]
+                part_ref[layer, dz] = total
+
+        def term(z):
+            near = [part_ref[layer, abs(z - layer)] for layer in range(layers) if abs(z - layer) <= reach]
+            return functools.reduce(lambda a, b: a + b, near)
+
+        for layer in range(layers):
+            own_out[way, layer] = term(layer)
+            up_out[way, layer] = term(layers + layer)
+            down_out[way, layer] = term(layer - layers)
+            far_out[way, layer] = term(4 * layers) if layer == 0 else term(1 - 4 * layers)
+            for block in range(2):
+                up_two_out[way, block * layers + layer] = term((2 + block) * layers + layer)
+                down_two_out[way, block * layers + layer] = term(-(2 + block) * layers + layer)
+
+
+def call(kernel, outs, scratch, *args, smem=(), hbm=(), copies=0, limit=12):
     vmem = pl.BlockSpec(memory_space=pltpu.VMEM)
     spaces = {i: pltpu.SMEM for i in smem} | {i: pltpu.HBM for i in hbm}
     specs = [pl.BlockSpec(memory_space=spaces.get(i, pltpu.VMEM)) for i in range(len(args))]
@@ -402,11 +390,11 @@
         scratch.append(pltpu.SemaphoreType.DMA((copies,)))
     return pl.pallas_call(
         kernel,
-        out_shape=tuple(shape(dims) for dims in outs),
+        out_shape=tuple(shape(dims) if isinstance(dims, tuple) else dims for dims in outs),
         in_specs=specs,
         out_specs=tuple(vmem for _ in outs),
         scratch_shapes=scratch,
-        compiler_params=pltpu.CompilerParams(vmem_limit_bytes=12 * 2**20),
+        compiler_params=pltpu.CompilerParams(vmem_limit_bytes=limit * 2**20),
     )(*args)
 
 
@@ -436,10 +424,25 @@
         start_kernel,
         [full, (depth, PLAN.total, NX), (depth, PLAN.total, NX)],
         [full, pltpu.VMEM(shifts.shape, jnp.int32), pltpu.SMEM(fractions.shape, jnp.float32)],
-        template, shifts, fractions, hbm=(0, 1, 2), copies=3,
+        template, shifts, fractions, hbm=(0, 1, 2), copies=3, limit=60,
     )
     before = shift_to(high, "gy", 1)
     after = shift_to(low, "gy", -1)
+    half, lanes = NX // 2, 128
+    across = NX // lanes
+    fine_x = hartley(NX)
+    coarse_x = np.repeat(hartley(half), 2, axis=0)
+    local, ends, spread, ratio, wrap = smoother_tables(length_y, NX, height)
+    pair_z = np.kron(np.eye(depth // 2), np.ones((1, 2)))
+    pair_y = np.kron(np.eye(height // 2), np.ones((1, 2)))
+    pairs = np.kron(np.eye(3), np.kron(pair_z, pair_y))
+    tables = (
+        target_image,
+        *bf16_pair(np.concatenate([fine_x, coarse_x], axis=1)),
+        jnp.asarray(pairs / 8.0, jnp.bfloat16),
+        f32(ends),
+    )
+    tables = call(load_kernel, [jax.ShapeDtypeStruct(t.shape, t.dtype) for t in tables], [], *tables)
     halos = (before, after, shifts, fractions)
 
     def y_step(step, image, low, high):
@@ -478,58 +481,45 @@
     rows = padded_rows(height + 2)
     (image,) = z_step(2, [(depth, rows, NX)], rows, below, image, above)
     below, above = exchange_z(image, image)
-
-    half, lanes = NX // 2, 128
-    across = NX // lanes
-    groups = peers_y // across
-    share = 2 * 3 * depth // groups
-    fine_x = hartley(NX)
-    coarse_x = np.repeat(hartley(half), 2, axis=0)
-    local, ends, spread, ratio, wrap = smoother_tables(length_y, NX, height)
-    pair_z = np.kron(np.eye(depth // 2), np.ones((1, 2)))
-    pair_y = np.kron(np.eye(height // 2), np.ones((1, 2)))
-    pairs = np.kron(np.eye(3), np.kron(pair_z, pair_y))
+    below, above, tables = lax.optimization_barrier((below, above, tables))
+
     lines = 3 * depth
     coarse_shape = (3, depth // 2, height // 2, half)
     image, spectrum, coarse, parcels = call(
         force_kernel,
-        [full, (lines * height, NX), coarse_shape, (peers_y, share, lanes)],
+        [full, (lines * height, NX), coarse_shape, (peers_y, 2 * lines * across, lanes)],
         [
-            (3 * depth - 3, rows, NX), (depth, rows, NX), (depth, rows, NX), (lines * height, NX), full,
-            pltpu.VMEM((NX, NX + half), jnp.bfloat16), pltpu.VMEM((NX, NX + half), jnp.bfloat16),
-            pltpu.VMEM(pairs.shape, jnp.bfloat16), ends.shape,
+            (3 * depth - 3, rows, NX), (depth, rows, NX), (depth, rows, NX), (lines * height, NX),
+            (2 * lines * across, lanes),
         ],
-        below, image, above, *halos, outer_low, outer_high, target_image,
-        *bf16_pair(np.concatenate([fine_x, coarse_x], axis=1)),
-        jnp.asarray(pairs / 8.0, jnp.bfloat16), f32(ends), smem=(6,), hbm=(9, 10, 11, 12, 13), copies=5,
+        below, image, above, *halos, outer_low, outer_high, *tables, smem=(6,),
     )
 
     carried = lax.all_to_all(parcels, "gy", 0, 0, tiled=True)
-    coarse_low = shift_to(coarse, "gz", 1)
-    coarse_high = shift_to(coarse, "gz", -1)
-    far_low = shift_to(jnp.concatenate([coarse_low[:, 1:], coarse, coarse_high], axis=1), "gz", 3)
-    far_high = shift_to(jnp.concatenate([coarse_low, coarse, coarse_high[:, :1]], axis=1), "gz", -3)
-
-    carried, far_low, far_high = lax.optimization_barrier((carried, far_low, far_high))
+    beside = shift_to(coarse, "gy", 1), shift_to(coarse, "gy", -1)
+    double = (3, depth, height // 2, half)
+    own, up, down, far, up_two, down_two = call(
+        stencil_kernel,
+        [coarse_shape] * 4 + [double] * 2,
+        [(depth // 2, 3 * height // 2, half), (depth // 2, CHEB, height // 2, half)],
+        beside[0], coarse, beside[1], f32(chebyshev_stencil(half)),
+    )
+    from_low = shift_to(up_two, "gz", 2)
+    from_high = shift_to(down_two, "gz", -2)
+    near = depth // 2
+    own = own + shift_to(far, "gz", 4) + from_low[:, :near] + from_high[:, :near]
+    solved = own + shift_to(up + from_low[:, near:], "gz", 1) + shift_to(down + from_high[:, near:], "gz", -1)
+
     place = lax.axis_index("gy").reshape(1).astype(jnp.int32)
-    tables = f32(np.stack([ratio, wrap]).reshape(2, across, lanes).transpose(1, 0, 2))
-    (sums,) = call(carry_kernel, [(peers_y, share, lanes)], [], place, carried, tables, smem=(0,))
-    returned = lax.all_to_all(sums, "gy", 0, 0, tiled=True)
-
-    own, up, down = call(
-        stencil_kernel,
-        [coarse_shape] * 3,
-        [(3, depth // 2, 3 * height // 2, half)],
-        far_low, coarse_low, coarse, coarse_high, far_high, f32(chebyshev_stencil(half)),
-    )
-    solved = own + shift_to(up, "gy", -1) + shift_to(down, "gy", 1)
+    weights = f32(np.tile(np.stack([ratio, wrap]).reshape(2, across, lanes), (1, lines, 1)))
+    (carries,) = call(
+        carry_kernel, [(2, lines, NX)], [(2, lines * across, lanes)], place, carried, weights, smem=(0,)
+    )
 
     spectrum = spectrum.reshape(lines, height, NX)
     smooth = f32(local[0]) * spectrum[:, 0:1]
     for y in range(1, height):
         smooth = smooth + f32(local[y]) * spectrum[:, y : y + 1]
-    carries = returned.reshape(groups, across, share, lanes).transpose(0, 2, 1, 3)
-    carries = carries.reshape(2, lines, NX)
     smooth = smooth + f32(spread[0]) * carries[0][:, None] + f32(spread[1]) * carries[1][:, None]
     smooth = smooth.reshape(lines * height, NX)
     solved = dot(f32(pairs.T), solved.reshape(lines * height // 4, half))

time: 115 us -> 98.6 us (0.86)
  the two profiles are of different devices: /device:TPU:64 before, /device:TPU:1 now
where the time goes in v1:
time: 98.6 us; the launch traced here: 98.1 us
  starting transfers between devices  47.6 us (48%)
  waiting for transfers between devices  27.6 us (28%)
  Pallas kernels  11.7 us (12%)
  local copies, waits for them, and re-layouts  7.24 us (7%)
  matrix products  2.05 us (2%)
  between operations  1.22 us (1%)
    ppermute x19, starting transfers between devices, shift_to(): return lax.ppermute(x, axis, ring(axis, offset))  38.7 us
    ppermute x19, waiting for transfers between devices, shift_to(): return lax.ppermute(x, axis, ring(axis, offset))  19 us
    pallas_call x10, Pallas kernels, call(): pl.pallas_call(kernel, out_shape=tuple((shape(dims) if isinstance(dims, t...  11.7 us
    all_to_all x1, starting transfers between devices, on_device(): carried = lax.all_to_all(parcels, 'gy', 0, 0, tiled=True)  8.83 us
    all_to_all x1, waiting for transfers between devices, on_device(): carried = lax.all_to_all(parcels, 'gy', 0, 0, tiled=True)  8.62 us
    unnamed x72, local copies, waits for them, and re-layouts  6.92 us
    dot_general x3, matrix products, dot(): return jnp.dot(a, b, precision=HIGH, preferred_element_type=jnp.float32)  2.05 us
  transfers between devices with their start and end apart: 20, of which 12 were waited for; matrix products, arithmetic and copies ran while one was open for 2% of the time, Pallas kernels for 0%

profile of v1, /device:TPU:1, one launch (start us, length us, event | category | flops | bytes accessed | tf_op | source)
XLA Modules:
  0.0 98.1 jit_solution(17973024192337907637)
XLA Ops:
  0.6 2.9 %shard_map.302 = (f32[4,16,512]{2,1,0:T(8,128)}, f32[4,29,512]{2,1,0:T(8,128)}, f32[4,29,512]{2,1,0:T(8,128)}) custom-call(f32[4,16,512]{2,1,0:T(8,128)} %image_hbm.1, s32[4,3,4,16,512]{4,3,2,1,0:T(8,128)} %shifts_ref.11, f32[4,3]{1,0:T(4,128)} %fractions_ref.11), custom_call_target="tpu_custom_call" | custom-call | tf_op jit(solution)/shard_map/pallas_call | solution.py:391
  3.5 2.8 %collective-permute-start = (f32[4,29,512]{2,1,0:T(8,128)}, f32[4,29,512]{2,1,0:T(8,128)S(1)}, u32[]{:S(2)}, u32[]{:S(2)}) collective-permute-start(f32[4,29,512]{2,1,0:T(8,128)} %get-tuple-element.34), channel_id=1, source_target_pairs={{0,8},{8,16},{16,24},{24,32},{32,40},{40,48},{48,56},{56,64},{64,7... | collective-permute-start | bytes 712712 | tf_op jit(solution)/shard_map/ppermute | solution.py:79
  6.9 3.0 %collective-permute-done.low_ref.before_ref = f32[4,29,512]{2,1,0:T(8,128)S(1)} collective-permute-done((f32[4,29,512]{2,1,0:T(8,128)}, f32[4,29,512]{2,1,0:T(8,128)S(1)}, u32[]{:S(2)}, u32[]{:S(2)}) %collective-permute-start) | collective-permute-done | bytes 237600 | tf_op jit(solution)/shard_map/ppermute | solution.py:79
  9.9 2.4 %collective-permute-done.1.high_ref.after_ref = f32[4,29,512]{2,1,0:T(8,128)S(1)} collective-permute-done((f32[4,29,512]{2,1,0:T(8,128)}, f32[4,29,512]{2,1,0:T(8,128)S(1)}, u32[]{:S(2)}, u32[]{:S(2)}) %collective-permute-start.1) | collective-permute-done | bytes 237600 | tf_op jit(solution)/shard_map/ppermute | solution.py:79
  14.1 2.0 %collective-permute-start.2 = (f32[3,24,512]{2,1,0:T(8,128)S(1)}, f32[3,24,512]{2,1,0:T(8,128)S(1)}, u32[]{:S(2)}, u32[]{:S(2)}) collective-permute-start(f32[3,24,512]{2,1,0:T(8,128)S(1)} %get-tuple-element.83), channel_id=1, source_target_pairs={{0,1},{1,2},{2,3},{3,4},{4,5},{5,6},{6,7},{7,0},{8,9},{9,10},{10,1... | collective-permute-start | bytes 442376 | tf_op jit(solution)/shard_map/ppermute | solution.py:79
  16.1 4.0 %collective-permute-start.3 = (f32[3,24,512]{2,1,0:T(8,128)S(1)}, f32[3,24,512]{2,1,0:T(8,128)S(1)}, u32[]{:S(2)}, u32[]{:S(2)}) collective-permute-start(f32[3,24,512]{2,1,0:T(8,128)S(1)} %get-tuple-element.82), channel_id=1, source_target_pairs={{0,7},{1,0},{2,1},{3,2},{4,3},{5,4},{6,5},{7,6},{8,15},{9,8},{10,9... | collective-permute-start | bytes 442376 | tf_op jit(solution)/shard_map/ppermute | solution.py:79
  20.1 2.4 %collective-permute-done.2.below_ref = f32[3,24,512]{2,1,0:T(8,128)S(1)} collective-permute-done((f32[3,24,512]{2,1,0:T(8,128)S(1)}, f32[3,24,512]{2,1,0:T(8,128)S(1)}, u32[]{:S(2)}, u32[]{:S(2)}) %collective-permute-start.2) | collective-permute-done | bytes 147488 | tf_op jit(solution)/shard_map/ppermute | solution.py:79
  24.0 2.8 %collective-permute-start.5 = (f32[4,16,512]{2,1,0:T(8,128)S(1)}, f32[4,16,512]{2,1,0:T(8,128)S(1)}, u32[]{:S(2)}, u32[]{:S(2)}) collective-permute-start(f32[4,16,512]{2,1,0:T(8,128)S(1)} %get-tuple-element.38), channel_id=1, source_target_pairs={{0,7},{1,0},{2,1},{3,2},{4,3},{5,4},{6,5},{7,6},{8,15},{9,8},{10,9... | collective-permute-start | bytes 393224 | tf_op jit(solution)/shard_map/ppermute | solution.py:79
  26.8 2.3 %collective-permute-done.4.below_ref.first_ref = f32[4,16,512]{2,1,0:T(8,128)S(1)} collective-permute-done((f32[4,16,512]{2,1,0:T(8,128)S(1)}, f32[4,16,512]{2,1,0:T(8,128)S(1)}, u32[]{:S(2)}, u32[]{:S(2)}) %collective-permute-start.4) | collective-permute-done | bytes 131104 | tf_op jit(solution)/shard_map/ppermute | solution.py:79
  30.1 3.9 %collective-permute-start.6 = (f32[4,7,512]{2,1,0:T(8,128)S(1)}, f32[4,7,512]{2,1,0:T(8,128)S(1)}, u32[]{:S(2)}, u32[]{:S(2)}) collective-permute-start(f32[4,7,512]{2,1,0:T(8,128)S(1)} %get-tuple-element.40), channel_id=1, source_target_pairs={{0,8},{8,16},{16,24},{24,32},{32,40},{40,48},{48,56},{56,64},{64,7... | collective-permute-start | bytes 172040 | tf_op jit(solution)/shard_map/ppermute | solution.py:79
  35.4 2.4 %collective-permute-done.7.high_ref = f32[4,7,512]{2,1,0:T(8,128)S(1)} collective-permute-done((f32[4,7,512]{2,1,0:T(8,128)S(1)}, f32[4,7,512]{2,1,0:T(8,128)S(1)}, u32[]{:S(2)}, u32[]{:S(2)}) %collective-permute-start.7) | collective-permute-done | bytes 57376 | tf_op jit(solution)/shard_map/ppermute | solution.py:79
  38.6 2.4 %collective-permute-start.8 = (f32[3,24,512]{2,1,0:T(8,128)S(1)}, f32[3,24,512]{2,1,0:T(8,128)S(1)}, u32[]{:S(2)}, u32[]{:S(2)}) collective-permute-start(f32[3,24,512]{2,1,0:T(8,128)S(1)} %get-tuple-element.81), channel_id=1, source_target_pairs={{0,1},{1,2},{2,3},{3,4},{4,5},{5,6},{6,7},{7,0},{8,9},{9,10},{10,1... | collective-permute-start | bytes 442376 | tf_op jit(solution)/shard_map/ppermute | solution.py:79
  41.5 2.4 %collective-permute-done.8.below_ref = f32[3,24,512]{2,1,0:T(8,128)S(1)} collective-permute-done((f32[3,24,512]{2,1,0:T(8,128)S(1)}, f32[3,24,512]{2,1,0:T(8,128)S(1)}, u32[]{:S(2)}, u32[]{:S(2)}) %collective-permute-start.8) | collective-permute-done | bytes 147488 | tf_op jit(solution)/shard_map/ppermute | solution.py:79
  46.4 1.5 %collective-permute-start.10 = (f32[4,24,512]{2,1,0:T(8,128)S(1)}, f32[4,24,512]{2,1,0:T(8,128)S(1)}, u32[]{:S(2)}, u32[]{:S(2)}) collective-permute-start(f32[4,24,512]{2,1,0:T(8,128)S(1)} %shard_map.307.image_ref), channel_id=1, source_target_pairs={{0,1},{1,2},{2,3},{3,4},{4,5},{5,6},{6,7},{7,0},{8,9},{9,10},{10,1... | collective-permute-start | bytes 589832 | tf_op jit(solution)/shard_map/ppermute | solution.py:79
  53.0 2.8 %shard_map.309 = (f32[4,16,512]{2,1,0:T(8,128)}, f32[192,512]{1,0:T(8,128)S(1)}, f32[3,2,8,256]{3,2,1,0:T(8,128)S(1)}, f32[32,96,128]{2,1,0:T(8,128)S(1)}) custom-call(f32[4,24,512]{2,1,0:T(8,128)S(1)} %collective-permute-done.10.below_ref, f32[4,24,512]{2,1,0:T(8,128)S(1)} %shard_map.307.image_ref, f32[4,24,512]{2,1,0:T(8,128)} %collective-permute-done.11.above_ref, ...), custom_call_target="tpu_custom_call" | custom-call | tf_op jit(solution)/shard_map/pallas_call | solution.py:391
  56.9 4.8 %collective-permute-start.12 = (f32[3,2,8,256]{3,2,1,0:T(8,128)S(1)}, f32[3,2,8,256]{3,2,1,0:T(8,128)S(1)}, u32[]{:S(2)}, u32[]{:S(2)}) collective-permute-start(f32[3,2,8,256]{3,2,1,0:T(8,128)S(1)} %get-tuple-element.56.own_ref), channel_id=1, source_target_pairs={{0,8},{8,16},{16,24},{24,32},{32,40},{40,48},{48,56},{56,64},{64,7... | collective-permute-start | bytes 147464 | tf_op jit(solution)/shard_map/ppermute | solution.py:79
  61.7 1.6 %collective-permute-start.13 = (f32[3,2,8,256]{3,2,1,0:T(8,128)S(1)}, f32[3,2,8,256]{3,2,1,0:T(8,128)S(1)}, u32[]{:S(2)}, u32[]{:S(2)}) collective-permute-start(f32[3,2,8,256]{3,2,1,0:T(8,128)S(1)} %get-tuple-element.56.own_ref), channel_id=1, source_target_pairs={{0,248},{8,0},{16,8},{24,16},{32,24},{40,32},{48,40},{56,48},{64,5... | collective-permute-start | bytes 147464 | tf_op jit(solution)/shard_map/ppermute | solution.py:79
  63.8 8.8 %all-to-all-start = ((f32[32,96,128]{2,1,0:T(8,128)}), f32[32,96,128]{2,1,0:T(8,128)S(1)}, u32[]{:S(2)}, u32[]{:S(2)}) async-start(f32[32,96,128]{2,1,0:T(8,128)} %copy-done.1), calls=%async_computation | async-start | bytes 3145728 | tf_op jit(solution)/shard_map/all_to_all | solution.py:498
  73.2 1.8 %collective-permute-start.15 = (f32[3,4,8,256]{3,2,1,0:T(8,128)S(1)}, f32[3,4,8,256]{3,2,1,0:T(8,128)S(1)}, u32[]{:S(2)}, u32[]{:S(2)}) collective-permute-start(f32[3,4,8,256]{3,2,1,0:T(8,128)S(1)} %get-tuple-element.59), channel_id=1, source_target_pairs={{0,2},{1,3},{2,4},{3,5},{4,6},{5,7},{6,0},{7,1},{8,10},{9,11},{10,... | collective-permute-start | bytes 294920 | tf_op jit(solution)/shard_map/ppermute | solution.py:79
  75.0 1.8 %collective-permute-start.16 = (f32[3,4,8,256]{3,2,1,0:T(8,128)S(1)}, f32[3,4,8,256]{3,2,1,0:T(8,128)S(1)}, u32[]{:S(2)}, u32[]{:S(2)}) collective-permute-start(f32[3,4,8,256]{3,2,1,0:T(8,128)S(1)} %get-tuple-element.60), channel_id=1, source_target_pairs={{0,6},{1,7},{2,0},{3,1},{4,2},{5,3},{6,4},{7,5},{8,14},{9,15},{10,... | collective-permute-start | bytes 294920 | tf_op jit(solution)/shard_map/ppermute | solution.py:79
  76.9 2.1 %collective-permute-start.14 = (f32[3,2,8,256]{3,2,1,0:T(8,128)S(1)}, f32[3,2,8,256]{3,2,1,0:T(8,128)S(1)}, u32[]{:S(2)}, u32[]{:S(2)}) collective-permute-start(f32[3,2,8,256]{3,2,1,0:T(8,128)S(1)} %get-tuple-element.58), channel_id=1, source_target_pairs={{0,4},{1,5},{2,6},{3,7},{4,0},{5,1},{6,2},{7,3},{8,12},{9,13},{10,... | collective-permute-start | bytes 147464 | tf_op jit(solution)/shard_map/ppermute | solution.py:79
  80.3 2.2 %collective-permute-start.17 = (f32[3,2,8,256]{3,2,1,0:T(8,128)S(1)}, f32[3,2,8,256]{3,2,1,0:T(8,128)S(1)}, u32[]{:S(2)}, u32[]{:S(2)}) collective-permute-start(f32[3,2,8,256]{3,2,1,0:T(8,128)S(1)} %slice_add_fusion.1), channel_id=1, source_target_pairs={{0,1},{1,2},{2,3},{3,4},{4,5},{5,6},{6,7},{7,0},{8,9},{9,10},{10,1... | collective-permute-start | bytes 147464 | tf_op jit(solution)/shard_map/ppermute | solution.py:79
  82.5 2.3 %collective-permute-start.18 = (f32[3,2,8,256]{3,2,1,0:T(8,128)S(1)}, f32[3,2,8,256]{3,2,1,0:T(8,128)S(1)}, u32[]{:S(2)}, u32[]{:S(2)}) collective-permute-start(f32[3,2,8,256]{3,2,1,0:T(8,128)S(1)} %slice_add_fusion), channel_id=1, source_target_pairs={{0,7},{1,0},{2,1},{3,2},{4,3},{5,4},{6,5},{7,6},{8,15},{9,8},{10,9... | collective-permute-start | bytes 147464 | tf_op jit(solution)/shard_map/ppermute | solution.py:79
  86.8 8.6 %all-to-all-done.carried_ref = f32[32,96,128]{2,1,0:T(8,128)S(1)} async-done(((f32[32,96,128]{2,1,0:T(8,128)}), f32[32,96,128]{2,1,0:T(8,128)S(1)}, u32[]{:S(2)}, u32[]{:S(2)}) %all-to-all-start) | async-done | bytes 1572896 | tf_op jit(solution)/shard_map/all_to_all | solution.py:498
  (111 shorter events, 22.7 us)
Async XLA Ops:
  3.5 6.4 %collective-permute-start = (f32[4,29,512]{2,1,0:T(8,128)}, f32[4,29,512]{2,1,0:T(8,128)S(1)}, u32[]{:S(2)}, u32[]{:S(2)}) collective-permute-start(f32[4,29,512]{2,1,0:T(8,128)} %get-tuple-element.34), channel_id=1, source_target_pairs={{0,8},{8,16},{16,24},{24,32},{32,40},{40,48},{48,56},{56,64},{64,7... | collective-permute-start | bytes 712712 | tf_op jit(solution)/shard_map/ppermute | solution.py:79
  6.3 6.0 %collective-permute-start.1 = (f32[4,29,512]{2,1,0:T(8,128)}, f32[4,29,512]{2,1,0:T(8,128)S(1)}, u32[]{:S(2)}, u32[]{:S(2)}) collective-permute-start(f32[4,29,512]{2,1,0:T(8,128)} %get-tuple-element.35), channel_id=1, source_target_pairs={{0,248},{8,0},{16,8},{24,16},{32,24},{40,32},{48,40},{56,48},{64,5... | collective-permute-start | bytes 712712 | tf_op jit(solution)/shard_map/ppermute | solution.py:79
  14.1 8.5 %collective-permute-start.2 = (f32[3,24,512]{2,1,0:T(8,128)S(1)}, f32[3,24,512]{2,1,0:T(8,128)S(1)}, u32[]{:S(2)}, u32[]{:S(2)}) collective-permute-start(f32[3,24,512]{2,1,0:T(8,128)S(1)} %get-tuple-element.83), channel_id=1, source_target_pairs={{0,1},{1,2},{2,3},{3,4},{4,5},{5,6},{6,7},{7,0},{8,9},{9,10},{10,1... | collective-permute-start | bytes 442376 | tf_op jit(solution)/shard_map/ppermute | solution.py:79
  16.1 6.5 %collective-permute-start.3 = (f32[3,24,512]{2,1,0:T(8,128)S(1)}, f32[3,24,512]{2,1,0:T(8,128)S(1)}, u32[]{:S(2)}, u32[]{:S(2)}) collective-permute-start(f32[3,24,512]{2,1,0:T(8,128)S(1)} %get-tuple-element.82), channel_id=1, source_target_pairs={{0,7},{1,0},{2,1},{3,2},{4,3},{5,4},{6,5},{7,6},{8,15},{9,8},{10,9... | collective-permute-start | bytes 442376 | tf_op jit(solution)/shard_map/ppermute | solution.py:79
  23.9 5.2 %collective-permute-start.4 = (f32[4,16,512]{2,1,0:T(8,128)S(1)}, f32[4,16,512]{2,1,0:T(8,128)S(1)}, u32[]{:S(2)}, u32[]{:S(2)}) collective-permute-start(f32[4,16,512]{2,1,0:T(8,128)S(1)} %get-tuple-element.36), channel_id=1, source_target_pairs={{0,1},{1,2},{2,3},{3,4},{4,5},{5,6},{6,7},{7,0},{8,9},{9,10},{10,1... | collective-permute-start | bytes 393224 | tf_op jit(solution)/shard_map/ppermute | solution.py:79
  24.0 5.1 %collective-permute-start.5 = (f32[4,16,512]{2,1,0:T(8,128)S(1)}, f32[4,16,512]{2,1,0:T(8,128)S(1)}, u32[]{:S(2)}, u32[]{:S(2)}) collective-permute-start(f32[4,16,512]{2,1,0:T(8,128)S(1)} %get-tuple-element.38), channel_id=1, source_target_pairs={{0,7},{1,0},{2,1},{3,2},{4,3},{5,4},{6,5},{7,6},{8,15},{9,8},{10,9... | collective-permute-start | bytes 393224 | tf_op jit(solution)/shard_map/ppermute | solution.py:79
  30.1 5.3 %collective-permute-start.6 = (f32[4,7,512]{2,1,0:T(8,128)S(1)}, f32[4,7,512]{2,1,0:T(8,128)S(1)}, u32[]{:S(2)}, u32[]{:S(2)}) collective-permute-start(f32[4,7,512]{2,1,0:T(8,128)S(1)} %get-tuple-element.40), channel_id=1, source_target_pairs={{0,8},{8,16},{16,24},{24,32},{32,40},{40,48},{48,56},{56,64},{64,7... | collective-permute-start | bytes 172040 | tf_op jit(solution)/shard_map/ppermute | solution.py:79
  34.0 3.7 %collective-permute-start.7 = (f32[4,7,512]{2,1,0:T(8,128)S(1)}, f32[4,7,512]{2,1,0:T(8,128)S(1)}, u32[]{:S(2)}, u32[]{:S(2)}) collective-permute-start(f32[4,7,512]{2,1,0:T(8,128)S(1)} %get-tuple-element.41), channel_id=1, source_target_pairs={{0,248},{8,0},{16,8},{24,16},{32,24},{40,32},{48,40},{56,48},{64,5... | collective-permute-start | bytes 172040 | tf_op jit(solution)/shard_map/ppermute | solution.py:79
  38.6 5.4 %collective-permute-start.8 = (f32[3,24,512]{2,1,0:T(8,128)S(1)}, f32[3,24,512]{2,1,0:T(8,128)S(1)}, u32[]{:S(2)}, u32[]{:S(2)}) collective-permute-start(f32[3,24,512]{2,1,0:T(8,128)S(1)} %get-tuple-element.81), channel_id=1, source_target_pairs={{0,1},{1,2},{2,3},{3,4},{4,5},{5,6},{6,7},{7,0},{8,9},{9,10},{10,1... | collective-permute-start | bytes 442376 | tf_op jit(solution)/shard_map/ppermute | solution.py:79
  41.0 4.0 %collective-permute-start.9 = (f32[3,24,512]{2,1,0:T(8,128)S(1)}, f32[3,24,512]{2,1,0:T(8,128)S(1)}, u32[]{:S(2)}, u32[]{:S(2)}) collective-permute-start(f32[3,24,512]{2,1,0:T(8,128)S(1)} %get-tuple-element.80), channel_id=1, source_target_pairs={{0,7},{1,0},{2,1},{3,2},{4,3},{5,4},{6,5},{7,6},{8,15},{9,8},{10,9... | collective-permute-start | bytes 442376 | tf_op jit(solution)/shard_map/ppermute | solution.py:79
  46.4 6.5 %collective-permute-start.10 = (f32[4,24,512]{2,1,0:T(8,128)S(1)}, f32[4,24,512]{2,1,0:T(8,128)S(1)}, u32[]{:S(2)}, u32[]{:S(2)}) collective-permute-start(f32[4,24,512]{2,1,0:T(8,128)S(1)} %shard_map.307.image_ref), channel_id=1, source_target_pairs={{0,1},{1,2},{2,3},{3,4},{4,5},{5,6},{6,7},{7,0},{8,9},{9,10},{10,1... | collective-permute-start | bytes 589832 | tf_op jit(solution)/shard_map/ppermute | solution.py:79
  48.0 5.0 %collective-permute-start.11 = (f32[4,24,512]{2,1,0:T(8,128)S(1)}, f32[4,24,512]{2,1,0:T(8,128)}, u32[]{:S(2)}, u32[]{:S(2)}) collective-permute-start(f32[4,24,512]{2,1,0:T(8,128)S(1)} %shard_map.307.image_ref), channel_id=1, source_target_pairs={{0,7},{1,0},{2,1},{3,2},{4,3},{5,4},{6,5},{7,6},{8,15},{9,8},{10,9... | collective-permute-start | bytes 589832 | tf_op jit(solution)/shard_map/ppermute | solution.py:79
  56.9 15.9 %collective-permute-start.12 = (f32[3,2,8,256]{3,2,1,0:T(8,128)S(1)}, f32[3,2,8,256]{3,2,1,0:T(8,128)S(1)}, u32[]{:S(2)}, u32[]{:S(2)}) collective-permute-start(f32[3,2,8,256]{3,2,1,0:T(8,128)S(1)} %get-tuple-element.56.own_ref), channel_id=1, source_target_pairs={{0,8},{8,16},{16,24},{24,32},{32,40},{40,48},{48,56},{56,64},{64,7... | collective-permute-start | bytes 147464 | tf_op jit(solution)/shard_map/ppermute | solution.py:79
  61.7 11.1 %collective-permute-start.13 = (f32[3,2,8,256]{3,2,1,0:T(8,128)S(1)}, f32[3,2,8,256]{3,2,1,0:T(8,128)S(1)}, u32[]{:S(2)}, u32[]{:S(2)}) collective-permute-start(f32[3,2,8,256]{3,2,1,0:T(8,128)S(1)} %get-tuple-element.56.own_ref), channel_id=1, source_target_pairs={{0,248},{8,0},{16,8},{24,16},{32,24},{40,32},{48,40},{56,48},{64,5... | collective-permute-start | bytes 147464 | tf_op jit(solution)/shard_map/ppermute | solution.py:79
  63.6 21.2 %copy-start.16 = (f32[16,512]{1,0:T(8,128)S(1)}, f32[16,512]{1,0:T(8,128)}, u32[]{:S(2)}) copy-start(f32[16,512]{1,0:T(8,128)} %constant.66.clone) | copy-start | bytes 98308
  63.6 21.2 %copy-start.17 = (f32[16,512]{1,0:T(8,128)S(1)}, f32[16,512]{1,0:T(8,128)}, u32[]{:S(2)}) copy-start(f32[16,512]{1,0:T(8,128)} %constant.67.clone) | copy-start | bytes 98308
  63.6 21.1 %copy-start.18 = (f32[16,512]{1,0:T(8,128)S(1)}, f32[16,512]{1,0:T(8,128)}, u32[]{:S(2)}) copy-start(f32[16,512]{1,0:T(8,128)} %constant.68.clone) | copy-start | bytes 98308
  63.7 21.1 %copy-start.19 = (f32[16,512]{1,0:T(8,128)S(1)}, f32[16,512]{1,0:T(8,128)}, u32[]{:S(2)}) copy-start(f32[16,512]{1,0:T(8,128)} %constant.69.clone) | copy-start | bytes 98308
  63.8 31.6 %all-to-all-start = ((f32[32,96,128]{2,1,0:T(8,128)}), f32[32,96,128]{2,1,0:T(8,128)S(1)}, u32[]{:S(2)}, u32[]{:S(2)}) async-start(f32[32,96,128]{2,1,0:T(8,128)} %copy-done.1), calls=%async_computation | async-start | bytes 3145728 | tf_op jit(solution)/shard_map/all_to_all | solution.py:498
  73.2 7.1 %collective-permute-start.15 = (f32[3,4,8,256]{3,2,1,0:T(8,128)S(1)}, f32[3,4,8,256]{3,2,1,0:T(8,128)S(1)}, u32[]{:S(2)}, u32[]{:S(2)}) collective-permute-start(f32[3,4,8,256]{3,2,1,0:T(8,128)S(1)} %get-tuple-element.59), channel_id=1, source_target_pairs={{0,2},{1,3},{2,4},{3,5},{4,6},{5,7},{6,0},{7,1},{8,10},{9,11},{10,... | collective-permute-start | bytes 294920 | tf_op jit(solution)/shard_map/ppermute | solution.py:79
  75.0 7.5 %collective-permute-start.16 = (f32[3,4,8,256]{3,2,1,0:T(8,128)S(1)}, f32[3,4,8,256]{3,2,1,0:T(8,128)S(1)}, u32[]{:S(2)}, u32[]{:S(2)}) collective-permute-start(f32[3,4,8,256]{3,2,1,0:T(8,128)S(1)} %get-tuple-element.60), channel_id=1, source_target_pairs={{0,6},{1,7},{2,0},{3,1},{4,2},{5,3},{6,4},{7,5},{8,14},{9,15},{10,... | collective-permute-start | bytes 294920 | tf_op jit(solution)/shard_map/ppermute | solution.py:79
  76.9 8.6 %collective-permute-start.14 = (f32[3,2,8,256]{3,2,1,0:T(8,128)S(1)}, f32[3,2,8,256]{3,2,1,0:T(8,128)S(1)}, u32[]{:S(2)}, u32[]{:S(2)}) collective-permute-start(f32[3,2,8,256]{3,2,1,0:T(8,128)S(1)} %get-tuple-element.58), channel_id=1, source_target_pairs={{0,4},{1,5},{2,6},{3,7},{4,0},{5,1},{6,2},{7,3},{8,12},{9,13},{10,... | collective-permute-start | bytes 147464 | tf_op jit(solution)/shard_map/ppermute | solution.py:79
  80.3 5.3 %collective-permute-start.17 = (f32[3,2,8,256]{3,2,1,0:T(8,128)S(1)}, f32[3,2,8,256]{3,2,1,0:T(8,128)S(1)}, u32[]{:S(2)}, u32[]{:S(2)}) collective-permute-start(f32[3,2,8,256]{3,2,1,0:T(8,128)S(1)} %slice_add_fusion.1), channel_id=1, source_target_pairs={{0,1},{1,2},{2,3},{3,4},{4,5},{5,6},{6,7},{7,0},{8,9},{9,10},{10,1... | collective-permute-start | bytes 147464 | tf_op jit(solution)/shard_map/ppermute | solution.py:79
  82.5 3.4 %collective-permute-start.18 = (f32[3,2,8,256]{3,2,1,0:T(8,128)S(1)}, f32[3,2,8,256]{3,2,1,0:T(8,128)S(1)}, u32[]{:S(2)}, u32[]{:S(2)}) collective-permute-start(f32[3,2,8,256]{3,2,1,0:T(8,128)S(1)} %slice_add_fusion), channel_id=1, source_target_pairs={{0,7},{1,0},{2,1},{3,2},{4,3},{5,4},{6,5},{7,6},{8,15},{9,8},{10,9... | collective-permute-start | bytes 147464 | tf_op jit(solution)/shard_map/ppermute | solution.py:79
  (28 other events, 359.5 us)

commit v2 on v1

--- a/solution.py
+++ b/solution.py
@@ -108,10 +108,31 @@
     return choose(moves, [turn(filtered, -offset) for offset in (-2, -1, 0, 1)])
 
 
+LANES = 128
+ACROSS = NX // LANES
+
+
+def lane_part(value, lane):
+    return value[:, lane * LANES : (lane + 1) * LANES]
+
+
+def read_lanes(ref, layer, start, stop):
+    return jnp.concatenate([ref[layer, lane, start:stop, :] for lane in range(ACROSS)], axis=1)
+
+
+def write_lanes(ref, layer, start, value):
+    for lane in range(ACROSS):
+        ref[layer, lane, start : start + value.shape[0], :] = lane_part(value, lane)
+
+
 def y_pass(padded_ref, filtered_ref, layer, rows, moves, w):
-    parts = [padded_ref[layer, node : node + rows + 3, :] for node in range(4)]
-    filtered_ref[layer, 0 : rows + 3, :] = blend(w, parts)
-    return choose(moves, [filtered_ref[layer, k : k + rows, :] for k in range(4)])
+    results = []
+    for lane in range(ACROSS):
+        parts = [padded_ref[layer, lane, node : node + rows + 3, :] for node in range(4)]
+        filtered_ref[layer, lane, 0 : rows + 3, :] = blend(w, parts)
+        parts = [filtered_ref[layer, lane, k : k + rows, :] for k in range(4)]
+        results.append(choose(lane_part(moves, lane), parts))
+    return jnp.concatenate(results, axis=1)
 
 
 def z_filter(layers, filtered_ref, w):
@@ -138,12 +159,11 @@
 def store_wide(wide_ref, layer, before, own, after):
     place = 0
     for part in (before, own, after):
-        if part is not None:
-            wide_ref[layer, place : place + part.shape[0], :] = part
-            place = place + part.shape[0]
-    rest = wide_ref.shape[1] - place
+        write_lanes(wide_ref, layer, place, part)
+        place = place + part.shape[0]
+    rest = wide_ref.shape[2] - place
     if rest > 0:
-        wide_ref[layer, place:, :] = jnp.zeros((rest, NX), wide_ref.dtype)
+        write_lanes(wide_ref, layer, place, jnp.zeros((rest, NX), wide_ref.dtype))
 
 
 class Plan:
@@ -184,7 +204,7 @@
             own.astype(jnp.float32),
             after_ref[layer, start:stop, :],
         )
-        return wide_ref[layer]
+        return read_lanes(wide_ref, layer, 0, wide_ref.shape[2])
 
 
 PLAN = Plan(1)
@@ -200,15 +220,19 @@
 
 def start_kernel(image_hbm, shifts_hbm, fractions_hbm, out_ref, low_ref, high_ref,
                  image_ref, shifts_ref, fractions_ref, sems):
-    copies = copies_of(
-        ((fractions_hbm, fractions_ref), (image_hbm, image_ref), (shifts_hbm, shifts_ref)), sems
-    )
-    for copy in copies:
+    keys = [(0, 0), *PLAN.places]
+    pairs = [(fractions_hbm, fractions_ref), (image_hbm, image_ref)]
+    pairs += [(shifts_hbm.at[step, way], shifts_ref.at[step, way]) for step, way in keys]
+    copies = copies_of(pairs, sems)
+    for copy in copies[:3]:
         copy.wait()
     w = weights_at(fractions_ref, 0, 0)
     depth = image_ref.shape[0]
     for layer in range(depth):
         out_ref[layer] = x_pass(image_ref[layer], shifts_ref[0, 0, layer], w)
+    for copy in copies[3:]:
+        copy.wait()
+    for layer in range(depth):
         low_ref[layer, 0 : PLAN.first, :] = out_ref[layer, 0 : PLAN.first, :]
         high_ref[layer, 0 : PLAN.first, :] = out_ref[layer, HEIGHT - PLAN.first :, :]
         for key, place in PLAN.places.items():
@@ -251,9 +275,9 @@
             outs[1][layer, 0 : PLAN.second, :] = outs[0][layer, 0 : PLAN.second, :]
             outs[2][layer, 0 : PLAN.second, :] = outs[0][layer, HEIGHT - PLAN.second :, :]
             continue
-        padded_ref[layer, 0:rows, :] = value
-        padded_ref[layer, rows:, :] = jnp.zeros((padded_ref.shape[1] - rows, NX), jnp.float32)
-        moves = PLAN.moves(refs, (step + 1, 1), layer, wide_ref.at[:, 0:rows_out, :])
+        write_lanes(padded_ref, layer, 0, value)
+        write_lanes(padded_ref, layer, rows, jnp.zeros((padded_ref.shape[2] - rows, NX), jnp.float32))
+        moves = PLAN.moves(refs, (step + 1, 1), layer, wide_ref.at[:, :, 0:rows_out, :])
         value = y_pass(padded_ref, filtered_y_ref, layer, rows_out, moves, wy)
         outs[0][layer] = value
         if len(outs) > 1:
@@ -282,23 +306,23 @@
     refs = (before_ref, after_ref, shifts_ref)
     depth = image_ref.shape[0]
     z_filter(layers_of(below_ref, image_ref, above_ref, 4), filtered_ref, weights_at(fractions_ref, 3, 2))
-    own = slice(1, 1 + HEIGHT)
-    outer = []
-    for moves_ref, base in ((first_ref, 0), (last_ref, depth + 1)):
-        outer.append(choose(moves_ref[3], [filtered_ref[base + k, own, :] for k in range(4)]))
+    blank = jnp.zeros((1, NX), jnp.float32)
+    for layer in range(-1, depth + 1):
+        if 0 <= layer < depth:
+            moves = PLAN.moves(refs, (3, 2), layer, wide_ref)
+        else:
+            store_wide(wide_ref, 0, blank, (first_ref if layer < 0 else last_ref)[3], blank)
+            moves = read_lanes(wide_ref, 0, 0, wide_ref.shape[2])
+        write_lanes(frame_ref, layer + 1, 0, choose(moves, [filtered_ref[layer + 1 + k] for k in range(4)]))
+    frames = [read_lanes(frame_ref, layer, 1, 1 + HEIGHT) for layer in range(depth + 2)]
     for layer in range(depth):
-        moves = PLAN.moves(refs, (3, 2), layer, wide_ref)
-        frame_ref[layer] = choose(moves, [filtered_ref[layer + 1 + k] for k in range(4)])
-    for layer in range(depth):
-        image = frame_ref[layer, own, :]
+        image = frames[layer + 1]
         out_ref[layer] = image
         miss = (image - target_ref[layer]) * 0.5
-        below = outer[0] if layer == 0 else frame_ref[layer - 1, own, :]
-        above = outer[1] if layer == depth - 1 else frame_ref[layer + 1, own, :]
         slopes = (
             pltpu.roll(image, NX - 1, 1) - pltpu.roll(image, 1, 1),
-            frame_ref[layer, 2 : 2 + HEIGHT, :] - frame_ref[layer, 0:HEIGHT, :],
-            above - below,
+            read_lanes(frame_ref, layer + 1, 2, 2 + HEIGHT) - read_lanes(frame_ref, layer + 1, 0, HEIGHT),
+            frames[layer + 2] - frames[layer],
         )
         for way in range(3):
             place = (way * depth + layer) * HEIGHT
@@ -424,10 +448,12 @@
         start_kernel,
         [full, (depth, PLAN.total, NX), (depth, PLAN.total, NX)],
         [full, pltpu.VMEM(shifts.shape, jnp.int32), pltpu.SMEM(fractions.shape, jnp.float32)],
-        template, shifts, fractions, hbm=(0, 1, 2), copies=3, limit=60,
+        template, shifts, fractions, hbm=(0, 1, 2), copies=3 + len(PLAN.places), limit=60,
     )
     before = shift_to(high, "gy", 1)
     after = shift_to(low, "gy", -1)
+    (image,) = call(load_kernel, [jax.ShapeDtypeStruct(full, jnp.float32)], [], image)
+    before, after, image = lax.optimization_barrier((before, after, image))
     half, lanes = NX // 2, 128
     across = NX // lanes
     fine_x = hartley(NX)
@@ -450,7 +476,7 @@
         (image,) = call(
             functools.partial(y_kernel, step),
             [(depth, rows, NX)],
-            [(depth, rows + 8, NX), (depth, rows + 8, NX), (depth, rows, NX)],
+            [(depth, ACROSS, rows + 8, LANES)] * 2 + [(depth, ACROSS, rows, LANES)],
             image, low, high, *halos, smem=(6,),
         )
         return image, image[:3], image[depth - 3 :]
@@ -464,7 +490,7 @@
         return call(
             functools.partial(z_x_y_kernel, step, rows_out),
             outs,
-            [(depth, rows + 8, NX), (depth, rows + 8, NX), (depth + 2 * layers - 3, rows, NX), (depth, rows, NX)],
+            [(depth, ACROSS, rows + 8, LANES)] * 2 + [(depth + 2 * layers - 3, rows, NX), (depth, ACROSS, rows, LANES)],
             below, image, above, *halos, smem=(6,),
         )
 
@@ -481,6 +507,7 @@
     rows = padded_rows(height + 2)
     (image,) = z_step(2, [(depth, rows, NX)], rows, below, image, above)
     below, above = exchange_z(image, image)
+    place = lax.axis_index("gy").reshape(1).astype(jnp.int32)
     below, above, tables = lax.optimization_barrier((below, above, tables))
 
     lines = 3 * depth
@@ -489,7 +516,7 @@
         force_kernel,
         [full, (lines * height, NX), coarse_shape, (peers_y, 2 * lines * across, lanes)],
         [
-            (3 * depth - 3, rows, NX), (depth, rows, NX), (depth, rows, NX), (lines * height, NX),
+            (3 * depth - 3, rows, NX), (depth, ACROSS, rows, LANES), (depth + 2, ACROSS, rows, LANES), (lines * height, NX),
             (2 * lines * across, lanes),
         ],
         below, image, above, *halos, outer_low, outer_high, *tables, smem=(6,),
@@ -504,13 +531,15 @@
         [(depth // 2, 3 * height // 2, half), (depth // 2, CHEB, height // 2, half)],
         beside[0], coarse, beside[1], f32(chebyshev_stencil(half)),
     )
+    own, spectrum, back_x = lax.optimization_barrier((own, spectrum, f32(-fine_x)))
     from_low = shift_to(up_two, "gz", 2)
     from_high = shift_to(down_two, "gz", -2)
     near = depth // 2
     own = own + shift_to(far, "gz", 4) + from_low[:, :near] + from_high[:, :near]
     solved = own + shift_to(up + from_low[:, near:], "gz", 1) + shift_to(down + from_high[:, near:], "gz", -1)
 
-    place = lax.axis_index("gy").reshape(1).astype(jnp.int32)
+    (back_x,) = call(load_kernel, [jax.ShapeDtypeStruct((NX, NX), jnp.float32)], [], back_x)
+    carried, back_x = lax.optimization_barrier((carried, back_x))
     weights = f32(np.tile(np.stack([ratio, wrap]).reshape(2, across, lanes), (1, lines, 1)))
     (carries,) = call(
         carry_kernel, [(2, lines, NX)], [(2, lines * across, lanes)], place, carried, weights, smem=(0,)
@@ -523,7 +552,7 @@
     smooth = smooth + f32(spread[0]) * carries[0][:, None] + f32(spread[1]) * carries[1][:, None]
     smooth = smooth.reshape(lines * height, NX)
     solved = dot(f32(pairs.T), solved.reshape(lines * height // 4, half))
-    update = dot(smooth, f32(-fine_x)) + dot(solved, f32(-coarse_x.T))
+    update = dot(smooth, back_x) + dot(solved, f32(-coarse_x.T))
     return (update.reshape(3, depth, height, NX), image)
 
 

time: 98.6 us -> 94.2 us (0.955)
  local copies, waits for them, and re-layouts: 7.24 us -> 1.82 us
  waiting for transfers between devices: 27.6 us -> 28.8 us
    unnamed x72 -> x70, local copies, waits for them, and re-layouts: 6.92 us -> 1.5 us
    ppermute x19, waiting for transfers between devices: 19 us -> 20.9 us  [shift_to(): return lax.ppermute(x, axis, ring(axis, offset))]
    pallas_call x10 -> x12, Pallas kernels: 11.7 us -> 11.3 us  [call(): pl.pallas_call(kernel, out_shape=tuple((shape(dims) if isinstance(dims, t...]
  transfers between devices with their start and end apart: 20 -> 20, of which waited for: 12 -> 13; matrix products, arithmetic and copies ran while one was open for 2% -> 2% of each run, Pallas kernels for 0% -> 1%
where the time goes in v2:
time: 94.2 us; the launch traced here: 94 us
  starting transfers between devices  48.1 us (51%)
  waiting for transfers between devices  28.8 us (31%)
  Pallas kernels  11.3 us (12%)
  matrix products  2.04 us (2%)
  local copies, waits for them, and re-layouts  1.82 us (2%)
  between operations  1.26 us (1%)
    ppermute x19, starting transfers between devices, shift_to(): return lax.ppermute(x, axis, ring(axis, offset))  39.3 us
    ppermute x19, waiting for transfers between devices, shift_to(): return lax.ppermute(x, axis, ring(axis, offset))  20.9 us
    pallas_call x12, Pallas kernels, call(): pl.pallas_call(kernel, out_shape=tuple((shape(dims) if isinstance(dims, t...  11.3 us
    all_to_all x1, starting transfers between devices, on_device(): carried = lax.all_to_all(parcels, 'gy', 0, 0, tiled=True)  8.82 us
    all_to_all x1, waiting for transfers between devices, on_device(): carried = lax.all_to_all(parcels, 'gy', 0, 0, tiled=True)  7.89 us
    dot_general x3, matrix products, dot(): return jnp.dot(a, b, precision=HIGH, preferred_element_type=jnp.float32)  2.04 us
  transfers between devices with their start and end apart: 20, of which 13 were waited for; matrix products, arithmetic and copies ran while one was open for 2% of the time, Pallas kernels for 1%

profile of v2, /device:TPU:1, one launch (start us, length us, event | category | flops | bytes accessed | tf_op | source)
XLA Modules:
  0.0 94.0 jit_solution(1781997947174630202)
XLA Ops:
  0.6 2.6 %shard_map.302 = (f32[4,16,512]{2,1,0:T(8,128)}, f32[4,29,512]{2,1,0:T(8,128)}, f32[4,29,512]{2,1,0:T(8,128)}) custom-call(f32[4,16,512]{2,1,0:T(8,128)} %image_hbm.1, s32[4,3,4,16,512]{4,3,2,1,0:T(8,128)} %shifts_ref.11, f32[4,3]{1,0:T(4,128)} %fractions_ref.11), custom_call_target="tpu_custom_call" | custom-call | tf_op jit(solution)/shard_map/pallas_call | solution.py:415
  3.2 2.8 %collective-permute-start = (f32[4,29,512]{2,1,0:T(8,128)}, f32[4,29,512]{2,1,0:T(8,128)S(1)}, u32[]{:S(2)}, u32[]{:S(2)}) collective-permute-start(f32[4,29,512]{2,1,0:T(8,128)} %get-tuple-element.41), channel_id=1, source_target_pairs={{0,8},{8,16},{16,24},{24,32},{32,40},{40,48},{48,56},{56,64},{64,7... | collective-permute-start | bytes 712712 | tf_op jit(solution)/shard_map/ppermute | solution.py:79
  7.5 2.1 %collective-permute-done.low_ref.before_ref = f32[4,29,512]{2,1,0:T(8,128)S(1)} collective-permute-done((f32[4,29,512]{2,1,0:T(8,128)}, f32[4,29,512]{2,1,0:T(8,128)S(1)}, u32[]{:S(2)}, u32[]{:S(2)}) %collective-permute-start) | collective-permute-done | bytes 237600 | tf_op jit(solution)/shard_map/ppermute | solution.py:79
  9.6 2.4 %collective-permute-done.1.high_ref.after_ref = f32[4,29,512]{2,1,0:T(8,128)S(1)} collective-permute-done((f32[4,29,512]{2,1,0:T(8,128)}, f32[4,29,512]{2,1,0:T(8,128)S(1)}, u32[]{:S(2)}, u32[]{:S(2)}) %collective-permute-start.1) | collective-permute-done | bytes 237600 | tf_op jit(solution)/shard_map/ppermute | solution.py:79
  12.8 2.0 %collective-permute-start.2 = (f32[3,24,512]{2,1,0:T(8,128)S(1)}, f32[3,24,512]{2,1,0:T(8,128)S(1)}, u32[]{:S(2)}, u32[]{:S(2)}) collective-permute-start(f32[3,24,512]{2,1,0:T(8,128)S(1)} %get-tuple-element.99), channel_id=1, source_target_pairs={{0,1},{1,2},{2,3},{3,4},{4,5},{5,6},{6,7},{7,0},{8,9},{9,10},{10,1... | collective-permute-start | bytes 442376 | tf_op jit(solution)/shard_map/ppermute | solution.py:79
  14.8 4.0 %collective-permute-start.3 = (f32[3,24,512]{2,1,0:T(8,128)S(1)}, f32[3,24,512]{2,1,0:T(8,128)S(1)}, u32[]{:S(2)}, u32[]{:S(2)}) collective-permute-start(f32[3,24,512]{2,1,0:T(8,128)S(1)} %get-tuple-element.98), channel_id=1, source_target_pairs={{0,7},{1,0},{2,1},{3,2},{4,3},{5,4},{6,5},{7,6},{8,15},{9,8},{10,9... | collective-permute-start | bytes 442376 | tf_op jit(solution)/shard_map/ppermute | solution.py:79
  18.8 2.4 %collective-permute-done.2.below_ref = f32[3,24,512]{2,1,0:T(8,128)S(1)} collective-permute-done((f32[3,24,512]{2,1,0:T(8,128)S(1)}, f32[3,24,512]{2,1,0:T(8,128)S(1)}, u32[]{:S(2)}, u32[]{:S(2)}) %collective-permute-start.2) | collective-permute-done | bytes 147488 | tf_op jit(solution)/shard_map/ppermute | solution.py:79
  22.7 2.8 %collective-permute-start.5 = (f32[4,16,512]{2,1,0:T(8,128)S(1)}, f32[4,16,512]{2,1,0:T(8,128)S(1)}, u32[]{:S(2)}, u32[]{:S(2)}) collective-permute-start(f32[4,16,512]{2,1,0:T(8,128)S(1)} %get-tuple-element.49), channel_id=1, source_target_pairs={{0,7},{1,0},{2,1},{3,2},{4,3},{5,4},{6,5},{7,6},{8,15},{9,8},{10,9... | collective-permute-start | bytes 393224 | tf_op jit(solution)/shard_map/ppermute | solution.py:79
  25.5 2.3 %collective-permute-done.4.below_ref.first_ref = f32[4,16,512]{2,1,0:T(8,128)S(1)} collective-permute-done((f32[4,16,512]{2,1,0:T(8,128)S(1)}, f32[4,16,512]{2,1,0:T(8,128)S(1)}, u32[]{:S(2)}, u32[]{:S(2)}) %collective-permute-start.4) | collective-permute-done | bytes 131104 | tf_op jit(solution)/shard_map/ppermute | solution.py:79
  28.8 3.9 %collective-permute-start.6 = (f32[4,7,512]{2,1,0:T(8,128)S(1)}, f32[4,7,512]{2,1,0:T(8,128)S(1)}, u32[]{:S(2)}, u32[]{:S(2)}) collective-permute-start(f32[4,7,512]{2,1,0:T(8,128)S(1)} %get-tuple-element.51), channel_id=1, source_target_pairs={{0,8},{8,16},{16,24},{24,32},{32,40},{40,48},{48,56},{56,64},{64,7... | collective-permute-start | bytes 172040 | tf_op jit(solution)/shard_map/ppermute | solution.py:79
  34.0 2.4 %collective-permute-done.7.high_ref = f32[4,7,512]{2,1,0:T(8,128)S(1)} collective-permute-done((f32[4,7,512]{2,1,0:T(8,128)S(1)}, f32[4,7,512]{2,1,0:T(8,128)S(1)}, u32[]{:S(2)}, u32[]{:S(2)}) %collective-permute-start.7) | collective-permute-done | bytes 57376 | tf_op jit(solution)/shard_map/ppermute | solution.py:79
  37.2 2.4 %collective-permute-start.8 = (f32[3,24,512]{2,1,0:T(8,128)S(1)}, f32[3,24,512]{2,1,0:T(8,128)S(1)}, u32[]{:S(2)}, u32[]{:S(2)}) collective-permute-start(f32[3,24,512]{2,1,0:T(8,128)S(1)} %get-tuple-element.97), channel_id=1, source_target_pairs={{0,1},{1,2},{2,3},{3,4},{4,5},{5,6},{6,7},{7,0},{8,9},{9,10},{10,1... | collective-permute-start | bytes 442376 | tf_op jit(solution)/shard_map/ppermute | solution.py:79
  40.2 2.4 %collective-permute-done.8.below_ref = f32[3,24,512]{2,1,0:T(8,128)S(1)} collective-permute-done((f32[3,24,512]{2,1,0:T(8,128)S(1)}, f32[3,24,512]{2,1,0:T(8,128)S(1)}, u32[]{:S(2)}, u32[]{:S(2)}) %collective-permute-start.8) | collective-permute-done | bytes 147488 | tf_op jit(solution)/shard_map/ppermute | solution.py:79
  47.9 2.9 %collective-permute-done.10.below_ref = f32[4,24,512]{2,1,0:T(8,128)S(1)} collective-permute-done((f32[4,24,512]{2,1,0:T(8,128)S(1)}, f32[4,24,512]{2,1,0:T(8,128)S(1)}, u32[]{:S(2)}, u32[]{:S(2)}) %collective-permute-start.10) | collective-permute-done | bytes 196640 | tf_op jit(solution)/shard_map/ppermute | solution.py:79
  51.1 2.8 %shard_map.310 = (f32[4,16,512]{2,1,0:T(8,128)}, f32[192,512]{1,0:T(8,128)S(1)}, f32[3,2,8,256]{3,2,1,0:T(8,128)S(1)}, f32[32,96,128]{2,1,0:T(8,128)}) custom-call(f32[4,24,512]{2,1,0:T(8,128)S(1)} %collective-permute-done.10.below_ref, f32[4,24,512]{2,1,0:T(8,128)S(1)} %shard_map.308.image_ref, f32[4,24,512]{2,1,0:T(8,128)S(1)} %collective-permute-done.11.above_ref, ...), custom_call_target="tpu_custom_call" | custom-call | tf_op jit(solution)/shard_map/pallas_call | solution.py:415
  53.9 5.1 %collective-permute-start.12 = (f32[3,2,8,256]{3,2,1,0:T(8,128)S(1)}, f32[3,2,8,256]{3,2,1,0:T(8,128)S(1)}, u32[]{:S(2)}, u32[]{:S(2)}) collective-permute-start(f32[3,2,8,256]{3,2,1,0:T(8,128)S(1)} %get-tuple-element.65.own_ref), channel_id=1, source_target_pairs={{0,8},{8,16},{16,24},{24,32},{32,40},{40,48},{48,56},{56,64},{64,7... | collective-permute-start | bytes 147464 | tf_op jit(solution)/shard_map/ppermute | solution.py:79
  59.0 1.6 %collective-permute-start.13 = (f32[3,2,8,256]{3,2,1,0:T(8,128)S(1)}, f32[3,2,8,256]{3,2,1,0:T(8,128)S(1)}, u32[]{:S(2)}, u32[]{:S(2)}) collective-permute-start(f32[3,2,8,256]{3,2,1,0:T(8,128)S(1)} %get-tuple-element.65.own_ref), channel_id=1, source_target_pairs={{0,248},{8,0},{16,8},{24,16},{32,24},{40,32},{48,40},{56,48},{64,5... | collective-permute-start | bytes 147464 | tf_op jit(solution)/shard_map/ppermute | solution.py:79
  60.7 8.8 %all-to-all-start = ((f32[32,96,128]{2,1,0:T(8,128)}), f32[32,96,128]{2,1,0:T(8,128)S(1)}, u32[]{:S(2)}, u32[]{:S(2)}) async-start(f32[32,96,128]{2,1,0:T(8,128)} %get-tuple-element.69), calls=%async_computation | async-start | bytes 3145728 | tf_op jit(solution)/shard_map/all_to_all | solution.py:525
  70.4 1.8 %collective-permute-start.15 = (f32[3,4,8,256]{3,2,1,0:T(8,128)S(1)}, f32[3,4,8,256]{3,2,1,0:T(8,128)S(1)}, u32[]{:S(2)}, u32[]{:S(2)}) collective-permute-start(f32[3,4,8,256]{3,2,1,0:T(8,128)S(1)} %get-tuple-element.75), channel_id=1, source_target_pairs={{0,2},{1,3},{2,4},{3,5},{4,6},{5,7},{6,0},{7,1},{8,10},{9,11},{10,... | collective-permute-start | bytes 294920 | tf_op jit(solution)/shard_map/ppermute | solution.py:79
  72.2 1.8 %collective-permute-start.16 = (f32[3,4,8,256]{3,2,1,0:T(8,128)S(1)}, f32[3,4,8,256]{3,2,1,0:T(8,128)S(1)}, u32[]{:S(2)}, u32[]{:S(2)}) collective-permute-start(f32[3,4,8,256]{3,2,1,0:T(8,128)S(1)} %get-tuple-element.76), channel_id=1, source_target_pairs={{0,6},{1,7},{2,0},{3,1},{4,2},{5,3},{6,4},{7,5},{8,14},{9,15},{10,... | collective-permute-start | bytes 294920 | tf_op jit(solution)/shard_map/ppermute | solution.py:79
  74.0 1.8 %collective-permute-start.14 = (f32[3,2,8,256]{3,2,1,0:T(8,128)S(1)}, f32[3,2,8,256]{3,2,1,0:T(8,128)S(1)}, u32[]{:S(2)}, u32[]{:S(2)}) collective-permute-start(f32[3,2,8,256]{3,2,1,0:T(8,128)S(1)} %get-tuple-element.74), channel_id=1, source_target_pairs={{0,4},{1,5},{2,6},{3,7},{4,0},{5,1},{6,2},{7,3},{8,12},{9,13},{10,... | collective-permute-start | bytes 147464 | tf_op jit(solution)/shard_map/ppermute | solution.py:79
  77.1 2.6 %collective-permute-start.17 = (f32[3,2,8,256]{3,2,1,0:T(8,128)S(1)}, f32[3,2,8,256]{3,2,1,0:T(8,128)S(1)}, u32[]{:S(2)}, u32[]{:S(2)}) collective-permute-start(f32[3,2,8,256]{3,2,1,0:T(8,128)S(1)} %slice_add_fusion.1), channel_id=1, source_target_pairs={{0,1},{1,2},{2,3},{3,4},{4,5},{5,6},{6,7},{7,0},{8,9},{9,10},{10,1... | collective-permute-start | bytes 147464 | tf_op jit(solution)/shard_map/ppermute | solution.py:79
  79.7 2.3 %collective-permute-start.18 = (f32[3,2,8,256]{3,2,1,0:T(8,128)S(1)}, f32[3,2,8,256]{3,2,1,0:T(8,128)S(1)}, u32[]{:S(2)}, u32[]{:S(2)}) collective-permute-start(f32[3,2,8,256]{3,2,1,0:T(8,128)S(1)} %slice_add_fusion), channel_id=1, source_target_pairs={{0,7},{1,0},{2,1},{3,2},{4,3},{5,4},{6,5},{7,6},{8,15},{9,8},{10,9... | collective-permute-start | bytes 147464 | tf_op jit(solution)/shard_map/ppermute | solution.py:79
  84.4 7.9 %all-to-all-done.carried_ref = f32[32,96,128]{2,1,0:T(8,128)S(1)} async-done(((f32[32,96,128]{2,1,0:T(8,128)}), f32[32,96,128]{2,1,0:T(8,128)S(1)}, u32[]{:S(2)}, u32[]{:S(2)}) %all-to-all-start) | async-done | bytes 1572896 | tf_op jit(solution)/shard_map/all_to_all | solution.py:525
  (111 shorter events, 18.6 us)
Async XLA Ops:
  3.2 6.4 %collective-permute-start = (f32[4,29,512]{2,1,0:T(8,128)}, f32[4,29,512]{2,1,0:T(8,128)S(1)}, u32[]{:S(2)}, u32[]{:S(2)}) collective-permute-start(f32[4,29,512]{2,1,0:T(8,128)} %get-tuple-element.41), channel_id=1, source_target_pairs={{0,8},{8,16},{16,24},{24,32},{32,40},{40,48},{48,56},{56,64},{64,7... | collective-permute-start | bytes 712712 | tf_op jit(solution)/shard_map/ppermute | solution.py:79
  6.0 6.0 %collective-permute-start.1 = (f32[4,29,512]{2,1,0:T(8,128)}, f32[4,29,512]{2,1,0:T(8,128)S(1)}, u32[]{:S(2)}, u32[]{:S(2)}) collective-permute-start(f32[4,29,512]{2,1,0:T(8,128)} %get-tuple-element.42), channel_id=1, source_target_pairs={{0,248},{8,0},{16,8},{24,16},{32,24},{40,32},{48,40},{56,48},{64,5... | collective-permute-start | bytes 712712 | tf_op jit(solution)/shard_map/ppermute | solution.py:79
  12.8 8.5 %collective-permute-start.2 = (f32[3,24,512]{2,1,0:T(8,128)S(1)}, f32[3,24,512]{2,1,0:T(8,128)S(1)}, u32[]{:S(2)}, u32[]{:S(2)}) collective-permute-start(f32[3,24,512]{2,1,0:T(8,128)S(1)} %get-tuple-element.99), channel_id=1, source_target_pairs={{0,1},{1,2},{2,3},{3,4},{4,5},{5,6},{6,7},{7,0},{8,9},{9,10},{10,1... | collective-permute-start | bytes 442376 | tf_op jit(solution)/shard_map/ppermute | solution.py:79
  14.8 6.5 %collective-permute-start.3 = (f32[3,24,512]{2,1,0:T(8,128)S(1)}, f32[3,24,512]{2,1,0:T(8,128)S(1)}, u32[]{:S(2)}, u32[]{:S(2)}) collective-permute-start(f32[3,24,512]{2,1,0:T(8,128)S(1)} %get-tuple-element.98), channel_id=1, source_target_pairs={{0,7},{1,0},{2,1},{3,2},{4,3},{5,4},{6,5},{7,6},{8,15},{9,8},{10,9... | collective-permute-start | bytes 442376 | tf_op jit(solution)/shard_map/ppermute | solution.py:79
  22.6 5.2 %collective-permute-start.4 = (f32[4,16,512]{2,1,0:T(8,128)S(1)}, f32[4,16,512]{2,1,0:T(8,128)S(1)}, u32[]{:S(2)}, u32[]{:S(2)}) collective-permute-start(f32[4,16,512]{2,1,0:T(8,128)S(1)} %get-tuple-element.47), channel_id=1, source_target_pairs={{0,1},{1,2},{2,3},{3,4},{4,5},{5,6},{6,7},{7,0},{8,9},{9,10},{10,1... | collective-permute-start | bytes 393224 | tf_op jit(solution)/shard_map/ppermute | solution.py:79
  22.7 5.1 %collective-permute-start.5 = (f32[4,16,512]{2,1,0:T(8,128)S(1)}, f32[4,16,512]{2,1,0:T(8,128)S(1)}, u32[]{:S(2)}, u32[]{:S(2)}) collective-permute-start(f32[4,16,512]{2,1,0:T(8,128)S(1)} %get-tuple-element.49), channel_id=1, source_target_pairs={{0,7},{1,0},{2,1},{3,2},{4,3},{5,4},{6,5},{7,6},{8,15},{9,8},{10,9... | collective-permute-start | bytes 393224 | tf_op jit(solution)/shard_map/ppermute | solution.py:79
  28.8 5.3 %collective-permute-start.6 = (f32[4,7,512]{2,1,0:T(8,128)S(1)}, f32[4,7,512]{2,1,0:T(8,128)S(1)}, u32[]{:S(2)}, u32[]{:S(2)}) collective-permute-start(f32[4,7,512]{2,1,0:T(8,128)S(1)} %get-tuple-element.51), channel_id=1, source_target_pairs={{0,8},{8,16},{16,24},{24,32},{32,40},{40,48},{48,56},{56,64},{64,7... | collective-permute-start | bytes 172040 | tf_op jit(solution)/shard_map/ppermute | solution.py:79
  32.7 3.7 %collective-permute-start.7 = (f32[4,7,512]{2,1,0:T(8,128)S(1)}, f32[4,7,512]{2,1,0:T(8,128)S(1)}, u32[]{:S(2)}, u32[]{:S(2)}) collective-permute-start(f32[4,7,512]{2,1,0:T(8,128)S(1)} %get-tuple-element.52), channel_id=1, source_target_pairs={{0,248},{8,0},{16,8},{24,16},{32,24},{40,32},{48,40},{56,48},{64,5... | collective-permute-start | bytes 172040 | tf_op jit(solution)/shard_map/ppermute | solution.py:79
  37.2 5.4 %collective-permute-start.8 = (f32[3,24,512]{2,1,0:T(8,128)S(1)}, f32[3,24,512]{2,1,0:T(8,128)S(1)}, u32[]{:S(2)}, u32[]{:S(2)}) collective-permute-start(f32[3,24,512]{2,1,0:T(8,128)S(1)} %get-tuple-element.97), channel_id=1, source_target_pairs={{0,1},{1,2},{2,3},{3,4},{4,5},{5,6},{6,7},{7,0},{8,9},{9,10},{10,1... | collective-permute-start | bytes 442376 | tf_op jit(solution)/shard_map/ppermute | solution.py:79
  39.7 4.0 %collective-permute-start.9 = (f32[3,24,512]{2,1,0:T(8,128)S(1)}, f32[3,24,512]{2,1,0:T(8,128)S(1)}, u32[]{:S(2)}, u32[]{:S(2)}) collective-permute-start(f32[3,24,512]{2,1,0:T(8,128)S(1)} %get-tuple-element.96), channel_id=1, source_target_pairs={{0,7},{1,0},{2,1},{3,2},{4,3},{5,4},{6,5},{7,6},{8,15},{9,8},{10,9... | collective-permute-start | bytes 442376 | tf_op jit(solution)/shard_map/ppermute | solution.py:79
  45.0 5.8 %collective-permute-start.10 = (f32[4,24,512]{2,1,0:T(8,128)S(1)}, f32[4,24,512]{2,1,0:T(8,128)S(1)}, u32[]{:S(2)}, u32[]{:S(2)}) collective-permute-start(f32[4,24,512]{2,1,0:T(8,128)S(1)} %shard_map.308.image_ref), channel_id=1, source_target_pairs={{0,1},{1,2},{2,3},{3,4},{4,5},{5,6},{6,7},{7,0},{8,9},{9,10},{10,1... | collective-permute-start | bytes 589832 | tf_op jit(solution)/shard_map/ppermute | solution.py:79
  46.6 4.5 %collective-permute-start.11 = (f32[4,24,512]{2,1,0:T(8,128)S(1)}, f32[4,24,512]{2,1,0:T(8,128)S(1)}, u32[]{:S(2)}, u32[]{:S(2)}) collective-permute-start(f32[4,24,512]{2,1,0:T(8,128)S(1)} %shard_map.308.image_ref), channel_id=1, source_target_pairs={{0,7},{1,0},{2,1},{3,2},{4,3},{5,4},{6,5},{7,6},{8,15},{9,8},{10,9... | collective-permute-start | bytes 589832 | tf_op jit(solution)/shard_map/ppermute | solution.py:79
  53.9 15.8 %collective-permute-start.12 = (f32[3,2,8,256]{3,2,1,0:T(8,128)S(1)}, f32[3,2,8,256]{3,2,1,0:T(8,128)S(1)}, u32[]{:S(2)}, u32[]{:S(2)}) collective-permute-start(f32[3,2,8,256]{3,2,1,0:T(8,128)S(1)} %get-tuple-element.65.own_ref), channel_id=1, source_target_pairs={{0,8},{8,16},{16,24},{24,32},{32,40},{40,48},{48,56},{56,64},{64,7... | collective-permute-start | bytes 147464 | tf_op jit(solution)/shard_map/ppermute | solution.py:79
  59.0 10.7 %collective-permute-start.13 = (f32[3,2,8,256]{3,2,1,0:T(8,128)S(1)}, f32[3,2,8,256]{3,2,1,0:T(8,128)S(1)}, u32[]{:S(2)}, u32[]{:S(2)}) collective-permute-start(f32[3,2,8,256]{3,2,1,0:T(8,128)S(1)} %get-tuple-element.65.own_ref), channel_id=1, source_target_pairs={{0,248},{8,0},{16,8},{24,16},{32,24},{40,32},{48,40},{56,48},{64,5... | collective-permute-start | bytes 147464 | tf_op jit(solution)/shard_map/ppermute | solution.py:79
  60.7 31.6 %all-to-all-start = ((f32[32,96,128]{2,1,0:T(8,128)}), f32[32,96,128]{2,1,0:T(8,128)S(1)}, u32[]{:S(2)}, u32[]{:S(2)}) async-start(f32[32,96,128]{2,1,0:T(8,128)} %get-tuple-element.69), calls=%async_computation | async-start | bytes 3145728 | tf_op jit(solution)/shard_map/all_to_all | solution.py:525
  69.5 12.5 %copy-start.15 = (f32[16,512]{1,0:T(8,128)S(1)}, f32[16,512]{1,0:T(8,128)}, u32[]{:S(2)}) copy-start(f32[16,512]{1,0:T(8,128)} %constant.67.clone) | copy-start | bytes 98308
  69.5 12.5 %copy-start.16 = (f32[16,512]{1,0:T(8,128)S(1)}, f32[16,512]{1,0:T(8,128)}, u32[]{:S(2)}) copy-start(f32[16,512]{1,0:T(8,128)} %constant.68.clone) | copy-start | bytes 98308
  69.5 12.5 %copy-start.17 = (f32[16,512]{1,0:T(8,128)S(1)}, f32[16,512]{1,0:T(8,128)}, u32[]{:S(2)}) copy-start(f32[16,512]{1,0:T(8,128)} %constant.69.clone) | copy-start | bytes 98308
  70.1 12.6 %copy-start.1 = (f32[512,512]{1,0:T(8,128)S(1)}, f32[512,512]{1,0:T(8,128)}, u32[]{:S(2)}) copy-start(f32[512,512]{1,0:T(8,128)} %constant.65.clone.refs_0_) | copy-start | bytes 3145732
  70.4 6.7 %collective-permute-start.15 = (f32[3,4,8,256]{3,2,1,0:T(8,128)S(1)}, f32[3,4,8,256]{3,2,1,0:T(8,128)S(1)}, u32[]{:S(2)}, u32[]{:S(2)}) collective-permute-start(f32[3,4,8,256]{3,2,1,0:T(8,128)S(1)} %get-tuple-element.75), channel_id=1, source_target_pairs={{0,2},{1,3},{2,4},{3,5},{4,6},{5,7},{6,0},{7,1},{8,10},{9,11},{10,... | collective-permute-start | bytes 294920 | tf_op jit(solution)/shard_map/ppermute | solution.py:79
  72.2 7.5 %collective-permute-start.16 = (f32[3,4,8,256]{3,2,1,0:T(8,128)S(1)}, f32[3,4,8,256]{3,2,1,0:T(8,128)S(1)}, u32[]{:S(2)}, u32[]{:S(2)}) collective-permute-start(f32[3,4,8,256]{3,2,1,0:T(8,128)S(1)} %get-tuple-element.76), channel_id=1, source_target_pairs={{0,6},{1,7},{2,0},{3,1},{4,2},{5,3},{6,4},{7,5},{8,14},{9,15},{10,... | collective-permute-start | bytes 294920 | tf_op jit(solution)/shard_map/ppermute | solution.py:79
  74.0 8.7 %collective-permute-start.14 = (f32[3,2,8,256]{3,2,1,0:T(8,128)S(1)}, f32[3,2,8,256]{3,2,1,0:T(8,128)S(1)}, u32[]{:S(2)}, u32[]{:S(2)}) collective-permute-start(f32[3,2,8,256]{3,2,1,0:T(8,128)S(1)} %get-tuple-element.74), channel_id=1, source_target_pairs={{0,4},{1,5},{2,6},{3,7},{4,0},{5,1},{6,2},{7,3},{8,12},{9,13},{10,... | collective-permute-start | bytes 147464 | tf_op jit(solution)/shard_map/ppermute | solution.py:79
  77.1 5.7 %collective-permute-start.17 = (f32[3,2,8,256]{3,2,1,0:T(8,128)S(1)}, f32[3,2,8,256]{3,2,1,0:T(8,128)S(1)}, u32[]{:S(2)}, u32[]{:S(2)}) collective-permute-start(f32[3,2,8,256]{3,2,1,0:T(8,128)S(1)} %slice_add_fusion.1), channel_id=1, source_target_pairs={{0,1},{1,2},{2,3},{3,4},{4,5},{5,6},{6,7},{7,0},{8,9},{9,10},{10,1... | collective-permute-start | bytes 147464 | tf_op jit(solution)/shard_map/ppermute | solution.py:79
  79.7 3.5 %collective-permute-start.18 = (f32[3,2,8,256]{3,2,1,0:T(8,128)S(1)}, f32[3,2,8,256]{3,2,1,0:T(8,128)S(1)}, u32[]{:S(2)}, u32[]{:S(2)}) collective-permute-start(f32[3,2,8,256]{3,2,1,0:T(8,128)S(1)} %slice_add_fusion), channel_id=1, source_target_pairs={{0,7},{1,0},{2,1},{3,2},{4,3},{5,4},{6,5},{7,6},{8,15},{9,8},{10,9... | collective-permute-start | bytes 147464 | tf_op jit(solution)/shard_map/ppermute | solution.py:79
  (27 other events, 276.8 us)

commit v3 on v2

--- a/solution.py
+++ b/solution.py
@@ -301,8 +301,7 @@
 
 def force_kernel(below_ref, image_ref, above_ref, before_ref, after_ref, shifts_ref, fractions_ref,
                  first_ref, last_ref, target_ref, table_high_ref, table_low_ref, pairs_ref, ends_ref,
-                 out_ref, spectrum_ref, coarse_ref, parcels_ref, filtered_ref, wide_ref, frame_ref, force_ref,
-                 tails_ref):
+                 out_ref, spectrum_ref, coarse_ref, tails_ref, filtered_ref, wide_ref, frame_ref, force_ref):
     refs = (before_ref, after_ref, shifts_ref)
     depth = image_ref.shape[0]
     z_filter(layers_of(below_ref, image_ref, above_ref, 4), filtered_ref, weights_at(fractions_ref, 3, 2))
@@ -343,8 +342,6 @@
             place = (side * 3 * depth + line) * across
             for lane in range(across):
                 tails_ref[place + lane, :] = row[0, lane * 128 : (lane + 1) * 128]
-    for peer in range(parcels_ref.shape[0]):
-        parcels_ref[peer] = tails_ref[...]
 
 
 def load_kernel(*refs):
@@ -353,18 +350,38 @@
         refs[count + i][...] = refs[i][...]
 
 
-def carry_kernel(place_ref, carried_ref, tables_ref, out_ref, sums_ref):
-    peers = carried_ref.shape[0]
+def chip_kernel(place_ref, own_ref, other_ref, tables_ref, out_ref):
+    rows = out_ref.shape[1]
+    core = lax.rem(place_ref[0], 2)
+    for side in range(2):
+
+        @pl.when(core == side)
+        def _():
+            part = slice(side * rows, (side + 1) * rows)
+            value = tables_ref[0] * own_ref[part, :] + other_ref[part, :]
+            for peer in range(out_ref.shape[0]):
+                out_ref[peer] = value
+
+
+def carry_kernel(place_ref, carried_ref, other_ref, tables_ref, out_ref, sums_ref):
+    chips = carried_ref.shape[0] // 2
     across = NX // 128
     lines = out_ref.shape[1]
     rows = lines * across
-    place = place_ref[0]
+    chip = place_ref[0] // 2
+    core = lax.rem(place_ref[0], 2)
+    ratio = tables_ref[0]
     for side, sign in ((0, -1), (1, 1)):
         total = jnp.zeros((rows, 128), jnp.float32)
-        for away in range(peers, 0, -1):
-            peer = lax.rem(place + sign * away + peers, peers)
-            total = total * tables_ref[0] + carried_ref[peer, side * rows : (side + 1) * rows, :]
+        for away in range(chips, 0, -1):
+            peer = 2 * lax.rem(chip + sign * away + chips, chips) + side
+            total = total * (ratio * ratio) + carried_ref[peer]
         sums_ref[side] = total * tables_ref[1]
+
+        @pl.when(core != side)
+        def _():
+            sums_ref[side] = other_ref[side * rows : (side + 1) * rows, :] + ratio * sums_ref[side]
+
         for line in range(lines):
             for lane in range(across):
                 out_ref[side, line, lane * 128 : (lane + 1) * 128] = sums_ref[side, line * across + lane, :]
@@ -512,16 +529,21 @@
 
     lines = 3 * depth
     coarse_shape = (3, depth // 2, height // 2, half)
-    image, spectrum, coarse, parcels = call(
+    image, spectrum, coarse, tails = call(
         force_kernel,
-        [full, (lines * height, NX), coarse_shape, (peers_y, 2 * lines * across, lanes)],
+        [full, (lines * height, NX), coarse_shape, (2 * lines * across, lanes)],
         [
             (3 * depth - 3, rows, NX), (depth, ACROSS, rows, LANES), (depth + 2, ACROSS, rows, LANES), (lines * height, NX),
-            (2 * lines * across, lanes),
         ],
         below, image, above, *halos, outer_low, outer_high, *tables, smem=(6,),
     )
 
+    place = lax.axis_index("gy").reshape(1).astype(jnp.int32)
+    weights = f32(np.tile(np.stack([ratio, wrap]).reshape(2, across, lanes), (1, lines, 1)))
+    other = lax.ppermute(tails, "gy", [(i, i ^ 1) for i in range(peers_y)])
+    (parcels,) = call(
+        chip_kernel, [(peers_y, lines * across, lanes)], [], place, tails, other, weights, smem=(0,)
+    )
     carried = lax.all_to_all(parcels, "gy", 0, 0, tiled=True)
     beside = shift_to(coarse, "gy", 1), shift_to(coarse, "gy", -1)
     double = (3, depth, height // 2, half)
@@ -540,9 +562,8 @@
 
     (back_x,) = call(load_kernel, [jax.ShapeDtypeStruct((NX, NX), jnp.float32)], [], back_x)
     carried, back_x = lax.optimization_barrier((carried, back_x))
-    weights = f32(np.tile(np.stack([ratio, wrap]).reshape(2, across, lanes), (1, lines, 1)))
     (carries,) = call(
-        carry_kernel, [(2, lines, NX)], [(2, lines * across, lanes)], place, carried, weights, smem=(0,)
+        carry_kernel, [(2, lines, NX)], [(2, lines * across, lanes)], place, carried, other, weights, smem=(0,)
     )
 
     spectrum = spectrum.reshape(lines, height, NX)

time: 94.2 us -> 92.1 us (0.978)
  waiting for transfers between devices: 28.8 us -> 23.2 us
  starting transfers between devices: 48.1 us -> 50.8 us
    all_to_all x1, waiting for transfers between devices: 7.89 us -> 0.18 us  [on_device(): carried = lax.all_to_all(parcels, 'gy', 0, 0, tiled=True)]
    ppermute x0 -> x1, starting transfers between devices: none -> 5.06 us  [on_device(): other = lax.ppermute(tails, 'gy', [(i, i ^ 1) for i in range(peers_y)])]
    ppermute x19, waiting for transfers between devices: 20.9 us -> 22.8 us  [shift_to(): return lax.ppermute(x, axis, ring(axis, offset))]
    ppermute x19, starting transfers between devices: 39.3 us -> 37.6 us  [shift_to(): return lax.ppermute(x, axis, ring(axis, offset))]
    pallas_call x12 -> x13, Pallas kernels: 11.3 us -> 11.6 us  [call(): pl.pallas_call(kernel, out_shape=tuple((shape(dims) if isinstance(dims, t...]
  transfers between devices with their start and end apart: 20 -> 21, of which waited for: 13 -> 14; matrix products, arithmetic and copies ran while one was open for 2% -> 2% of each run, Pallas kernels for 1% -> 1%
where the time goes in v3:
time: 92.1 us; the launch traced here: 91.2 us
  starting transfers between devices  50.8 us (55%)
  waiting for transfers between devices  23.2 us (25%)
  Pallas kernels  11.6 us (13%)
  matrix products  2.04 us (2%)
  local copies, waits for them, and re-layouts  1.68 us (2%)
  between operations  1.2 us (1%)
    ppermute x19, starting transfers between devices, shift_to(): return lax.ppermute(x, axis, ring(axis, offset))  37.6 us
    ppermute x19, waiting for transfers between devices, shift_to(): return lax.ppermute(x, axis, ring(axis, offset))  22.8 us
    pallas_call x13, Pallas kernels, call(): pl.pallas_call(kernel, out_shape=tuple((shape(dims) if isinstance(dims, t...  11.6 us
    all_to_all x1, starting transfers between devices, on_device(): carried = lax.all_to_all(parcels, 'gy', 0, 0, tiled=True)  8.21 us
    ppermute x1, starting transfers between devices, on_device(): other = lax.ppermute(tails, 'gy', [(i, i ^ 1) for i in range(peers_y)])  5.06 us
    dot_general x3, matrix products, dot(): return jnp.dot(a, b, precision=HIGH, preferred_element_type=jnp.float32)  2.04 us
  transfers between devices with their start and end apart: 21, of which 14 were waited for; matrix products, arithmetic and copies ran while one was open for 2% of the time, Pallas kernels for 1%

profile of v3, /device:TPU:1, one launch (start us, length us, event | category | flops | bytes accessed | tf_op | source)
XLA Modules:
  0.0 91.2 jit_solution(2947177481345064565)
XLA Ops:
  0.6 2.6 %shard_map.302 = (f32[4,16,512]{2,1,0:T(8,128)}, f32[4,29,512]{2,1,0:T(8,128)}, f32[4,29,512]{2,1,0:T(8,128)}) custom-call(f32[4,16,512]{2,1,0:T(8,128)} %image_hbm.1, s32[4,3,4,16,512]{4,3,2,1,0:T(8,128)} %shifts_ref.11, f32[4,3]{1,0:T(4,128)} %fractions_ref.11), custom_call_target="tpu_custom_call" | custom-call | tf_op jit(solution)/shard_map/pallas_call | solution.py:432
  3.2 2.8 %collective-permute-start = (f32[4,29,512]{2,1,0:T(8,128)}, f32[4,29,512]{2,1,0:T(8,128)S(1)}, u32[]{:S(2)}, u32[]{:S(2)}) collective-permute-start(f32[4,29,512]{2,1,0:T(8,128)} %get-tuple-element.41), channel_id=1, source_target_pairs={{0,8},{8,16},{16,24},{24,32},{32,40},{40,48},{48,56},{56,64},{64,7... | collective-permute-start | bytes 712712 | tf_op jit(solution)/shard_map/ppermute | solution.py:79
  7.5 2.1 %collective-permute-done.low_ref.before_ref = f32[4,29,512]{2,1,0:T(8,128)S(1)} collective-permute-done((f32[4,29,512]{2,1,0:T(8,128)}, f32[4,29,512]{2,1,0:T(8,128)S(1)}, u32[]{:S(2)}, u32[]{:S(2)}) %collective-permute-start) | collective-permute-done | bytes 237600 | tf_op jit(solution)/shard_map/ppermute | solution.py:79
  9.6 2.4 %collective-permute-done.1.high_ref.after_ref = f32[4,29,512]{2,1,0:T(8,128)S(1)} collective-permute-done((f32[4,29,512]{2,1,0:T(8,128)}, f32[4,29,512]{2,1,0:T(8,128)S(1)}, u32[]{:S(2)}, u32[]{:S(2)}) %collective-permute-start.1) | collective-permute-done | bytes 237600 | tf_op jit(solution)/shard_map/ppermute | solution.py:79
  12.8 2.0 %collective-permute-start.2 = (f32[3,24,512]{2,1,0:T(8,128)S(1)}, f32[3,24,512]{2,1,0:T(8,128)S(1)}, u32[]{:S(2)}, u32[]{:S(2)}) collective-permute-start(f32[3,24,512]{2,1,0:T(8,128)S(1)} %get-tuple-element.99), channel_id=1, source_target_pairs={{0,1},{1,2},{2,3},{3,4},{4,5},{5,6},{6,7},{7,0},{8,9},{9,10},{10,1... | collective-permute-start | bytes 442376 | tf_op jit(solution)/shard_map/ppermute | solution.py:79
  14.8 4.0 %collective-permute-start.3 = (f32[3,24,512]{2,1,0:T(8,128)S(1)}, f32[3,24,512]{2,1,0:T(8,128)S(1)}, u32[]{:S(2)}, u32[]{:S(2)}) collective-permute-start(f32[3,24,512]{2,1,0:T(8,128)S(1)} %get-tuple-element.98), channel_id=1, source_target_pairs={{0,7},{1,0},{2,1},{3,2},{4,3},{5,4},{6,5},{7,6},{8,15},{9,8},{10,9... | collective-permute-start | bytes 442376 | tf_op jit(solution)/shard_map/ppermute | solution.py:79
  18.8 2.4 %collective-permute-done.2.below_ref = f32[3,24,512]{2,1,0:T(8,128)S(1)} collective-permute-done((f32[3,24,512]{2,1,0:T(8,128)S(1)}, f32[3,24,512]{2,1,0:T(8,128)S(1)}, u32[]{:S(2)}, u32[]{:S(2)}) %collective-permute-start.2) | collective-permute-done | bytes 147488 | tf_op jit(solution)/shard_map/ppermute | solution.py:79
  22.7 2.8 %collective-permute-start.5 = (f32[4,16,512]{2,1,0:T(8,128)S(1)}, f32[4,16,512]{2,1,0:T(8,128)S(1)}, u32[]{:S(2)}, u32[]{:S(2)}) collective-permute-start(f32[4,16,512]{2,1,0:T(8,128)S(1)} %get-tuple-element.49), channel_id=1, source_target_pairs={{0,7},{1,0},{2,1},{3,2},{4,3},{5,4},{6,5},{7,6},{8,15},{9,8},{10,9... | collective-permute-start | bytes 393224 | tf_op jit(solution)/shard_map/ppermute | solution.py:79
  25.5 2.3 %collective-permute-done.4.below_ref.first_ref = f32[4,16,512]{2,1,0:T(8,128)S(1)} collective-permute-done((f32[4,16,512]{2,1,0:T(8,128)S(1)}, f32[4,16,512]{2,1,0:T(8,128)S(1)}, u32[]{:S(2)}, u32[]{:S(2)}) %collective-permute-start.4) | collective-permute-done | bytes 131104 | tf_op jit(solution)/shard_map/ppermute | solution.py:79
  28.8 3.9 %collective-permute-start.6 = (f32[4,7,512]{2,1,0:T(8,128)S(1)}, f32[4,7,512]{2,1,0:T(8,128)S(1)}, u32[]{:S(2)}, u32[]{:S(2)}) collective-permute-start(f32[4,7,512]{2,1,0:T(8,128)S(1)} %get-tuple-element.51), channel_id=1, source_target_pairs={{0,8},{8,16},{16,24},{24,32},{32,40},{40,48},{48,56},{56,64},{64,7... | collective-permute-start | bytes 172040 | tf_op jit(solution)/shard_map/ppermute | solution.py:79
  34.0 2.4 %collective-permute-done.7.high_ref = f32[4,7,512]{2,1,0:T(8,128)S(1)} collective-permute-done((f32[4,7,512]{2,1,0:T(8,128)S(1)}, f32[4,7,512]{2,1,0:T(8,128)S(1)}, u32[]{:S(2)}, u32[]{:S(2)}) %collective-permute-start.7) | collective-permute-done | bytes 57376 | tf_op jit(solution)/shard_map/ppermute | solution.py:79
  37.2 2.4 %collective-permute-start.8 = (f32[3,24,512]{2,1,0:T(8,128)S(1)}, f32[3,24,512]{2,1,0:T(8,128)S(1)}, u32[]{:S(2)}, u32[]{:S(2)}) collective-permute-start(f32[3,24,512]{2,1,0:T(8,128)S(1)} %get-tuple-element.97), channel_id=1, source_target_pairs={{0,1},{1,2},{2,3},{3,4},{4,5},{5,6},{6,7},{7,0},{8,9},{9,10},{10,1... | collective-permute-start | bytes 442376 | tf_op jit(solution)/shard_map/ppermute | solution.py:79
  40.2 2.4 %collective-permute-done.8.below_ref = f32[3,24,512]{2,1,0:T(8,128)S(1)} collective-permute-done((f32[3,24,512]{2,1,0:T(8,128)S(1)}, f32[3,24,512]{2,1,0:T(8,128)S(1)}, u32[]{:S(2)}, u32[]{:S(2)}) %collective-permute-start.8) | collective-permute-done | bytes 147488 | tf_op jit(solution)/shard_map/ppermute | solution.py:79
  47.9 2.9 %collective-permute-done.10.below_ref = f32[4,24,512]{2,1,0:T(8,128)S(1)} collective-permute-done((f32[4,24,512]{2,1,0:T(8,128)S(1)}, f32[4,24,512]{2,1,0:T(8,128)S(1)}, u32[]{:S(2)}, u32[]{:S(2)}) %collective-permute-start.10) | collective-permute-done | bytes 196640 | tf_op jit(solution)/shard_map/ppermute | solution.py:79
  51.1 2.2 %shard_map.310 = (f32[4,16,512]{2,1,0:T(8,128)}, f32[192,512]{1,0:T(8,128)S(1)}, f32[3,2,8,256]{3,2,1,0:T(8,128)S(1)}, f32[96,128]{1,0:T(8,128)S(1)}) custom-call(f32[4,24,512]{2,1,0:T(8,128)S(1)} %collective-permute-done.10.below_ref, f32[4,24,512]{2,1,0:T(8,128)S(1)} %shard_map.308.image_ref, f32[4,24,512]{2,1,0:T(8,128)S(1)} %collective-permute-done.11.above_ref, ...), custom_call_target="tpu_custom_call" | custom-call | tf_op jit(solution)/shard_map/pallas_call | solution.py:432
  53.3 5.1 %collective-permute-start.12 = (f32[3,2,8,256]{3,2,1,0:T(8,128)S(1)}, f32[3,2,8,256]{3,2,1,0:T(8,128)S(1)}, u32[]{:S(2)}, u32[]{:S(2)}) collective-permute-start(f32[3,2,8,256]{3,2,1,0:T(8,128)S(1)} %get-tuple-element.65.own_ref), channel_id=1, source_target_pairs={{0,8},{8,16},{16,24},{24,32},{32,40},{40,48},{48,56},{56,64},{64,7... | collective-permute-start | bytes 147464 | tf_op jit(solution)/shard_map/ppermute | solution.py:79
  58.4 1.6 %collective-permute-start.13 = (f32[3,2,8,256]{3,2,1,0:T(8,128)S(1)}, f32[3,2,8,256]{3,2,1,0:T(8,128)S(1)}, u32[]{:S(2)}, u32[]{:S(2)}) collective-permute-start(f32[3,2,8,256]{3,2,1,0:T(8,128)S(1)} %get-tuple-element.65.own_ref), channel_id=1, source_target_pairs={{0,248},{8,0},{16,8},{24,16},{32,24},{40,32},{48,40},{56,48},{64,5... | collective-permute-start | bytes 147464 | tf_op jit(solution)/shard_map/ppermute | solution.py:79
  60.0 5.1 %collective-permute-start.14 = (f32[96,128]{1,0:T(8,128)S(1)}, f32[96,128]{1,0:T(8,128)S(1)}, u32[]{:S(2)}, u32[]{:S(2)}) collective-permute-start(f32[96,128]{1,0:T(8,128)S(1)} %get-tuple-element.69.own_ref), channel_id=1, source_target_pairs={{0,8},{8,0},{16,24},{24,16},{32,40},{40,32},{48,56},{56,48},{64,72... | collective-permute-start | bytes 147464 | tf_op jit(solution)/shard_map/ppermute | solution.py:543
  67.1 8.2 %all-to-all-start = ((f32[32,48,128]{2,1,0:T(8,128)}), f32[32,48,128]{2,1,0:T(8,128)S(1)}, u32[]{:S(2)}, u32[]{:S(2)}) async-start(f32[32,48,128]{2,1,0:T(8,128)} %shard_map.312), calls=%async_computation | async-start | bytes 1572864 | tf_op jit(solution)/shard_map/all_to_all | solution.py:547
  75.4 1.8 %collective-permute-start.16 = (f32[3,4,8,256]{3,2,1,0:T(8,128)S(1)}, f32[3,4,8,256]{3,2,1,0:T(8,128)S(1)}, u32[]{:S(2)}, u32[]{:S(2)}) collective-permute-start(f32[3,4,8,256]{3,2,1,0:T(8,128)S(1)} %get-tuple-element.75), channel_id=1, source_target_pairs={{0,2},{1,3},{2,4},{3,5},{4,6},{5,7},{6,0},{7,1},{8,10},{9,11},{10,... | collective-permute-start | bytes 294920 | tf_op jit(solution)/shard_map/ppermute | solution.py:79
  77.2 1.8 %collective-permute-start.17 = (f32[3,4,8,256]{3,2,1,0:T(8,128)S(1)}, f32[3,4,8,256]{3,2,1,0:T(8,128)S(1)}, u32[]{:S(2)}, u32[]{:S(2)}) collective-permute-start(f32[3,4,8,256]{3,2,1,0:T(8,128)S(1)} %get-tuple-element.76), channel_id=1, source_target_pairs={{0,6},{1,7},{2,0},{3,1},{4,2},{5,3},{6,4},{7,5},{8,14},{9,15},{10,... | collective-permute-start | bytes 294920 | tf_op jit(solution)/shard_map/ppermute | solution.py:79
  79.0 1.9 %collective-permute-start.15 = (f32[3,2,8,256]{3,2,1,0:T(8,128)S(1)}, f32[3,2,8,256]{3,2,1,0:T(8,128)S(1)}, u32[]{:S(2)}, u32[]{:S(2)}) collective-permute-start(f32[3,2,8,256]{3,2,1,0:T(8,128)S(1)} %get-tuple-element.74), channel_id=1, source_target_pairs={{0,4},{1,5},{2,6},{3,7},{4,0},{5,1},{6,2},{7,3},{8,12},{9,13},{10,... | collective-permute-start | bytes 147464 | tf_op jit(solution)/shard_map/ppermute | solution.py:79
  81.0 2.9 %collective-permute-done.16 = f32[3,4,8,256]{3,2,1,0:T(8,128)S(1)} collective-permute-done((f32[3,4,8,256]{3,2,1,0:T(8,128)S(1)}, f32[3,4,8,256]{3,2,1,0:T(8,128)S(1)}, u32[]{:S(2)}, u32[]{:S(2)}) %collective-permute-start.16) | collective-permute-done | bytes 98336 | tf_op jit(solution)/shard_map/ppermute | solution.py:79
  84.7 2.4 %collective-permute-start.19 = (f32[3,2,8,256]{3,2,1,0:T(8,128)S(1)}, f32[3,2,8,256]{3,2,1,0:T(8,128)S(1)}, u32[]{:S(2)}, u32[]{:S(2)}) collective-permute-start(f32[3,2,8,256]{3,2,1,0:T(8,128)S(1)} %slice_add_fusion), channel_id=1, source_target_pairs={{0,7},{1,0},{2,1},{3,2},{4,3},{5,4},{6,5},{7,6},{8,15},{9,8},{10,9... | collective-permute-start | bytes 147464 | tf_op jit(solution)/shard_map/ppermute | solution.py:79
  (114 shorter events, 19.6 us)
Async XLA Ops:
  3.2 6.4 %collective-permute-start = (f32[4,29,512]{2,1,0:T(8,128)}, f32[4,29,512]{2,1,0:T(8,128)S(1)}, u32[]{:S(2)}, u32[]{:S(2)}) collective-permute-start(f32[4,29,512]{2,1,0:T(8,128)} %get-tuple-element.41), channel_id=1, source_target_pairs={{0,8},{8,16},{16,24},{24,32},{32,40},{40,48},{48,56},{56,64},{64,7... | collective-permute-start | bytes 712712 | tf_op jit(solution)/shard_map/ppermute | solution.py:79
  6.0 6.0 %collective-permute-start.1 = (f32[4,29,512]{2,1,0:T(8,128)}, f32[4,29,512]{2,1,0:T(8,128)S(1)}, u32[]{:S(2)}, u32[]{:S(2)}) collective-permute-start(f32[4,29,512]{2,1,0:T(8,128)} %get-tuple-element.42), channel_id=1, source_target_pairs={{0,248},{8,0},{16,8},{24,16},{32,24},{40,32},{48,40},{56,48},{64,5... | collective-permute-start | bytes 712712 | tf_op jit(solution)/shard_map/ppermute | solution.py:79
  12.8 8.5 %collective-permute-start.2 = (f32[3,24,512]{2,1,0:T(8,128)S(1)}, f32[3,24,512]{2,1,0:T(8,128)S(1)}, u32[]{:S(2)}, u32[]{:S(2)}) collective-permute-start(f32[3,24,512]{2,1,0:T(8,128)S(1)} %get-tuple-element.99), channel_id=1, source_target_pairs={{0,1},{1,2},{2,3},{3,4},{4,5},{5,6},{6,7},{7,0},{8,9},{9,10},{10,1... | collective-permute-start | bytes 442376 | tf_op jit(solution)/shard_map/ppermute | solution.py:79
  14.8 6.5 %collective-permute-start.3 = (f32[3,24,512]{2,1,0:T(8,128)S(1)}, f32[3,24,512]{2,1,0:T(8,128)S(1)}, u32[]{:S(2)}, u32[]{:S(2)}) collective-permute-start(f32[3,24,512]{2,1,0:T(8,128)S(1)} %get-tuple-element.98), channel_id=1, source_target_pairs={{0,7},{1,0},{2,1},{3,2},{4,3},{5,4},{6,5},{7,6},{8,15},{9,8},{10,9... | collective-permute-start | bytes 442376 | tf_op jit(solution)/shard_map/ppermute | solution.py:79
  22.6 5.2 %collective-permute-start.4 = (f32[4,16,512]{2,1,0:T(8,128)S(1)}, f32[4,16,512]{2,1,0:T(8,128)S(1)}, u32[]{:S(2)}, u32[]{:S(2)}) collective-permute-start(f32[4,16,512]{2,1,0:T(8,128)S(1)} %get-tuple-element.47), channel_id=1, source_target_pairs={{0,1},{1,2},{2,3},{3,4},{4,5},{5,6},{6,7},{7,0},{8,9},{9,10},{10,1... | collective-permute-start | bytes 393224 | tf_op jit(solution)/shard_map/ppermute | solution.py:79
  22.7 5.1 %collective-permute-start.5 = (f32[4,16,512]{2,1,0:T(8,128)S(1)}, f32[4,16,512]{2,1,0:T(8,128)S(1)}, u32[]{:S(2)}, u32[]{:S(2)}) collective-permute-start(f32[4,16,512]{2,1,0:T(8,128)S(1)} %get-tuple-element.49), channel_id=1, source_target_pairs={{0,7},{1,0},{2,1},{3,2},{4,3},{5,4},{6,5},{7,6},{8,15},{9,8},{10,9... | collective-permute-start | bytes 393224 | tf_op jit(solution)/shard_map/ppermute | solution.py:79
  28.8 5.3 %collective-permute-start.6 = (f32[4,7,512]{2,1,0:T(8,128)S(1)}, f32[4,7,512]{2,1,0:T(8,128)S(1)}, u32[]{:S(2)}, u32[]{:S(2)}) collective-permute-start(f32[4,7,512]{2,1,0:T(8,128)S(1)} %get-tuple-element.51), channel_id=1, source_target_pairs={{0,8},{8,16},{16,24},{24,32},{32,40},{40,48},{48,56},{56,64},{64,7... | collective-permute-start | bytes 172040 | tf_op jit(solution)/shard_map/ppermute | solution.py:79
  32.7 3.7 %collective-permute-start.7 = (f32[4,7,512]{2,1,0:T(8,128)S(1)}, f32[4,7,512]{2,1,0:T(8,128)S(1)}, u32[]{:S(2)}, u32[]{:S(2)}) collective-permute-start(f32[4,7,512]{2,1,0:T(8,128)S(1)} %get-tuple-element.52), channel_id=1, source_target_pairs={{0,248},{8,0},{16,8},{24,16},{32,24},{40,32},{48,40},{56,48},{64,5... | collective-permute-start | bytes 172040 | tf_op jit(solution)/shard_map/ppermute | solution.py:79
  37.2 5.4 %collective-permute-start.8 = (f32[3,24,512]{2,1,0:T(8,128)S(1)}, f32[3,24,512]{2,1,0:T(8,128)S(1)}, u32[]{:S(2)}, u32[]{:S(2)}) collective-permute-start(f32[3,24,512]{2,1,0:T(8,128)S(1)} %get-tuple-element.97), channel_id=1, source_target_pairs={{0,1},{1,2},{2,3},{3,4},{4,5},{5,6},{6,7},{7,0},{8,9},{9,10},{10,1... | collective-permute-start | bytes 442376 | tf_op jit(solution)/shard_map/ppermute | solution.py:79
  39.7 4.0 %collective-permute-start.9 = (f32[3,24,512]{2,1,0:T(8,128)S(1)}, f32[3,24,512]{2,1,0:T(8,128)S(1)}, u32[]{:S(2)}, u32[]{:S(2)}) collective-permute-start(f32[3,24,512]{2,1,0:T(8,128)S(1)} %get-tuple-element.96), channel_id=1, source_target_pairs={{0,7},{1,0},{2,1},{3,2},{4,3},{5,4},{6,5},{7,6},{8,15},{9,8},{10,9... | collective-permute-start | bytes 442376 | tf_op jit(solution)/shard_map/ppermute | solution.py:79
  45.0 5.8 %collective-permute-start.10 = (f32[4,24,512]{2,1,0:T(8,128)S(1)}, f32[4,24,512]{2,1,0:T(8,128)S(1)}, u32[]{:S(2)}, u32[]{:S(2)}) collective-permute-start(f32[4,24,512]{2,1,0:T(8,128)S(1)} %shard_map.308.image_ref), channel_id=1, source_target_pairs={{0,1},{1,2},{2,3},{3,4},{4,5},{5,6},{6,7},{7,0},{8,9},{9,10},{10,1... | collective-permute-start | bytes 589832 | tf_op jit(solution)/shard_map/ppermute | solution.py:79
  46.5 4.5 %collective-permute-start.11 = (f32[4,24,512]{2,1,0:T(8,128)S(1)}, f32[4,24,512]{2,1,0:T(8,128)S(1)}, u32[]{:S(2)}, u32[]{:S(2)}) collective-permute-start(f32[4,24,512]{2,1,0:T(8,128)S(1)} %shard_map.308.image_ref), channel_id=1, source_target_pairs={{0,7},{1,0},{2,1},{3,2},{4,3},{5,4},{6,5},{7,6},{8,15},{9,8},{10,9... | collective-permute-start | bytes 589832 | tf_op jit(solution)/shard_map/ppermute | solution.py:79
  53.3 11.8 %collective-permute-start.12 = (f32[3,2,8,256]{3,2,1,0:T(8,128)S(1)}, f32[3,2,8,256]{3,2,1,0:T(8,128)S(1)}, u32[]{:S(2)}, u32[]{:S(2)}) collective-permute-start(f32[3,2,8,256]{3,2,1,0:T(8,128)S(1)} %get-tuple-element.65.own_ref), channel_id=1, source_target_pairs={{0,8},{8,16},{16,24},{24,32},{32,40},{40,48},{48,56},{56,64},{64,7... | collective-permute-start | bytes 147464 | tf_op jit(solution)/shard_map/ppermute | solution.py:79
  58.4 6.7 %collective-permute-start.13 = (f32[3,2,8,256]{3,2,1,0:T(8,128)S(1)}, f32[3,2,8,256]{3,2,1,0:T(8,128)S(1)}, u32[]{:S(2)}, u32[]{:S(2)}) collective-permute-start(f32[3,2,8,256]{3,2,1,0:T(8,128)S(1)} %get-tuple-element.65.own_ref), channel_id=1, source_target_pairs={{0,248},{8,0},{16,8},{24,16},{32,24},{40,32},{48,40},{56,48},{64,5... | collective-permute-start | bytes 147464 | tf_op jit(solution)/shard_map/ppermute | solution.py:79
  60.0 5.9 %collective-permute-start.14 = (f32[96,128]{1,0:T(8,128)S(1)}, f32[96,128]{1,0:T(8,128)S(1)}, u32[]{:S(2)}, u32[]{:S(2)}) collective-permute-start(f32[96,128]{1,0:T(8,128)S(1)} %get-tuple-element.69.own_ref), channel_id=1, source_target_pairs={{0,8},{8,0},{16,24},{24,16},{32,40},{40,32},{48,56},{56,48},{64,72... | collective-permute-start | bytes 147464 | tf_op jit(solution)/shard_map/ppermute | solution.py:543
  67.0 20.1 %copy-start.17 = (f32[16,512]{1,0:T(8,128)S(1)}, f32[16,512]{1,0:T(8,128)}, u32[]{:S(2)}) copy-start(f32[16,512]{1,0:T(8,128)} %constant.69.clone) | copy-start | bytes 98308
  67.0 20.1 %copy-start.18 = (f32[16,512]{1,0:T(8,128)S(1)}, f32[16,512]{1,0:T(8,128)}, u32[]{:S(2)}) copy-start(f32[16,512]{1,0:T(8,128)} %constant.70.clone) | copy-start | bytes 98308
  67.0 20.1 %copy-start.19 = (f32[16,512]{1,0:T(8,128)S(1)}, f32[16,512]{1,0:T(8,128)}, u32[]{:S(2)}) copy-start(f32[16,512]{1,0:T(8,128)} %constant.71.clone) | copy-start | bytes 98308
  67.1 22.4 %all-to-all-start = ((f32[32,48,128]{2,1,0:T(8,128)}), f32[32,48,128]{2,1,0:T(8,128)S(1)}, u32[]{:S(2)}, u32[]{:S(2)}) async-start(f32[32,48,128]{2,1,0:T(8,128)} %shard_map.312), calls=%async_computation | async-start | bytes 1572864 | tf_op jit(solution)/shard_map/all_to_all | solution.py:547
  75.4 8.5 %collective-permute-start.16 = (f32[3,4,8,256]{3,2,1,0:T(8,128)S(1)}, f32[3,4,8,256]{3,2,1,0:T(8,128)S(1)}, u32[]{:S(2)}, u32[]{:S(2)}) collective-permute-start(f32[3,4,8,256]{3,2,1,0:T(8,128)S(1)} %get-tuple-element.75), channel_id=1, source_target_pairs={{0,2},{1,3},{2,4},{3,5},{4,6},{5,7},{6,0},{7,1},{8,10},{9,11},{10,... | collective-permute-start | bytes 294920 | tf_op jit(solution)/shard_map/ppermute | solution.py:79
  77.2 7.5 %collective-permute-start.17 = (f32[3,4,8,256]{3,2,1,0:T(8,128)S(1)}, f32[3,4,8,256]{3,2,1,0:T(8,128)S(1)}, u32[]{:S(2)}, u32[]{:S(2)}) collective-permute-start(f32[3,4,8,256]{3,2,1,0:T(8,128)S(1)} %get-tuple-element.76), channel_id=1, source_target_pairs={{0,6},{1,7},{2,0},{3,1},{4,2},{5,3},{6,4},{7,5},{8,14},{9,15},{10,... | collective-permute-start | bytes 294920 | tf_op jit(solution)/shard_map/ppermute | solution.py:79
  79.0 8.8 %collective-permute-start.15 = (f32[3,2,8,256]{3,2,1,0:T(8,128)S(1)}, f32[3,2,8,256]{3,2,1,0:T(8,128)S(1)}, u32[]{:S(2)}, u32[]{:S(2)}) collective-permute-start(f32[3,2,8,256]{3,2,1,0:T(8,128)S(1)} %get-tuple-element.74), channel_id=1, source_target_pairs={{0,4},{1,5},{2,6},{3,7},{4,0},{5,1},{6,2},{7,3},{8,12},{9,13},{10,... | collective-permute-start | bytes 147464 | tf_op jit(solution)/shard_map/ppermute | solution.py:79
  83.8 4.5 %collective-permute-start.18 = (f32[3,2,8,256]{3,2,1,0:T(8,128)S(1)}, f32[3,2,8,256]{3,2,1,0:T(8,128)S(1)}, u32[]{:S(2)}, u32[]{:S(2)}) collective-permute-start(f32[3,2,8,256]{3,2,1,0:T(8,128)S(1)} %slice_add_fusion.1), channel_id=1, source_target_pairs={{0,1},{1,2},{2,3},{3,4},{4,5},{5,6},{6,7},{7,0},{8,9},{9,10},{10,1... | collective-permute-start | bytes 147464 | tf_op jit(solution)/shard_map/ppermute | solution.py:79
  84.7 3.7 %collective-permute-start.19 = (f32[3,2,8,256]{3,2,1,0:T(8,128)S(1)}, f32[3,2,8,256]{3,2,1,0:T(8,128)S(1)}, u32[]{:S(2)}, u32[]{:S(2)}) collective-permute-start(f32[3,2,8,256]{3,2,1,0:T(8,128)S(1)} %slice_add_fusion), channel_id=1, source_target_pairs={{0,7},{1,0},{2,1},{3,2},{4,3},{5,4},{6,5},{7,6},{8,15},{9,8},{10,9... | collective-permute-start | bytes 147464 | tf_op jit(solution)/shard_map/ppermute | solution.py:79
  (28 other events, 385.1 us)

commit v4 on v3

--- a/solution.py
+++ b/solution.py
@@ -363,10 +363,11 @@
                 out_ref[peer] = value
 
 
-def carry_kernel(place_ref, carried_ref, other_ref, tables_ref, out_ref, sums_ref):
+def final_kernel(place_ref, carried_ref, other_ref, tables_ref, smooth_ref, solved_ref, spread_ref, pairs_ref,
+                 table_high_ref, table_low_ref, out_ref, sums_ref, carries_ref, joined_ref):
     chips = carried_ref.shape[0] // 2
     across = NX // 128
-    lines = out_ref.shape[1]
+    lines = carries_ref.shape[1]
     rows = lines * across
     chip = place_ref[0] // 2
     core = lax.rem(place_ref[0], 2)
@@ -384,7 +385,17 @@
 
         for line in range(lines):
             for lane in range(across):
-                out_ref[side, line, lane * 128 : (lane + 1) * 128] = sums_ref[side, line * across + lane, :]
+                carries_ref[side, line, lane * 128 : (lane + 1) * 128] = sums_ref[side, line * across + lane, :]
+    for line in range(lines):
+        part = slice(line * HEIGHT, (line + 1) * HEIGHT)
+        value = smooth_ref[part, :] + spread_ref[0] * carries_ref[0, line : line + 1, :]
+        joined_ref[part, 0:NX] = value + spread_ref[1] * carries_ref[1, line : line + 1, :]
+    high, low = split(solved_ref[...])
+    joined_ref[:, NX:] = product(pairs_ref[...], high) + product(pairs_ref[...], low)
+    high, low = split(joined_ref[...])
+    result = product(high, table_high_ref[...])
+    result = result + product(high, table_low_ref[...])
+    out_ref[...] = result + product(low, table_high_ref[...])
 
 
 def stencil_kernel(before_ref, own_ref, after_ref, stencil_ref, own_out, up_out, down_out, far_out,
@@ -544,7 +555,6 @@
     (parcels,) = call(
         chip_kernel, [(peers_y, lines * across, lanes)], [], place, tails, other, weights, smem=(0,)
     )
-    carried = lax.all_to_all(parcels, "gy", 0, 0, tiled=True)
     beside = shift_to(coarse, "gy", 1), shift_to(coarse, "gy", -1)
     double = (3, depth, height // 2, half)
     own, up, down, far, up_two, down_two = call(
@@ -553,27 +563,35 @@
         [(depth // 2, 3 * height // 2, half), (depth // 2, CHEB, height // 2, half)],
         beside[0], coarse, beside[1], f32(chebyshev_stencil(half)),
     )
-    own, spectrum, back_x = lax.optimization_barrier((own, spectrum, f32(-fine_x)))
+    back = (
+        *bf16_pair(np.concatenate([-fine_x, -coarse_x.T], axis=0)),
+        jnp.asarray(pairs.T, jnp.bfloat16),
+        f32(spread),
+    )
+    own, spectrum, back = lax.optimization_barrier((own, spectrum, back))
+    parcels, up_two, down_two, far = lax.optimization_barrier((parcels, up_two, down_two, far))
+    carried = lax.all_to_all(parcels, "gy", 0, 0, tiled=True)
     from_low = shift_to(up_two, "gz", 2)
     from_high = shift_to(down_two, "gz", -2)
     near = depth // 2
     own = own + shift_to(far, "gz", 4) + from_low[:, :near] + from_high[:, :near]
     solved = own + shift_to(up + from_low[:, near:], "gz", 1) + shift_to(down + from_high[:, near:], "gz", -1)
 
-    (back_x,) = call(load_kernel, [jax.ShapeDtypeStruct((NX, NX), jnp.float32)], [], back_x)
-    carried, back_x = lax.optimization_barrier((carried, back_x))
-    (carries,) = call(
-        carry_kernel, [(2, lines, NX)], [(2, lines * across, lanes)], place, carried, other, weights, smem=(0,)
-    )
+    back = call(load_kernel, [jax.ShapeDtypeStruct(t.shape, t.dtype) for t in back], [], *back)
+    carried, back = lax.optimization_barrier((carried, back))
 
     spectrum = spectrum.reshape(lines, height, NX)
     smooth = f32(local[0]) * spectrum[:, 0:1]
     for y in range(1, height):
         smooth = smooth + f32(local[y]) * spectrum[:, y : y + 1]
-    smooth = smooth + f32(spread[0]) * carries[0][:, None] + f32(spread[1]) * carries[1][:, None]
-    smooth = smooth.reshape(lines * height, NX)
-    solved = dot(f32(pairs.T), solved.reshape(lines * height // 4, half))
-    update = dot(smooth, back_x) + dot(solved, f32(-coarse_x.T))
+    high_x, low_x, repeats, spread = back
+    (update,) = call(
+        final_kernel,
+        [(lines * height, NX)],
+        [(2, lines * across, lanes), (2, lines, NX), (lines * height, NX + half)],
+        place, carried, other, weights, smooth.reshape(lines * height, NX),
+        solved.reshape(lines * height // 4, half), spread, repeats, high_x, low_x, smem=(0,),
+    )
     return (update.reshape(3, depth, height, NX), image)
 
 

time: 92.1 us -> 96.4 us (1.047)
  waiting for transfers between devices: 23.2 us -> 32.1 us
  starting transfers between devices: 50.8 us -> 46.9 us
  matrix products: 2.04 us -> 0 us
  Pallas kernels: 11.6 us -> 13 us
    ppermute x19, waiting for transfers between devices: 22.8 us -> 32.1 us  [shift_to(): return lax.ppermute(x, axis, ring(axis, offset))]
    ppermute x19, starting transfers between devices: 37.6 us -> 34.6 us  [shift_to(): return lax.ppermute(x, axis, ring(axis, offset))]
    ppermute x1, starting transfers between devices: 5.06 us -> 2.48 us  [on_device(): other = lax.ppermute(tails, 'gy', [(i, i ^ 1) for i in range(peers_y)])]
    dot_general x3 -> x0, matrix products: 2.04 us -> none  [dot(): return jnp.dot(a, b, precision=HIGH, preferred_element_type=jnp.float32)]
    all_to_all x1, starting transfers between devices: 8.21 us -> 9.82 us  [on_device(): carried = lax.all_to_all(parcels, 'gy', 0, 0, tiled=True)]
    pallas_call x13, Pallas kernels: 11.6 us -> 13 us  [call(): pl.pallas_call(kernel, out_shape=tuple((shape(dims) if isinstance(dims, t...]
  transfers between devices with their start and end apart: 21 -> 21, of which waited for: 14 -> 16; matrix products, arithmetic and copies ran while one was open for 2% -> 1% of each run, Pallas kernels for 1% -> 1%
where the time goes in v4:
time: 96.4 us; the launch traced here: 95.2 us
  starting transfers between devices  46.9 us (49%)
  waiting for transfers between devices  32.1 us (33%)
  Pallas kernels  13 us (13%)
  local copies, waits for them, and re-layouts  1.45 us (2%)
  between operations  1.21 us (1%)
    ppermute x19, starting transfers between devices, shift_to(): return lax.ppermute(x, axis, ring(axis, offset))  34.6 us
    ppermute x19, waiting for transfers between devices, shift_to(): return lax.ppermute(x, axis, ring(axis, offset))  32.1 us
    pallas_call x13, Pallas kernels, call(): pl.pallas_call(kernel, out_shape=tuple((shape(dims) if isinstance(dims, t...  13 us
    all_to_all x1, starting transfers between devices, on_device(): carried = lax.all_to_all(parcels, 'gy', 0, 0, tiled=True)  9.82 us
    ppermute x1, starting transfers between devices, on_device(): other = lax.ppermute(tails, 'gy', [(i, i ^ 1) for i in range(peers_y)])  2.48 us
  transfers between devices with their start and end apart: 21, of which 16 were waited for; matrix products, arithmetic and copies ran while one was open for 1% of the time, Pallas kernels for 1%

profile of v4, /device:TPU:1, one launch (start us, length us, event | category | flops | bytes accessed | tf_op | source)
XLA Modules:
  0.0 95.2 jit_solution(15651016810780188997)
XLA Ops:
  0.6 2.5 %shard_map.293 = (f32[4,16,512]{2,1,0:T(8,128)}, f32[4,29,512]{2,1,0:T(8,128)}, f32[4,29,512]{2,1,0:T(8,128)}) custom-call(f32[4,16,512]{2,1,0:T(8,128)} %image_hbm.1, s32[4,3,4,16,512]{4,3,2,1,0:T(8,128)} %shifts_ref.11, f32[4,3]{1,0:T(4,128)} %fractions_ref.11), custom_call_target="tpu_custom_call" | custom-call | tf_op jit(solution)/shard_map/pallas_call | solution.py:443
  3.2 2.8 %collective-permute-start = (f32[4,29,512]{2,1,0:T(8,128)}, f32[4,29,512]{2,1,0:T(8,128)S(1)}, u32[]{:S(2)}, u32[]{:S(2)}) collective-permute-start(f32[4,29,512]{2,1,0:T(8,128)} %get-tuple-element.55), channel_id=1, source_target_pairs={{0,8},{8,16},{16,24},{24,32},{32,40},{40,48},{48,56},{56,64},{64,7... | collective-permute-start | bytes 712712 | tf_op jit(solution)/shard_map/ppermute | solution.py:79
  7.5 2.1 %collective-permute-done.low_ref.before_ref = f32[4,29,512]{2,1,0:T(8,128)S(1)} collective-permute-done((f32[4,29,512]{2,1,0:T(8,128)}, f32[4,29,512]{2,1,0:T(8,128)S(1)}, u32[]{:S(2)}, u32[]{:S(2)}) %collective-permute-start) | collective-permute-done | bytes 237600 | tf_op jit(solution)/shard_map/ppermute | solution.py:79
  9.6 2.4 %collective-permute-done.1.high_ref.after_ref = f32[4,29,512]{2,1,0:T(8,128)S(1)} collective-permute-done((f32[4,29,512]{2,1,0:T(8,128)}, f32[4,29,512]{2,1,0:T(8,128)S(1)}, u32[]{:S(2)}, u32[]{:S(2)}) %collective-permute-start.1) | collective-permute-done | bytes 237600 | tf_op jit(solution)/shard_map/ppermute | solution.py:79
  12.8 5.9 %collective-permute-start.3 = (f32[3,24,512]{2,1,0:T(8,128)S(1)}, f32[3,24,512]{2,1,0:T(8,128)S(1)}, u32[]{:S(2)}, u32[]{:S(2)}) collective-permute-start(f32[3,24,512]{2,1,0:T(8,128)S(1)} %get-tuple-element.126), channel_id=1, source_target_pairs={{0,7},{1,0},{2,1},{3,2},{4,3},{5,4},{6,5},{7,6},{8,15},{9,8},{10,9... | collective-permute-start | bytes 442376 | tf_op jit(solution)/shard_map/ppermute | solution.py:79
  18.7 2.1 %collective-permute-done.3.above_ref = f32[3,24,512]{2,1,0:T(8,128)S(1)} collective-permute-done((f32[3,24,512]{2,1,0:T(8,128)S(1)}, f32[3,24,512]{2,1,0:T(8,128)S(1)}, u32[]{:S(2)}, u32[]{:S(2)}) %collective-permute-start.3) | collective-permute-done | bytes 147488 | tf_op jit(solution)/shard_map/ppermute | solution.py:79
  20.8 3.1 %collective-permute-done.2.below_ref = f32[3,24,512]{2,1,0:T(8,128)S(1)} collective-permute-done((f32[3,24,512]{2,1,0:T(8,128)S(1)}, f32[3,24,512]{2,1,0:T(8,128)S(1)}, u32[]{:S(2)}, u32[]{:S(2)}) %collective-permute-start.2) | collective-permute-done | bytes 147488 | tf_op jit(solution)/shard_map/ppermute | solution.py:79
  25.3 2.7 %collective-permute-start.5 = (f32[4,16,512]{2,1,0:T(8,128)S(1)}, f32[4,16,512]{2,1,0:T(8,128)S(1)}, u32[]{:S(2)}, u32[]{:S(2)}) collective-permute-start(f32[4,16,512]{2,1,0:T(8,128)S(1)} %get-tuple-element.63), channel_id=1, source_target_pairs={{0,7},{1,0},{2,1},{3,2},{4,3},{5,4},{6,5},{7,6},{8,15},{9,8},{10,9... | collective-permute-start | bytes 393224 | tf_op jit(solution)/shard_map/ppermute | solution.py:79
  28.0 2.4 %collective-permute-done.4.below_ref.first_ref = f32[4,16,512]{2,1,0:T(8,128)S(1)} collective-permute-done((f32[4,16,512]{2,1,0:T(8,128)S(1)}, f32[4,16,512]{2,1,0:T(8,128)S(1)}, u32[]{:S(2)}, u32[]{:S(2)}) %collective-permute-start.4) | collective-permute-done | bytes 131104 | tf_op jit(solution)/shard_map/ppermute | solution.py:79
  31.4 4.2 %collective-permute-start.6 = (f32[4,7,512]{2,1,0:T(8,128)S(1)}, f32[4,7,512]{2,1,0:T(8,128)S(1)}, u32[]{:S(2)}, u32[]{:S(2)}) collective-permute-start(f32[4,7,512]{2,1,0:T(8,128)S(1)} %get-tuple-element.65), channel_id=1, source_target_pairs={{0,8},{8,16},{16,24},{24,32},{32,40},{40,48},{48,56},{56,64},{64,7... | collective-permute-start | bytes 172040 | tf_op jit(solution)/shard_map/ppermute | solution.py:79
  36.9 2.4 %collective-permute-done.7.high_ref = f32[4,7,512]{2,1,0:T(8,128)S(1)} collective-permute-done((f32[4,7,512]{2,1,0:T(8,128)S(1)}, f32[4,7,512]{2,1,0:T(8,128)S(1)}, u32[]{:S(2)}, u32[]{:S(2)}) %collective-permute-start.7) | collective-permute-done | bytes 57376 | tf_op jit(solution)/shard_map/ppermute | solution.py:79
  40.1 2.7 %collective-permute-start.9 = (f32[3,24,512]{2,1,0:T(8,128)S(1)}, f32[3,24,512]{2,1,0:T(8,128)S(1)}, u32[]{:S(2)}, u32[]{:S(2)}) collective-permute-start(f32[3,24,512]{2,1,0:T(8,128)S(1)} %get-tuple-element.124), channel_id=1, source_target_pairs={{0,7},{1,0},{2,1},{3,2},{4,3},{5,4},{6,5},{7,6},{8,15},{9,8},{10,9... | collective-permute-start | bytes 442376 | tf_op jit(solution)/shard_map/ppermute | solution.py:79
  42.8 2.1 %collective-permute-done.9.above_ref = f32[3,24,512]{2,1,0:T(8,128)S(1)} collective-permute-done((f32[3,24,512]{2,1,0:T(8,128)S(1)}, f32[3,24,512]{2,1,0:T(8,128)S(1)}, u32[]{:S(2)}, u32[]{:S(2)}) %collective-permute-start.9) | collective-permute-done | bytes 147488 | tf_op jit(solution)/shard_map/ppermute | solution.py:79
  44.9 3.1 %collective-permute-done.8.below_ref = f32[3,24,512]{2,1,0:T(8,128)S(1)} collective-permute-done((f32[3,24,512]{2,1,0:T(8,128)S(1)}, f32[3,24,512]{2,1,0:T(8,128)S(1)}, u32[]{:S(2)}, u32[]{:S(2)}) %collective-permute-start.8) | collective-permute-done | bytes 147488 | tf_op jit(solution)/shard_map/ppermute | solution.py:79
  51.1 2.9 %collective-permute-done.11.above_ref = f32[4,24,512]{2,1,0:T(8,128)S(1)} collective-permute-done((f32[4,24,512]{2,1,0:T(8,128)S(1)}, f32[4,24,512]{2,1,0:T(8,128)S(1)}, u32[]{:S(2)}, u32[]{:S(2)}) %collective-permute-start.11) | collective-permute-done | bytes 196640 | tf_op jit(solution)/shard_map/ppermute | solution.py:79
  54.0 1.5 %collective-permute-done.10.below_ref = f32[4,24,512]{2,1,0:T(8,128)S(1)} collective-permute-done((f32[4,24,512]{2,1,0:T(8,128)S(1)}, f32[4,24,512]{2,1,0:T(8,128)S(1)}, u32[]{:S(2)}, u32[]{:S(2)}) %collective-permute-start.10) | collective-permute-done | bytes 196640 | tf_op jit(solution)/shard_map/ppermute | solution.py:79
  55.5 2.2 %shard_map.301 = (f32[4,16,512]{2,1,0:T(8,128)}, f32[192,512]{1,0:T(8,128)S(1)}, f32[3,2,8,256]{3,2,1,0:T(8,128)S(1)}, f32[96,128]{1,0:T(8,128)S(1)}) custom-call(f32[4,24,512]{2,1,0:T(8,128)S(1)} %collective-permute-done.10.below_ref, f32[4,24,512]{2,1,0:T(8,128)S(1)} %shard_map.299.image_ref, f32[4,24,512]{2,1,0:T(8,128)S(1)} %collective-permute-done.11.above_ref, ...), custom_call_target="tpu_custom_call" | custom-call | tf_op jit(solution)/shard_map/pallas_call | solution.py:443
  57.6 6.5 %collective-permute-start.14 = (f32[3,2,8,256]{3,2,1,0:T(8,128)S(1)}, f32[3,2,8,256]{3,2,1,0:T(8,128)S(1)}, u32[]{:S(2)}, u32[]{:S(2)}) collective-permute-start(f32[3,2,8,256]{3,2,1,0:T(8,128)S(1)} %get-tuple-element.80.own_ref), channel_id=1, source_target_pairs={{0,248},{8,0},{16,8},{24,16},{32,24},{40,32},{48,40},{56,48},{64,5... | collective-permute-start | bytes 147464 | tf_op jit(solution)/shard_map/ppermute | solution.py:79
  64.1 2.5 %collective-permute-start.12 = (f32[96,128]{1,0:T(8,128)S(1)}, f32[96,128]{1,0:T(8,128)S(1)}, u32[]{:S(2)}, u32[]{:S(2)}) collective-permute-start(f32[96,128]{1,0:T(8,128)S(1)} %get-tuple-element.79.own_ref), channel_id=1, source_target_pairs={{0,8},{8,0},{16,24},{24,16},{32,40},{40,32},{48,56},{56,48},{64,72... | collective-permute-start | bytes 147464 | tf_op jit(solution)/shard_map/ppermute | solution.py:554
  69.1 9.8 %all-to-all-start = ((f32[32,48,128]{2,1,0:T(8,128)}), f32[32,48,128]{2,1,0:T(8,128)S(1)}, u32[]{:S(2)}, u32[]{:S(2)}) async-start(f32[32,48,128]{2,1,0:T(8,128)} %shard_map.302), calls=%async_computation | async-start | bytes 1572864 | tf_op jit(solution)/shard_map/all_to_all | solution.py:573
  80.3 3.6 %collective-permute-start.17 = (f32[3,4,8,256]{3,2,1,0:T(8,128)S(1)}, f32[3,4,8,256]{3,2,1,0:T(8,128)S(1)}, u32[]{:S(2)}, u32[]{:S(2)}) collective-permute-start(f32[3,4,8,256]{3,2,1,0:T(8,128)S(1)} %get-tuple-element.100), channel_id=1, source_target_pairs={{0,6},{1,7},{2,0},{3,1},{4,2},{5,3},{6,4},{7,5},{8,14},{9,15},{10,... | collective-permute-start | bytes 294920 | tf_op jit(solution)/shard_map/ppermute | solution.py:79
  84.0 3.9 %collective-permute-done.16 = f32[3,4,8,256]{3,2,1,0:T(8,128)S(1)} collective-permute-done((f32[3,4,8,256]{3,2,1,0:T(8,128)S(1)}, f32[3,4,8,256]{3,2,1,0:T(8,128)S(1)}, u32[]{:S(2)}, u32[]{:S(2)}) %collective-permute-start.16) | collective-permute-done | bytes 98336 | tf_op jit(solution)/shard_map/ppermute | solution.py:79
  87.8 2.2 %collective-permute-start.18 = (f32[3,2,8,256]{3,2,1,0:T(8,128)S(1)}, f32[3,2,8,256]{3,2,1,0:T(8,128)S(1)}, u32[]{:S(2)}, u32[]{:S(2)}) collective-permute-start(f32[3,2,8,256]{3,2,1,0:T(8,128)S(1)} %slice_add_fusion.1), channel_id=1, source_target_pairs={{0,1},{1,2},{2,3},{3,4},{4,5},{5,6},{6,7},{7,0},{8,9},{9,10},{10,1... | collective-permute-start | bytes 147464 | tf_op jit(solution)/shard_map/ppermute | solution.py:79
  93.7 1.5 %shard_map.305 = f32[192,512]{1,0:T(8,128)} custom-call(s32[1]{0:T(128)} %bitcast.place_ref, f32[32,48,128]{2,1,0:T(8,128)S(1)} %all-to-all-done.carried_ref, f32[96,128]{1,0:T(8,128)S(1)} %collective-permute-done.12.other_ref, f32[2,48,128]{2,1,0:T(8,128)S(1)} %copy-done.5, f32[192,512]{1,0:T(8,128)S(1)} %bitcast.37, f32[48,256]{1,0:T(8,128)S(1)} %bitcast.39, ...), custom_call_target="tpu_custom_call" | custom-call | tf_op jit(solution)/shard_map/pallas_call | solution.py:443
  (106 shorter events, 17.0 us)
Async XLA Ops:
  3.2 6.4 %collective-permute-start = (f32[4,29,512]{2,1,0:T(8,128)}, f32[4,29,512]{2,1,0:T(8,128)S(1)}, u32[]{:S(2)}, u32[]{:S(2)}) collective-permute-start(f32[4,29,512]{2,1,0:T(8,128)} %get-tuple-element.55), channel_id=1, source_target_pairs={{0,8},{8,16},{16,24},{24,32},{32,40},{40,48},{48,56},{56,64},{64,7... | collective-permute-start | bytes 712712 | tf_op jit(solution)/shard_map/ppermute | solution.py:79
  6.0 6.0 %collective-permute-start.1 = (f32[4,29,512]{2,1,0:T(8,128)}, f32[4,29,512]{2,1,0:T(8,128)S(1)}, u32[]{:S(2)}, u32[]{:S(2)}) collective-permute-start(f32[4,29,512]{2,1,0:T(8,128)} %get-tuple-element.56), channel_id=1, source_target_pairs={{0,248},{8,0},{16,8},{24,16},{32,24},{40,32},{48,40},{56,48},{64,5... | collective-permute-start | bytes 712712 | tf_op jit(solution)/shard_map/ppermute | solution.py:79
  12.8 8.0 %collective-permute-start.3 = (f32[3,24,512]{2,1,0:T(8,128)S(1)}, f32[3,24,512]{2,1,0:T(8,128)S(1)}, u32[]{:S(2)}, u32[]{:S(2)}) collective-permute-start(f32[3,24,512]{2,1,0:T(8,128)S(1)} %get-tuple-element.126), channel_id=1, source_target_pairs={{0,7},{1,0},{2,1},{3,2},{4,3},{5,4},{6,5},{7,6},{8,15},{9,8},{10,9... | collective-permute-start | bytes 442376 | tf_op jit(solution)/shard_map/ppermute | solution.py:79
  18.7 5.2 %collective-permute-start.2 = (f32[3,24,512]{2,1,0:T(8,128)S(1)}, f32[3,24,512]{2,1,0:T(8,128)S(1)}, u32[]{:S(2)}, u32[]{:S(2)}) collective-permute-start(f32[3,24,512]{2,1,0:T(8,128)S(1)} %get-tuple-element.127), channel_id=1, source_target_pairs={{0,1},{1,2},{2,3},{3,4},{4,5},{5,6},{6,7},{7,0},{8,9},{9,10},{10,1... | collective-permute-start | bytes 442376 | tf_op jit(solution)/shard_map/ppermute | solution.py:79
  25.2 5.1 %collective-permute-start.4 = (f32[4,16,512]{2,1,0:T(8,128)S(1)}, f32[4,16,512]{2,1,0:T(8,128)S(1)}, u32[]{:S(2)}, u32[]{:S(2)}) collective-permute-start(f32[4,16,512]{2,1,0:T(8,128)S(1)} %get-tuple-element.61), channel_id=1, source_target_pairs={{0,1},{1,2},{2,3},{3,4},{4,5},{5,6},{6,7},{7,0},{8,9},{9,10},{10,1... | collective-permute-start | bytes 393224 | tf_op jit(solution)/shard_map/ppermute | solution.py:79
  25.3 5.0 %collective-permute-start.5 = (f32[4,16,512]{2,1,0:T(8,128)S(1)}, f32[4,16,512]{2,1,0:T(8,128)S(1)}, u32[]{:S(2)}, u32[]{:S(2)}) collective-permute-start(f32[4,16,512]{2,1,0:T(8,128)S(1)} %get-tuple-element.63), channel_id=1, source_target_pairs={{0,7},{1,0},{2,1},{3,2},{4,3},{5,4},{6,5},{7,6},{8,15},{9,8},{10,9... | collective-permute-start | bytes 393224 | tf_op jit(solution)/shard_map/ppermute | solution.py:79
  31.4 5.5 %collective-permute-start.6 = (f32[4,7,512]{2,1,0:T(8,128)S(1)}, f32[4,7,512]{2,1,0:T(8,128)S(1)}, u32[]{:S(2)}, u32[]{:S(2)}) collective-permute-start(f32[4,7,512]{2,1,0:T(8,128)S(1)} %get-tuple-element.65), channel_id=1, source_target_pairs={{0,8},{8,16},{16,24},{24,32},{32,40},{40,48},{48,56},{56,64},{64,7... | collective-permute-start | bytes 172040 | tf_op jit(solution)/shard_map/ppermute | solution.py:79
  35.6 3.7 %collective-permute-start.7 = (f32[4,7,512]{2,1,0:T(8,128)S(1)}, f32[4,7,512]{2,1,0:T(8,128)S(1)}, u32[]{:S(2)}, u32[]{:S(2)}) collective-permute-start(f32[4,7,512]{2,1,0:T(8,128)S(1)} %get-tuple-element.66), channel_id=1, source_target_pairs={{0,248},{8,0},{16,8},{24,16},{32,24},{40,32},{48,40},{56,48},{64,5... | collective-permute-start | bytes 172040 | tf_op jit(solution)/shard_map/ppermute | solution.py:79
  40.1 4.9 %collective-permute-start.9 = (f32[3,24,512]{2,1,0:T(8,128)S(1)}, f32[3,24,512]{2,1,0:T(8,128)S(1)}, u32[]{:S(2)}, u32[]{:S(2)}) collective-permute-start(f32[3,24,512]{2,1,0:T(8,128)S(1)} %get-tuple-element.124), channel_id=1, source_target_pairs={{0,7},{1,0},{2,1},{3,2},{4,3},{5,4},{6,5},{7,6},{8,15},{9,8},{10,9... | collective-permute-start | bytes 442376 | tf_op jit(solution)/shard_map/ppermute | solution.py:79
  42.8 5.2 %collective-permute-start.8 = (f32[3,24,512]{2,1,0:T(8,128)S(1)}, f32[3,24,512]{2,1,0:T(8,128)S(1)}, u32[]{:S(2)}, u32[]{:S(2)}) collective-permute-start(f32[3,24,512]{2,1,0:T(8,128)S(1)} %get-tuple-element.125), channel_id=1, source_target_pairs={{0,1},{1,2},{2,3},{3,4},{4,5},{5,6},{6,7},{7,0},{8,9},{9,10},{10,1... | collective-permute-start | bytes 442376 | tf_op jit(solution)/shard_map/ppermute | solution.py:79
  49.4 4.6 %collective-permute-start.11 = (f32[4,24,512]{2,1,0:T(8,128)S(1)}, f32[4,24,512]{2,1,0:T(8,128)S(1)}, u32[]{:S(2)}, u32[]{:S(2)}) collective-permute-start(f32[4,24,512]{2,1,0:T(8,128)S(1)} %shard_map.299.image_ref), channel_id=1, source_target_pairs={{0,7},{1,0},{2,1},{3,2},{4,3},{5,4},{6,5},{7,6},{8,15},{9,8},{10,9... | collective-permute-start | bytes 589832 | tf_op jit(solution)/shard_map/ppermute | solution.py:79
  49.5 6.0 %collective-permute-start.10 = (f32[4,24,512]{2,1,0:T(8,128)S(1)}, f32[4,24,512]{2,1,0:T(8,128)S(1)}, u32[]{:S(2)}, u32[]{:S(2)}) collective-permute-start(f32[4,24,512]{2,1,0:T(8,128)S(1)} %shard_map.299.image_ref), channel_id=1, source_target_pairs={{0,1},{1,2},{2,3},{3,4},{4,5},{5,6},{6,7},{7,0},{8,9},{9,10},{10,1... | collective-permute-start | bytes 589832 | tf_op jit(solution)/shard_map/ppermute | solution.py:79
  57.6 9.0 %collective-permute-start.14 = (f32[3,2,8,256]{3,2,1,0:T(8,128)S(1)}, f32[3,2,8,256]{3,2,1,0:T(8,128)S(1)}, u32[]{:S(2)}, u32[]{:S(2)}) collective-permute-start(f32[3,2,8,256]{3,2,1,0:T(8,128)S(1)} %get-tuple-element.80.own_ref), channel_id=1, source_target_pairs={{0,248},{8,0},{16,8},{24,16},{32,24},{40,32},{48,40},{56,48},{64,5... | collective-permute-start | bytes 147464 | tf_op jit(solution)/shard_map/ppermute | solution.py:79
  64.1 3.2 %collective-permute-start.13 = (f32[3,2,8,256]{3,2,1,0:T(8,128)S(1)}, f32[3,2,8,256]{3,2,1,0:T(8,128)S(1)}, u32[]{:S(2)}, u32[]{:S(2)}) collective-permute-start(f32[3,2,8,256]{3,2,1,0:T(8,128)S(1)} %get-tuple-element.80.own_ref), channel_id=1, source_target_pairs={{0,8},{8,16},{16,24},{24,32},{32,40},{40,48},{48,56},{56,64},{64,7... | collective-permute-start | bytes 147464 | tf_op jit(solution)/shard_map/ppermute | solution.py:79
  64.1 3.9 %collective-permute-start.12 = (f32[96,128]{1,0:T(8,128)S(1)}, f32[96,128]{1,0:T(8,128)S(1)}, u32[]{:S(2)}, u32[]{:S(2)}) collective-permute-start(f32[96,128]{1,0:T(8,128)S(1)} %get-tuple-element.79.own_ref), channel_id=1, source_target_pairs={{0,8},{8,0},{16,24},{24,16},{32,40},{40,32},{48,56},{56,48},{64,72... | collective-permute-start | bytes 147464 | tf_op jit(solution)/shard_map/ppermute | solution.py:554
  69.0 21.7 %copy-start.17 = (f32[16,512]{1,0:T(8,128)S(1)}, f32[16,512]{1,0:T(8,128)}, u32[]{:S(2)}) copy-start(f32[16,512]{1,0:T(8,128)} %constant.80.clone) | copy-start | bytes 98308
  69.0 21.7 %copy-start.18 = (f32[16,512]{1,0:T(8,128)S(1)}, f32[16,512]{1,0:T(8,128)}, u32[]{:S(2)}) copy-start(f32[16,512]{1,0:T(8,128)} %constant.79.clone) | copy-start | bytes 98308
  69.0 21.7 %copy-start.19 = (f32[16,512]{1,0:T(8,128)S(1)}, f32[16,512]{1,0:T(8,128)}, u32[]{:S(2)}) copy-start(f32[16,512]{1,0:T(8,128)} %constant.78.clone) | copy-start | bytes 98308
  69.1 24.5 %all-to-all-start = ((f32[32,48,128]{2,1,0:T(8,128)}), f32[32,48,128]{2,1,0:T(8,128)S(1)}, u32[]{:S(2)}, u32[]{:S(2)}) async-start(f32[32,48,128]{2,1,0:T(8,128)} %shard_map.302), calls=%async_computation | async-start | bytes 1572864 | tf_op jit(solution)/shard_map/all_to_all | solution.py:573
  79.0 12.5 %collective-permute-start.15 = (f32[3,2,8,256]{3,2,1,0:T(8,128)S(1)}, f32[3,2,8,256]{3,2,1,0:T(8,128)S(1)}, u32[]{:S(2)}, u32[]{:S(2)}) collective-permute-start(f32[3,2,8,256]{3,2,1,0:T(8,128)S(1)} %get-tuple-element.98), channel_id=1, source_target_pairs={{0,4},{1,5},{2,6},{3,7},{4,0},{5,1},{6,2},{7,3},{8,12},{9,13},{10,... | collective-permute-start | bytes 147464 | tf_op jit(solution)/shard_map/ppermute | solution.py:79
  80.3 7.6 %collective-permute-start.16 = (f32[3,4,8,256]{3,2,1,0:T(8,128)S(1)}, f32[3,4,8,256]{3,2,1,0:T(8,128)S(1)}, u32[]{:S(2)}, u32[]{:S(2)}) collective-permute-start(f32[3,4,8,256]{3,2,1,0:T(8,128)S(1)} %get-tuple-element.99), channel_id=1, source_target_pairs={{0,2},{1,3},{2,4},{3,5},{4,6},{5,7},{6,0},{7,1},{8,10},{9,11},{10,... | collective-permute-start | bytes 294920 | tf_op jit(solution)/shard_map/ppermute | solution.py:79
  80.3 10.3 %collective-permute-start.17 = (f32[3,4,8,256]{3,2,1,0:T(8,128)S(1)}, f32[3,4,8,256]{3,2,1,0:T(8,128)S(1)}, u32[]{:S(2)}, u32[]{:S(2)}) collective-permute-start(f32[3,4,8,256]{3,2,1,0:T(8,128)S(1)} %get-tuple-element.100), channel_id=1, source_target_pairs={{0,6},{1,7},{2,0},{3,1},{4,2},{5,3},{6,4},{7,5},{8,14},{9,15},{10,... | collective-permute-start | bytes 294920 | tf_op jit(solution)/shard_map/ppermute | solution.py:79
  87.8 4.5 %collective-permute-start.18 = (f32[3,2,8,256]{3,2,1,0:T(8,128)S(1)}, f32[3,2,8,256]{3,2,1,0:T(8,128)S(1)}, u32[]{:S(2)}, u32[]{:S(2)}) collective-permute-start(f32[3,2,8,256]{3,2,1,0:T(8,128)S(1)} %slice_add_fusion.1), channel_id=1, source_target_pairs={{0,1},{1,2},{2,3},{3,4},{4,5},{5,6},{6,7},{7,0},{8,9},{9,10},{10,1... | collective-permute-start | bytes 147464 | tf_op jit(solution)/shard_map/ppermute | solution.py:79
  90.6 3.0 %collective-permute-start.19 = (f32[3,2,8,256]{3,2,1,0:T(8,128)S(1)}, f32[3,2,8,256]{3,2,1,0:T(8,128)S(1)}, u32[]{:S(2)}, u32[]{:S(2)}) collective-permute-start(f32[3,2,8,256]{3,2,1,0:T(8,128)S(1)} %slice_add_fusion), channel_id=1, source_target_pairs={{0,7},{1,0},{2,1},{3,2},{4,3},{5,4},{6,5},{7,6},{8,15},{9,8},{10,9... | collective-permute-start | bytes 147464 | tf_op jit(solution)/shard_map/ppermute | solution.py:79
  (27 other events, 434.5 us)

commit v5 on v3

--- a/solution.py
+++ b/solution.py
@@ -553,9 +553,10 @@
         [(depth // 2, 3 * height // 2, half), (depth // 2, CHEB, height // 2, half)],
         beside[0], coarse, beside[1], f32(chebyshev_stencil(half)),
     )
-    own, spectrum, back_x = lax.optimization_barrier((own, spectrum, f32(-fine_x)))
+    own, back_x = lax.optimization_barrier((own, f32(-fine_x)))
     from_low = shift_to(up_two, "gz", 2)
     from_high = shift_to(down_two, "gz", -2)
+    from_low, spectrum = lax.optimization_barrier((from_low, spectrum))
     near = depth // 2
     own = own + shift_to(far, "gz", 4) + from_low[:, :near] + from_high[:, :near]
     solved = own + shift_to(up + from_low[:, near:], "gz", 1) + shift_to(down + from_high[:, near:], "gz", -1)

time: 92.1 us -> 95.9 us (1.041)
  other arithmetic: 0.72 us -> 2.37 us
  local copies, waits for them, and re-layouts: 1.68 us -> 3.3 us
    ppermute x19, starting transfers between devices: 37.6 us -> 40 us  [shift_to(): return lax.ppermute(x, axis, ring(axis, offset))]
    unnamed x70 -> x78, local copies, waits for them, and re-layouts: 1.36 us -> 2.99 us
    all_to_all x1, starting transfers between devices: 8.21 us -> 6.61 us  [on_device(): carried = lax.all_to_all(parcels, 'gy', 0, 0, tiled=True)]
    ppermute x19, waiting for transfers between devices: 22.8 us -> 21.6 us  [shift_to(): return lax.ppermute(x, axis, ring(axis, offset))]
  transfers between devices with their start and end apart: 21 -> 21, of which waited for: 14 -> 15; matrix products, arithmetic and copies ran while one was open for 2% -> 3% of each run, Pallas kernels for 1% -> 1%
where the time goes in v5:
time: 95.9 us; the launch traced here: 95.5 us
  starting transfers between devices  51.4 us (54%)
  waiting for transfers between devices  22.9 us (24%)
  Pallas kernels  12.2 us (13%)
  local copies, waits for them, and re-layouts  3.3 us (3%)
  other arithmetic  2.37 us (2%)
  matrix products  2.04 us (2%)
  between operations  1.26 us (1%)
    ppermute x19, starting transfers between devices, shift_to(): return lax.ppermute(x, axis, ring(axis, offset))  40 us
    ppermute x19, waiting for transfers between devices, shift_to(): return lax.ppermute(x, axis, ring(axis, offset))  21.6 us
    pallas_call x13, Pallas kernels, call(): pl.pallas_call(kernel, out_shape=tuple((shape(dims) if isinstance(dims, t...  12.2 us
    all_to_all x1, starting transfers between devices, on_device(): carried = lax.all_to_all(parcels, 'gy', 0, 0, tiled=True)  6.61 us
    ppermute x1, starting transfers between devices, on_device(): other = lax.ppermute(tails, 'gy', [(i, i ^ 1) for i in range(peers_y)])  4.86 us
    unnamed x78, local copies, waits for them, and re-layouts  2.99 us
    dot_general x3, matrix products, dot(): return jnp.dot(a, b, precision=HIGH, preferred_element_type=jnp.float32)  2.04 us
  transfers between devices with their start and end apart: 21, of which 15 were waited for; matrix products, arithmetic and copies ran while one was open for 3% of the time, Pallas kernels for 1%

profile of v5, /device:TPU:1, one launch (start us, length us, event | category | flops | bytes accessed | tf_op | source)
XLA Modules:
  0.0 95.5 jit_solution(18302473085390190958)
XLA Ops:
  0.6 2.6 %shard_map.302 = (f32[4,16,512]{2,1,0:T(8,128)}, f32[4,29,512]{2,1,0:T(8,128)}, f32[4,29,512]{2,1,0:T(8,128)}) custom-call(f32[4,16,512]{2,1,0:T(8,128)} %image_hbm.1, s32[4,3,4,16,512]{4,3,2,1,0:T(8,128)} %shifts_ref.11, f32[4,3]{1,0:T(4,128)} %fractions_ref.11), custom_call_target="tpu_custom_call" | custom-call | tf_op jit(solution)/shard_map/pallas_call | solution.py:432
  3.2 2.8 %collective-permute-start = (f32[4,29,512]{2,1,0:T(8,128)}, f32[4,29,512]{2,1,0:T(8,128)S(1)}, u32[]{:S(2)}, u32[]{:S(2)}) collective-permute-start(f32[4,29,512]{2,1,0:T(8,128)} %get-tuple-element.42), channel_id=1, source_target_pairs={{0,8},{8,16},{16,24},{24,32},{32,40},{40,48},{48,56},{56,64},{64,7... | collective-permute-start | bytes 712712 | tf_op jit(solution)/shard_map/ppermute | solution.py:79
  7.5 2.1 %collective-permute-done.low_ref.before_ref = f32[4,29,512]{2,1,0:T(8,128)S(1)} collective-permute-done((f32[4,29,512]{2,1,0:T(8,128)}, f32[4,29,512]{2,1,0:T(8,128)S(1)}, u32[]{:S(2)}, u32[]{:S(2)}) %collective-permute-start) | collective-permute-done | bytes 237600 | tf_op jit(solution)/shard_map/ppermute | solution.py:79
  9.6 2.4 %collective-permute-done.1.high_ref.after_ref = f32[4,29,512]{2,1,0:T(8,128)S(1)} collective-permute-done((f32[4,29,512]{2,1,0:T(8,128)}, f32[4,29,512]{2,1,0:T(8,128)S(1)}, u32[]{:S(2)}, u32[]{:S(2)}) %collective-permute-start.1) | collective-permute-done | bytes 237600 | tf_op jit(solution)/shard_map/ppermute | solution.py:79
  12.8 2.0 %collective-permute-start.2 = (f32[3,24,512]{2,1,0:T(8,128)S(1)}, f32[3,24,512]{2,1,0:T(8,128)S(1)}, u32[]{:S(2)}, u32[]{:S(2)}) collective-permute-start(f32[3,24,512]{2,1,0:T(8,128)S(1)} %get-tuple-element.101), channel_id=1, source_target_pairs={{0,1},{1,2},{2,3},{3,4},{4,5},{5,6},{6,7},{7,0},{8,9},{9,10},{10,1... | collective-permute-start | bytes 442376 | tf_op jit(solution)/shard_map/ppermute | solution.py:79
  14.8 4.0 %collective-permute-start.3 = (f32[3,24,512]{2,1,0:T(8,128)S(1)}, f32[3,24,512]{2,1,0:T(8,128)S(1)}, u32[]{:S(2)}, u32[]{:S(2)}) collective-permute-start(f32[3,24,512]{2,1,0:T(8,128)S(1)} %get-tuple-element.100), channel_id=1, source_target_pairs={{0,7},{1,0},{2,1},{3,2},{4,3},{5,4},{6,5},{7,6},{8,15},{9,8},{10,9... | collective-permute-start | bytes 442376 | tf_op jit(solution)/shard_map/ppermute | solution.py:79
  18.8 2.4 %collective-permute-done.2.below_ref = f32[3,24,512]{2,1,0:T(8,128)S(1)} collective-permute-done((f32[3,24,512]{2,1,0:T(8,128)S(1)}, f32[3,24,512]{2,1,0:T(8,128)S(1)}, u32[]{:S(2)}, u32[]{:S(2)}) %collective-permute-start.2) | collective-permute-done | bytes 147488 | tf_op jit(solution)/shard_map/ppermute | solution.py:79
  22.7 2.8 %collective-permute-start.5 = (f32[4,16,512]{2,1,0:T(8,128)S(1)}, f32[4,16,512]{2,1,0:T(8,128)S(1)}, u32[]{:S(2)}, u32[]{:S(2)}) collective-permute-start(f32[4,16,512]{2,1,0:T(8,128)S(1)} %get-tuple-element.50), channel_id=1, source_target_pairs={{0,7},{1,0},{2,1},{3,2},{4,3},{5,4},{6,5},{7,6},{8,15},{9,8},{10,9... | collective-permute-start | bytes 393224 | tf_op jit(solution)/shard_map/ppermute | solution.py:79
  25.5 2.3 %collective-permute-done.4.below_ref.first_ref = f32[4,16,512]{2,1,0:T(8,128)S(1)} collective-permute-done((f32[4,16,512]{2,1,0:T(8,128)S(1)}, f32[4,16,512]{2,1,0:T(8,128)S(1)}, u32[]{:S(2)}, u32[]{:S(2)}) %collective-permute-start.4) | collective-permute-done | bytes 131104 | tf_op jit(solution)/shard_map/ppermute | solution.py:79
  28.8 3.9 %collective-permute-start.6 = (f32[4,7,512]{2,1,0:T(8,128)S(1)}, f32[4,7,512]{2,1,0:T(8,128)S(1)}, u32[]{:S(2)}, u32[]{:S(2)}) collective-permute-start(f32[4,7,512]{2,1,0:T(8,128)S(1)} %get-tuple-element.52), channel_id=1, source_target_pairs={{0,8},{8,16},{16,24},{24,32},{32,40},{40,48},{48,56},{56,64},{64,7... | collective-permute-start | bytes 172040 | tf_op jit(solution)/shard_map/ppermute | solution.py:79
  34.0 2.4 %collective-permute-done.7.high_ref = f32[4,7,512]{2,1,0:T(8,128)S(1)} collective-permute-done((f32[4,7,512]{2,1,0:T(8,128)S(1)}, f32[4,7,512]{2,1,0:T(8,128)S(1)}, u32[]{:S(2)}, u32[]{:S(2)}) %collective-permute-start.7) | collective-permute-done | bytes 57376 | tf_op jit(solution)/shard_map/ppermute | solution.py:79
  37.2 2.4 %collective-permute-start.8 = (f32[3,24,512]{2,1,0:T(8,128)S(1)}, f32[3,24,512]{2,1,0:T(8,128)S(1)}, u32[]{:S(2)}, u32[]{:S(2)}) collective-permute-start(f32[3,24,512]{2,1,0:T(8,128)S(1)} %get-tuple-element.99), channel_id=1, source_target_pairs={{0,1},{1,2},{2,3},{3,4},{4,5},{5,6},{6,7},{7,0},{8,9},{9,10},{10,1... | collective-permute-start | bytes 442376 | tf_op jit(solution)/shard_map/ppermute | solution.py:79
  40.2 2.4 %collective-permute-done.8.below_ref = f32[3,24,512]{2,1,0:T(8,128)S(1)} collective-permute-done((f32[3,24,512]{2,1,0:T(8,128)S(1)}, f32[3,24,512]{2,1,0:T(8,128)S(1)}, u32[]{:S(2)}, u32[]{:S(2)}) %collective-permute-start.8) | collective-permute-done | bytes 147488 | tf_op jit(solution)/shard_map/ppermute | solution.py:79
  45.0 1.5 %collective-permute-start.10 = (f32[4,24,512]{2,1,0:T(8,128)S(1)}, f32[4,24,512]{2,1,0:T(8,128)S(1)}, u32[]{:S(2)}, u32[]{:S(2)}) collective-permute-start(f32[4,24,512]{2,1,0:T(8,128)S(1)} %shard_map.308.image_ref), channel_id=1, source_target_pairs={{0,1},{1,2},{2,3},{3,4},{4,5},{5,6},{6,7},{7,0},{8,9},{9,10},{10,1... | collective-permute-start | bytes 589832 | tf_op jit(solution)/shard_map/ppermute | solution.py:79
  47.9 2.9 %collective-permute-done.10.below_ref = f32[4,24,512]{2,1,0:T(8,128)S(1)} collective-permute-done((f32[4,24,512]{2,1,0:T(8,128)S(1)}, f32[4,24,512]{2,1,0:T(8,128)S(1)}, u32[]{:S(2)}, u32[]{:S(2)}) %collective-permute-start.10) | collective-permute-done | bytes 196640 | tf_op jit(solution)/shard_map/ppermute | solution.py:79
  51.1 2.2 %shard_map.310 = (f32[4,16,512]{2,1,0:T(8,128)}, f32[192,512]{1,0:T(8,128)S(1)}, f32[3,2,8,256]{3,2,1,0:T(8,128)S(1)}, f32[96,128]{1,0:T(8,128)S(1)}) custom-call(f32[4,24,512]{2,1,0:T(8,128)S(1)} %collective-permute-done.10.below_ref, f32[4,24,512]{2,1,0:T(8,128)S(1)} %shard_map.308.image_ref, f32[4,24,512]{2,1,0:T(8,128)S(1)} %collective-permute-done.11.above_ref, ...), custom_call_target="tpu_custom_call" | custom-call | tf_op jit(solution)/shard_map/pallas_call | solution.py:432
  53.3 5.1 %collective-permute-start.12 = (f32[3,2,8,256]{3,2,1,0:T(8,128)S(1)}, f32[3,2,8,256]{3,2,1,0:T(8,128)S(1)}, u32[]{:S(2)}, u32[]{:S(2)}) collective-permute-start(f32[3,2,8,256]{3,2,1,0:T(8,128)S(1)} %get-tuple-element.66.own_ref), channel_id=1, source_target_pairs={{0,8},{8,16},{16,24},{24,32},{32,40},{40,48},{48,56},{56,64},{64,7... | collective-permute-start | bytes 147464 | tf_op jit(solution)/shard_map/ppermute | solution.py:79
  58.4 1.6 %collective-permute-start.13 = (f32[3,2,8,256]{3,2,1,0:T(8,128)S(1)}, f32[3,2,8,256]{3,2,1,0:T(8,128)S(1)}, u32[]{:S(2)}, u32[]{:S(2)}) collective-permute-start(f32[3,2,8,256]{3,2,1,0:T(8,128)S(1)} %get-tuple-element.66.own_ref), channel_id=1, source_target_pairs={{0,248},{8,0},{16,8},{24,16},{32,24},{40,32},{48,40},{56,48},{64,5... | collective-permute-start | bytes 147464 | tf_op jit(solution)/shard_map/ppermute | solution.py:79
  64.2 2.1 %collective-permute-start.14 = (f32[3,4,8,256]{3,2,1,0:T(8,128)}, f32[3,4,8,256]{3,2,1,0:T(8,128)}, u32[]{:S(2)}, u32[]{:S(2)}) collective-permute-start(f32[3,4,8,256]{3,2,1,0:T(8,128)} %get-tuple-element.67), channel_id=1, source_target_pairs={{0,2},{1,3},{2,4},{3,5},{4,6},{5,7},{6,0},{7,1},{8,10},{9,11},{10,... | collective-permute-start | bytes 294920 | tf_op jit(solution)/shard_map/ppermute | solution.py:79
  66.3 4.9 %collective-permute-start.15 = (f32[96,128]{1,0:T(8,128)S(1)}, f32[96,128]{1,0:T(8,128)S(1)}, u32[]{:S(2)}, u32[]{:S(2)}) collective-permute-start(f32[96,128]{1,0:T(8,128)S(1)} %get-tuple-element.70.own_ref), channel_id=1, source_target_pairs={{0,8},{8,0},{16,24},{24,16},{32,40},{40,32},{48,56},{56,48},{64,72... | collective-permute-start | bytes 147464 | tf_op jit(solution)/shard_map/ppermute | solution.py:543
  73.0 6.6 %all-to-all-start = ((f32[32,48,128]{2,1,0:T(8,128)}), f32[32,48,128]{2,1,0:T(8,128)S(1)}, u32[]{:S(2)}, u32[]{:S(2)}) async-start(f32[32,48,128]{2,1,0:T(8,128)} %shard_map.312), calls=%async_computation | async-start | bytes 1572864 | tf_op jit(solution)/shard_map/all_to_all | solution.py:547
  80.5 1.8 %collective-permute-start.17 = (f32[3,4,8,256]{3,2,1,0:T(8,128)S(1)}, f32[3,4,8,256]{3,2,1,0:T(8,128)S(1)}, u32[]{:S(2)}, u32[]{:S(2)}) collective-permute-start(f32[3,4,8,256]{3,2,1,0:T(8,128)S(1)} %copy-done.12), channel_id=1, source_target_pairs={{0,6},{1,7},{2,0},{3,1},{4,2},{5,3},{6,4},{7,5},{8,14},{9,15},{10,... | collective-permute-start | bytes 294920 | tf_op jit(solution)/shard_map/ppermute | solution.py:79
  82.4 1.9 %collective-permute-start.16 = (f32[3,2,8,256]{3,2,1,0:T(8,128)S(1)}, f32[3,2,8,256]{3,2,1,0:T(8,128)S(1)}, u32[]{:S(2)}, u32[]{:S(2)}) collective-permute-start(f32[3,2,8,256]{3,2,1,0:T(8,128)S(1)} %copy-done.14), channel_id=1, source_target_pairs={{0,4},{1,5},{2,6},{3,7},{4,0},{5,1},{6,2},{7,3},{8,12},{9,13},{10,... | collective-permute-start | bytes 147464 | tf_op jit(solution)/shard_map/ppermute | solution.py:79
  86.2 4.5 %collective-permute-start.19 = (f32[3,2,8,256]{3,2,1,0:T(8,128)S(1)}, f32[3,2,8,256]{3,2,1,0:T(8,128)S(1)}, u32[]{:S(2)}, u32[]{:S(2)}) collective-permute-start(f32[3,2,8,256]{3,2,1,0:T(8,128)S(1)} %slice_add_fusion), channel_id=1, source_target_pairs={{0,7},{1,0},{2,1},{3,2},{4,3},{5,4},{6,5},{7,6},{8,15},{9,8},{10,9... | collective-permute-start | bytes 147464 | tf_op jit(solution)/shard_map/ppermute | solution.py:79
  (122 shorter events, 24.6 us)
Async XLA Ops:
  0.6 11.4 %copy-start = (s32[4,3,4,16,512]{4,3,2,1,0:T(8,128)S(1)}, s32[4,3,4,16,512]{4,3,2,1,0:T(8,128)}, u32[]{:S(2)}) copy-start(s32[4,3,4,16,512]{4,3,2,1,0:T(8,128)} %shifts_ref.11) | copy-start | bytes 4718596
  3.2 6.4 %collective-permute-start = (f32[4,29,512]{2,1,0:T(8,128)}, f32[4,29,512]{2,1,0:T(8,128)S(1)}, u32[]{:S(2)}, u32[]{:S(2)}) collective-permute-start(f32[4,29,512]{2,1,0:T(8,128)} %get-tuple-element.42), channel_id=1, source_target_pairs={{0,8},{8,16},{16,24},{24,32},{32,40},{40,48},{48,56},{56,64},{64,7... | collective-permute-start | bytes 712712 | tf_op jit(solution)/shard_map/ppermute | solution.py:79
  6.0 6.0 %collective-permute-start.1 = (f32[4,29,512]{2,1,0:T(8,128)}, f32[4,29,512]{2,1,0:T(8,128)S(1)}, u32[]{:S(2)}, u32[]{:S(2)}) collective-permute-start(f32[4,29,512]{2,1,0:T(8,128)} %get-tuple-element.43), channel_id=1, source_target_pairs={{0,248},{8,0},{16,8},{24,16},{32,24},{40,32},{48,40},{56,48},{64,5... | collective-permute-start | bytes 712712 | tf_op jit(solution)/shard_map/ppermute | solution.py:79
  12.8 8.5 %collective-permute-start.2 = (f32[3,24,512]{2,1,0:T(8,128)S(1)}, f32[3,24,512]{2,1,0:T(8,128)S(1)}, u32[]{:S(2)}, u32[]{:S(2)}) collective-permute-start(f32[3,24,512]{2,1,0:T(8,128)S(1)} %get-tuple-element.101), channel_id=1, source_target_pairs={{0,1},{1,2},{2,3},{3,4},{4,5},{5,6},{6,7},{7,0},{8,9},{9,10},{10,1... | collective-permute-start | bytes 442376 | tf_op jit(solution)/shard_map/ppermute | solution.py:79
  14.8 6.5 %collective-permute-start.3 = (f32[3,24,512]{2,1,0:T(8,128)S(1)}, f32[3,24,512]{2,1,0:T(8,128)S(1)}, u32[]{:S(2)}, u32[]{:S(2)}) collective-permute-start(f32[3,24,512]{2,1,0:T(8,128)S(1)} %get-tuple-element.100), channel_id=1, source_target_pairs={{0,7},{1,0},{2,1},{3,2},{4,3},{5,4},{6,5},{7,6},{8,15},{9,8},{10,9... | collective-permute-start | bytes 442376 | tf_op jit(solution)/shard_map/ppermute | solution.py:79
  22.6 5.2 %collective-permute-start.4 = (f32[4,16,512]{2,1,0:T(8,128)S(1)}, f32[4,16,512]{2,1,0:T(8,128)S(1)}, u32[]{:S(2)}, u32[]{:S(2)}) collective-permute-start(f32[4,16,512]{2,1,0:T(8,128)S(1)} %get-tuple-element.48), channel_id=1, source_target_pairs={{0,1},{1,2},{2,3},{3,4},{4,5},{5,6},{6,7},{7,0},{8,9},{9,10},{10,1... | collective-permute-start | bytes 393224 | tf_op jit(solution)/shard_map/ppermute | solution.py:79
  22.7 5.1 %collective-permute-start.5 = (f32[4,16,512]{2,1,0:T(8,128)S(1)}, f32[4,16,512]{2,1,0:T(8,128)S(1)}, u32[]{:S(2)}, u32[]{:S(2)}) collective-permute-start(f32[4,16,512]{2,1,0:T(8,128)S(1)} %get-tuple-element.50), channel_id=1, source_target_pairs={{0,7},{1,0},{2,1},{3,2},{4,3},{5,4},{6,5},{7,6},{8,15},{9,8},{10,9... | collective-permute-start | bytes 393224 | tf_op jit(solution)/shard_map/ppermute | solution.py:79
  28.8 5.3 %collective-permute-start.6 = (f32[4,7,512]{2,1,0:T(8,128)S(1)}, f32[4,7,512]{2,1,0:T(8,128)S(1)}, u32[]{:S(2)}, u32[]{:S(2)}) collective-permute-start(f32[4,7,512]{2,1,0:T(8,128)S(1)} %get-tuple-element.52), channel_id=1, source_target_pairs={{0,8},{8,16},{16,24},{24,32},{32,40},{40,48},{48,56},{56,64},{64,7... | collective-permute-start | bytes 172040 | tf_op jit(solution)/shard_map/ppermute | solution.py:79
  32.7 3.7 %collective-permute-start.7 = (f32[4,7,512]{2,1,0:T(8,128)S(1)}, f32[4,7,512]{2,1,0:T(8,128)S(1)}, u32[]{:S(2)}, u32[]{:S(2)}) collective-permute-start(f32[4,7,512]{2,1,0:T(8,128)S(1)} %get-tuple-element.53), channel_id=1, source_target_pairs={{0,248},{8,0},{16,8},{24,16},{32,24},{40,32},{48,40},{56,48},{64,5... | collective-permute-start | bytes 172040 | tf_op jit(solution)/shard_map/ppermute | solution.py:79
  37.2 5.4 %collective-permute-start.8 = (f32[3,24,512]{2,1,0:T(8,128)S(1)}, f32[3,24,512]{2,1,0:T(8,128)S(1)}, u32[]{:S(2)}, u32[]{:S(2)}) collective-permute-start(f32[3,24,512]{2,1,0:T(8,128)S(1)} %get-tuple-element.99), channel_id=1, source_target_pairs={{0,1},{1,2},{2,3},{3,4},{4,5},{5,6},{6,7},{7,0},{8,9},{9,10},{10,1... | collective-permute-start | bytes 442376 | tf_op jit(solution)/shard_map/ppermute | solution.py:79
  39.7 4.0 %collective-permute-start.9 = (f32[3,24,512]{2,1,0:T(8,128)S(1)}, f32[3,24,512]{2,1,0:T(8,128)S(1)}, u32[]{:S(2)}, u32[]{:S(2)}) collective-permute-start(f32[3,24,512]{2,1,0:T(8,128)S(1)} %get-tuple-element.98), channel_id=1, source_target_pairs={{0,7},{1,0},{2,1},{3,2},{4,3},{5,4},{6,5},{7,6},{8,15},{9,8},{10,9... | collective-permute-start | bytes 442376 | tf_op jit(solution)/shard_map/ppermute | solution.py:79
  45.0 5.8 %collective-permute-start.10 = (f32[4,24,512]{2,1,0:T(8,128)S(1)}, f32[4,24,512]{2,1,0:T(8,128)S(1)}, u32[]{:S(2)}, u32[]{:S(2)}) collective-permute-start(f32[4,24,512]{2,1,0:T(8,128)S(1)} %shard_map.308.image_ref), channel_id=1, source_target_pairs={{0,1},{1,2},{2,3},{3,4},{4,5},{5,6},{6,7},{7,0},{8,9},{9,10},{10,1... | collective-permute-start | bytes 589832 | tf_op jit(solution)/shard_map/ppermute | solution.py:79
  46.6 4.5 %collective-permute-start.11 = (f32[4,24,512]{2,1,0:T(8,128)S(1)}, f32[4,24,512]{2,1,0:T(8,128)S(1)}, u32[]{:S(2)}, u32[]{:S(2)}) collective-permute-start(f32[4,24,512]{2,1,0:T(8,128)S(1)} %shard_map.308.image_ref), channel_id=1, source_target_pairs={{0,7},{1,0},{2,1},{3,2},{4,3},{5,4},{6,5},{7,6},{8,15},{9,8},{10,9... | collective-permute-start | bytes 589832 | tf_op jit(solution)/shard_map/ppermute | solution.py:79
  51.1 21.0 %copy-start.4 = (f32[2,48,128]{2,1,0:T(8,128)S(1)}, f32[2,48,128]{2,1,0:T(8,128)}, u32[]{:S(2)}) copy-start(f32[2,48,128]{2,1,0:T(8,128)} %constant.64.clone.tables_ref) | copy-start | bytes 147460
  53.3 26.4 %copy-start.1 = (f32[512,512]{1,0:T(8,128)S(1)}, f32[512,512]{1,0:T(8,128)}, u32[]{:S(2)}) copy-start(f32[512,512]{1,0:T(8,128)} %constant.66.clone.refs_0_) | copy-start | bytes 3145732
  53.3 7.5 %collective-permute-start.12 = (f32[3,2,8,256]{3,2,1,0:T(8,128)S(1)}, f32[3,2,8,256]{3,2,1,0:T(8,128)S(1)}, u32[]{:S(2)}, u32[]{:S(2)}) collective-permute-start(f32[3,2,8,256]{3,2,1,0:T(8,128)S(1)} %get-tuple-element.66.own_ref), channel_id=1, source_target_pairs={{0,8},{8,16},{16,24},{24,32},{32,40},{40,48},{48,56},{56,64},{64,7... | collective-permute-start | bytes 147464 | tf_op jit(solution)/shard_map/ppermute | solution.py:79
  58.4 3.5 %collective-permute-start.13 = (f32[3,2,8,256]{3,2,1,0:T(8,128)S(1)}, f32[3,2,8,256]{3,2,1,0:T(8,128)S(1)}, u32[]{:S(2)}, u32[]{:S(2)}) collective-permute-start(f32[3,2,8,256]{3,2,1,0:T(8,128)S(1)} %get-tuple-element.66.own_ref), channel_id=1, source_target_pairs={{0,248},{8,0},{16,8},{24,16},{32,24},{40,32},{48,40},{56,48},{64,5... | collective-permute-start | bytes 147464 | tf_op jit(solution)/shard_map/ppermute | solution.py:79
  64.2 20.1 %collective-permute-start.14 = (f32[3,4,8,256]{3,2,1,0:T(8,128)}, f32[3,4,8,256]{3,2,1,0:T(8,128)}, u32[]{:S(2)}, u32[]{:S(2)}) collective-permute-start(f32[3,4,8,256]{3,2,1,0:T(8,128)} %get-tuple-element.67), channel_id=1, source_target_pairs={{0,2},{1,3},{2,4},{3,5},{4,6},{5,7},{6,0},{7,1},{8,10},{9,11},{10,... | collective-permute-start | bytes 294920 | tf_op jit(solution)/shard_map/ppermute | solution.py:79
  66.3 5.7 %collective-permute-start.15 = (f32[96,128]{1,0:T(8,128)S(1)}, f32[96,128]{1,0:T(8,128)S(1)}, u32[]{:S(2)}, u32[]{:S(2)}) collective-permute-start(f32[96,128]{1,0:T(8,128)S(1)} %get-tuple-element.70.own_ref), channel_id=1, source_target_pairs={{0,8},{8,0},{16,24},{24,16},{32,40},{40,32},{48,56},{56,48},{64,72... | collective-permute-start | bytes 147464 | tf_op jit(solution)/shard_map/ppermute | solution.py:543
  73.0 20.8 %all-to-all-start = ((f32[32,48,128]{2,1,0:T(8,128)}), f32[32,48,128]{2,1,0:T(8,128)S(1)}, u32[]{:S(2)}, u32[]{:S(2)}) async-start(f32[32,48,128]{2,1,0:T(8,128)} %shard_map.312), calls=%async_computation | async-start | bytes 1572864 | tf_op jit(solution)/shard_map/all_to_all | solution.py:547
  80.5 5.6 %collective-permute-start.17 = (f32[3,4,8,256]{3,2,1,0:T(8,128)S(1)}, f32[3,4,8,256]{3,2,1,0:T(8,128)S(1)}, u32[]{:S(2)}, u32[]{:S(2)}) collective-permute-start(f32[3,4,8,256]{3,2,1,0:T(8,128)S(1)} %copy-done.12), channel_id=1, source_target_pairs={{0,6},{1,7},{2,0},{3,1},{4,2},{5,3},{6,4},{7,5},{8,14},{9,15},{10,... | collective-permute-start | bytes 294920 | tf_op jit(solution)/shard_map/ppermute | solution.py:79
  82.4 9.1 %collective-permute-start.16 = (f32[3,2,8,256]{3,2,1,0:T(8,128)S(1)}, f32[3,2,8,256]{3,2,1,0:T(8,128)S(1)}, u32[]{:S(2)}, u32[]{:S(2)}) collective-permute-start(f32[3,2,8,256]{3,2,1,0:T(8,128)S(1)} %copy-done.14), channel_id=1, source_target_pairs={{0,4},{1,5},{2,6},{3,7},{4,0},{5,1},{6,2},{7,3},{8,12},{9,13},{10,... | collective-permute-start | bytes 147464 | tf_op jit(solution)/shard_map/ppermute | solution.py:79
  85.3 6.2 %collective-permute-start.18 = (f32[3,2,8,256]{3,2,1,0:T(8,128)S(1)}, f32[3,2,8,256]{3,2,1,0:T(8,128)S(1)}, u32[]{:S(2)}, u32[]{:S(2)}) collective-permute-start(f32[3,2,8,256]{3,2,1,0:T(8,128)S(1)} %slice_add_fusion.2), channel_id=1, source_target_pairs={{0,1},{1,2},{2,3},{3,4},{4,5},{5,6},{6,7},{7,0},{8,9},{9,10},{10,1... | collective-permute-start | bytes 147464 | tf_op jit(solution)/shard_map/ppermute | solution.py:79
  86.2 5.7 %collective-permute-start.19 = (f32[3,2,8,256]{3,2,1,0:T(8,128)S(1)}, f32[3,2,8,256]{3,2,1,0:T(8,128)S(1)}, u32[]{:S(2)}, u32[]{:S(2)}) collective-permute-start(f32[3,2,8,256]{3,2,1,0:T(8,128)S(1)} %slice_add_fusion), channel_id=1, source_target_pairs={{0,7},{1,0},{2,1},{3,2},{4,3},{5,4},{6,5},{7,6},{8,15},{9,8},{10,9... | collective-permute-start | bytes 147464 | tf_op jit(solution)/shard_map/ppermute | solution.py:79
  (32 other events, 274.4 us)
